TPU v7x, 256 devices: a whole 4x4x8 slice. The times are simulated.
256 devices in a mesh: blk: 16 (over x, y_lo, core), wide: 16 (over y_hi, z).
Axes of the slice: x: 4, y: 4 (y_hi: 2, y_lo: 2; y = y_hi * 2 + y_lo), z: 8, core: 2. Of those that a mesh axis runs over, the one named last changes fastest.
Arguments:
- points: bfloat16 [65536, 32], P(('blk', 'wide')), may hold values from -6 to 6
- inv_length: float32 [32], replicated, may hold values from 0.2 to 0.7
- noise_var: float32 [], replicated, may hold values from 0.1 to 1
- solution: float32 [65536, 128], P(('blk', 'wide')), may hold values from -6 to 6
- residual: float32 [65536, 128], P(('blk', 'wide')), may hold values from -6 to 6
- direction: float32 [65536, 128], P(('blk', 'wide')), may hold values from -6 to 6
Outputs:
- new_solution: float32 [65536, 128], P(('blk', 'wide'))
- new_residual: float32 [65536, 128], P(('blk', 'wide'))
- new_direction: float32 [65536, 128], P(('blk', 'wide'))
All inputs are finite; a program needn't handle non-finite values.
Results may differ from a plain program's by a relative error of at most 0.01.
Values may be sent and summed in bfloat16 or wider, within the bound.
No kernel may reach another device: no remote copies, remote signals or barrier semaphores. Data moves between devices by JAX's collectives and lax.ppermute only.
A program may use at most 64 MiB of HBM per device.

v0:
```python
import functools

import jax
import jax.numpy as jnp
from jax import lax
from jax.sharding import Mesh
from jax.sharding import PartitionSpec as P

WIDE = ("wide_0", "wide_1")
BLK = ("blk_0", "blk_1", "blk_2")
BLK_WIDE = ("blk_0", "blk_1", "blk_2", "wide_0", "wide_1")


def shifted(x, axis, by):
    count = lax.axis_size(axis)
    return lax.ppermute(x, axis, [(i, (i + by) % count) for i in range(count)])


def cut_along(x, dim, count):
    before, after = (x.shape[:dim], x.shape[dim + 1 :])
    return jnp.moveaxis(x.reshape(*before, count, -1, *after), dim, 0)


def sent_and_summed(x, axis, dim):
    count = lax.axis_size(axis)
    blocks = lax.all_to_all(cut_along(x, dim, count), axis, 0, 0, tiled=True)
    return jnp.sum(blocks.astype(jnp.float32), axis=0)


def over_axes(x, axes):
    return functools.reduce(lax.psum, axes, x)


def squares_of(values):
    wide_values = values.astype(jnp.float32)
    return jnp.sum(wide_values * wide_values, axis=1)


def kernel_tile(rows_x, rows_sq, cols_x, cols_sq):
    inner_prod = lax.dot_general(
        rows_x, cols_x, (((1,), (1,)), ((), ())), preferred_element_type=jnp.float32
    )
    dist_sq = jnp.maximum(rows_sq[:, None] + cols_sq[None, :] - 2.0 * inner_prod, 0.0)
    radius = jnp.sqrt(5.0 * dist_sq)
    return ((1.0 + radius + radius * radius / 3.0) * jnp.exp(-radius)).astype(jnp.bfloat16)


def on_device(points, inv_length, noise_var, solution, residual, direction):
    scaled = (points.astype(jnp.float32) * inv_length).astype(jnp.bfloat16)
    low_dir = direction.astype(jnp.bfloat16)
    own_sq = squares_of(scaled)
    block_x, block_p = (
        lax.all_gather(scaled, WIDE, axis=0, tiled=True),
        lax.all_gather(low_dir, WIDE, axis=0, tiled=True),
    )
    block_sq = squares_of(block_x)
    cycle_size = lax.axis_size(BLK)
    empty_sums = jnp.zeros(direction.shape, jnp.float32)
    half_cycle = cycle_size // 2
    row_sums = jnp.dot(
        kernel_tile(block_x, block_sq, scaled, own_sq), low_dir, preferred_element_type=jnp.float32
    )

    def paired_turn(counter, carried):
        piece_x, piece_p, piece_sum, row_total = carried
        piece_x, piece_p = shifted((piece_x, piece_p), BLK, 1)
        piece_sum = shifted(piece_sum, BLK, 1)
        kernel_block = kernel_tile(block_x, block_sq, piece_x, squares_of(piece_x))
        row_total = row_total + jnp.dot(kernel_block, piece_p, preferred_element_type=jnp.float32)
        piece_sum = piece_sum + lax.dot_general(
            kernel_block, block_p, (((0,), (0,)), ((), ())), preferred_element_type=jnp.float32
        )
        return (piece_x, piece_p, piece_sum, row_total)

    result = lax.fori_loop(0, half_cycle - 1, paired_turn, (scaled, low_dir, empty_sums, row_sums))
    home_sums = shifted(result[2], BLK, 1 - half_cycle)
    far_x, far_p = shifted((scaled, low_dir), BLK, half_cycle)
    far_block = kernel_tile(block_x, block_sq, far_x, squares_of(far_x))
    row_sums = result[3] + jnp.dot(far_block, far_p, preferred_element_type=jnp.float32)
    own_image = sent_and_summed(row_sums.astype(jnp.bfloat16), WIDE, 0) + home_sums
    kernel_image = own_image + noise_var * direction
    old_norm = over_axes(jnp.sum(residual * residual, axis=0), BLK_WIDE)
    curvature = over_axes(jnp.sum(direction * kernel_image, axis=0), BLK_WIDE)
    step_length = old_norm / curvature
    new_residual = residual - step_length * kernel_image
    new_norm = over_axes(jnp.sum(new_residual * new_residual, axis=0), BLK_WIDE)
    new_solution = solution + step_length * direction
    new_direction = new_residual + new_norm / old_norm * direction
    return (new_solution, new_residual, new_direction)


def solution(mesh):
    finer = Mesh(
        mesh.devices.reshape(4, 2, 2, 2, 8), ("blk_0", "blk_1", "blk_2", "wide_0", "wide_1")
    )
    placed = (P(BLK_WIDE, None), P(), P(), P(BLK_WIDE, None), P(BLK_WIDE, None), P(BLK_WIDE, None))
    return jax.shard_map(
        on_device,
        mesh=finer,
        in_specs=placed,
        out_specs=(P(BLK_WIDE, None), P(BLK_WIDE, None), P(BLK_WIDE, None)),
        check_vma=False,
    )
```

profile of v0, /device:TPU:1, one launch (start us, length us, event | category | flops | bytes accessed | tf_op | source)
XLA Modules:
  0.0 297.1 jit_solution(7086538707987538601)
XLA Ops:
  7.2 1.5 convert_element_type.38
  8.8 3.7 %collective-permute-start.4 = (bf16[256,128]{1,0:T(8,128)(2,1)}, bf16[256,128]{1,0:T(8,128)(2,1)S(1)}, u32[]{:S(2)}, u32[]{:S(2)}) collective-permute-start(bf16[256,128]{1,0:T(8,128)(2,1)} %convert_element_type.38), channel_id=1, source_target_pairs={{0,128},{16,144},{32,160},{48,176},{64,192},{80,208},{96,224},{112... | collective-permute-start | bytes 196616 | tf_op jit(solution)/shard_map/ppermute | solution.py:16
  12.4 0.8 copy.9
  13.3 1.3 multiply_reduce_fusion.5
  14.6 44.2 %all_gather.6 = bf16[4096,32]{1,0:T(8,128)(2,1)S(1)} all-gather(bf16[256,32]{1,0:T(8,128)(2,1)} %get-tuple-element.156), channel_id=1, replica_groups=mesh['blk_0'=4,'blk_1'=2,'blk_2'=2,'wide_0'=2,'wide_1'=8] {'wide_0','wid..., dimensions={0}, use_global_device_ids=true | all-gather | bytes 278528 | tf_op jit(solution)/shard_map/all_gather | solution.py:53
  59.5 3.8 %fusion.5 = f32[4096,128]{1,0:T(8,128)S(1)} fusion(bf16[256,128]{1,0:T(8,128)(2,1)S(1)} %copy-done.4, bf16[4096,32]{1,0:T(8,128)(2,1)S(1)} %all_gather.6, bf16[256,32]{1,0:T(8,128)(2,1)} %get-tuple-element.156, f32[256]{0:T(256)S(1)} %get-tuple-element.103, f32[4096]{0:T(1024)S(1)} %multiply_reduce_fusion.1), kind=kOutput, calls=%fused_computation.18 | convolution fusion | flops 348127232 | bytes 2458624 | tf_op jit(solution)/shard_map/dot_general | solution.py:60
  63.3 0.7 multiply_reduce_fusion.4
  64.0 26.2 %all-gather.2.cloned.1.call-done = bf16[4096,128]{1,0:T(8,128)(2,1)} async-done(((bf16[256,128]{1,0:T(8,128)(2,1)}), bf16[4096,128]{1,0:T(8,128)(2,1)}) %all-gather.2.cloned.1.call-update) | async-done | bytes 1048592 | tf_op jit(solution)/shard_map/all_gather | solution.py:54
  90.2 89.3 %while.17 = (s32[]{:T(128)}, bf16[256,32]{1,0:T(8,128)(2,1)}, bf16[256,128]{1,0:T(8,128)(2,1)S(1)}, f32[256,128]{1,0:T(8,128)S(1)}, f32[4096,128]{1,0:T(8,128)S(...) while((s32[]{:T(128)}, bf16[256,32]{1,0:T(8,128)(2,1)}, ...), condition=%wide.region_10.0_spmd.clone, body=%wide.region_8.10_spmd.clone.sunk | while | flops 617176832 | bytes 17647876 | solution.py:75
  90.2 4.6 %collective-permute-start = (bf16[256,32]{1,0:T(8,128)(2,1)}, bf16[256,32]{1,0:T(8,128)(2,1)S(1)}, u32[]{:S(2)}, u32[]{:S(2)}) collective-permute-start(bf16[256,32]{1,0:T(8,128)(2,1)} %get-tuple-element.166), channel_id=1, source_target_pairs={{0,16},{16,32},{32,48},{48,64},{64,80},{80,96},{96,112},{112,128},... | collective-permute-start | bytes 49160 | tf_op jit(solution)/shard_map/while/body/eval_jaxpr/ppermute | solution.py:16
  94.9 2.4 collective-permute-start.1
  97.5 3.1 %multiply_convert_fusion.6 = bf16[4096,256]{1,0:T(8,128)(2,1)S(1)} fusion(bf16[4096,32]{1,0:T(8,128)(2,1)S(1)} %get-tuple-element.181, bf16[256,32]{1,0:T(8,128)(2,1)S(1)} %collective-permute-done, f32[256]{0:T(256)S(1)} %multiply_reduce_fusion.8, f32[4096]{0:T(1024)S(1)} %get-tuple-element.180), kind=kOutput, calls=%fused_computation.2.clone.1 | convolution fusion | flops 79691776 | bytes 2393088 | tf_op jit(solution)/shard_map/while/body/eval_jaxpr/dot_general | solution.py:40
  100.6 0.6 copy.21
  101.2 0.8 convolution_add_fusion.6
  102.4 1.7 convolution_add_fusion.5
  104.1 1.4 collective-permute-start
  105.8 3.2 %collective-permute-start.1 = (bf16[256,128]{1,0:T(8,128)(2,1)S(1)}, bf16[256,128]{1,0:T(8,128)(2,1)S(1)}, u32[]{:S(2)}, u32[]{:S(2)}) collective-permute-start(bf16[256,128]{1,0:T(8,128)(2,1)S(1)} %get-tuple-element.167), channel_id=1, source_target_pairs={{0,16},{16,32},{32,48},{48,64},{64,80},{80,96},{96,112},{112,128},... | collective-permute-start | bytes 196616 | tf_op jit(solution)/shard_map/while/body/eval_jaxpr/ppermute | solution.py:16
  109.1 3.1 %multiply_convert_fusion.6 = bf16[4096,256]{1,0:T(8,128)(2,1)S(1)} fusion(bf16[4096,32]{1,0:T(8,128)(2,1)S(1)} %get-tuple-element.181, bf16[256,32]{1,0:T(8,128)(2,1)S(1)} %collective-permute-done, f32[256]{0:T(256)S(1)} %multiply_reduce_fusion.8, f32[4096]{0:T(1024)S(1)} %get-tuple-element.180), kind=kOutput, calls=%fused_computation.2.clone.1 | convolution fusion | flops 79691776 | bytes 2393088 | tf_op jit(solution)/shard_map/while/body/eval_jaxpr/dot_general | solution.py:40
  112.2 0.6 copy.21
  112.8 0.8 convolution_add_fusion.6
  114.1 1.7 convolution_add_fusion.5
  116.3 1.2 collective-permute-start.2
  117.5 3.2 %collective-permute-start.1 = (bf16[256,128]{1,0:T(8,128)(2,1)S(1)}, bf16[256,128]{1,0:T(8,128)(2,1)S(1)}, u32[]{:S(2)}, u32[]{:S(2)}) collective-permute-start(bf16[256,128]{1,0:T(8,128)(2,1)S(1)} %get-tuple-element.167), channel_id=1, source_target_pairs={{0,16},{16,32},{32,48},{48,64},{64,80},{80,96},{96,112},{112,128},... | collective-permute-start | bytes 196616 | tf_op jit(solution)/shard_map/while/body/eval_jaxpr/ppermute | solution.py:16
  120.6 0.6 collective-permute-done
  121.4 3.1 %multiply_convert_fusion.6 = bf16[4096,256]{1,0:T(8,128)(2,1)S(1)} fusion(bf16[4096,32]{1,0:T(8,128)(2,1)S(1)} %get-tuple-element.181, bf16[256,32]{1,0:T(8,128)(2,1)S(1)} %collective-permute-done, f32[256]{0:T(256)S(1)} %multiply_reduce_fusion.8, f32[4096]{0:T(1024)S(1)} %get-tuple-element.180), kind=kOutput, calls=%fused_computation.2.clone.1 | convolution fusion | flops 79691776 | bytes 2393088 | tf_op jit(solution)/shard_map/while/body/eval_jaxpr/dot_general | solution.py:40
  124.5 0.6 copy.21
  125.1 0.8 convolution_add_fusion.6
  126.3 1.7 convolution_add_fusion.5
  128.1 1.0 collective-permute-start.2
  129.1 3.2 %collective-permute-start.1 = (bf16[256,128]{1,0:T(8,128)(2,1)S(1)}, bf16[256,128]{1,0:T(8,128)(2,1)S(1)}, u32[]{:S(2)}, u32[]{:S(2)}) collective-permute-start(bf16[256,128]{1,0:T(8,128)(2,1)S(1)} %get-tuple-element.167), channel_id=1, source_target_pairs={{0,16},{16,32},{32,48},{48,64},{64,80},{80,96},{96,112},{112,128},... | collective-permute-start | bytes 196616 | tf_op jit(solution)/shard_map/while/body/eval_jaxpr/ppermute | solution.py:16
  132.3 1.9 collective-permute-done
  134.2 3.1 %multiply_convert_fusion.6 = bf16[4096,256]{1,0:T(8,128)(2,1)S(1)} fusion(bf16[4096,32]{1,0:T(8,128)(2,1)S(1)} %get-tuple-element.181, bf16[256,32]{1,0:T(8,128)(2,1)S(1)} %collective-permute-done, f32[256]{0:T(256)S(1)} %multiply_reduce_fusion.8, f32[4096]{0:T(1024)S(1)} %get-tuple-element.180), kind=kOutput, calls=%fused_computation.2.clone.1 | convolution fusion | flops 79691776 | bytes 2393088 | tf_op jit(solution)/shard_map/while/body/eval_jaxpr/dot_general | solution.py:40
  138.0 0.8 convolution_add_fusion.6
  139.2 1.7 convolution_add_fusion.5
  141.1 2.8 collective-permute-start.1
  143.9 3.1 %collective-permute-done = bf16[256,32]{1,0:T(8,128)(2,1)S(1)} collective-permute-done((bf16[256,32]{1,0:T(8,128)(2,1)}, bf16[256,32]{1,0:T(8,128)(2,1)S(1)}, u32[]{:S(2)}, u32[]{:S(2)}) %collective-permute-start) | collective-permute-done | bytes 16416 | tf_op jit(solution)/shard_map/while/body/eval_jaxpr/ppermute | solution.py:16
  147.1 3.1 %multiply_convert_fusion.6 = bf16[4096,256]{1,0:T(8,128)(2,1)S(1)} fusion(bf16[4096,32]{1,0:T(8,128)(2,1)S(1)} %get-tuple-element.181, bf16[256,32]{1,0:T(8,128)(2,1)S(1)} %collective-permute-done, f32[256]{0:T(256)S(1)} %multiply_reduce_fusion.8, f32[4096]{0:T(1024)S(1)} %get-tuple-element.180), kind=kOutput, calls=%fused_computation.2.clone.1 | convolution fusion | flops 79691776 | bytes 2393088 | tf_op jit(solution)/shard_map/while/body/eval_jaxpr/dot_general | solution.py:40
  150.8 0.8 convolution_add_fusion.6
  152.0 1.7 convolution_add_fusion.5
  154.0 1.6 collective-permute-start.1
  155.6 4.3 %collective-permute-done = bf16[256,32]{1,0:T(8,128)(2,1)S(1)} collective-permute-done((bf16[256,32]{1,0:T(8,128)(2,1)}, bf16[256,32]{1,0:T(8,128)(2,1)S(1)}, u32[]{:S(2)}, u32[]{:S(2)}) %collective-permute-start) | collective-permute-done | bytes 16416 | tf_op jit(solution)/shard_map/while/body/eval_jaxpr/ppermute | solution.py:16
  160.0 3.1 %multiply_convert_fusion.6 = bf16[4096,256]{1,0:T(8,128)(2,1)S(1)} fusion(bf16[4096,32]{1,0:T(8,128)(2,1)S(1)} %get-tuple-element.181, bf16[256,32]{1,0:T(8,128)(2,1)S(1)} %collective-permute-done, f32[256]{0:T(256)S(1)} %multiply_reduce_fusion.8, f32[4096]{0:T(1024)S(1)} %get-tuple-element.180), kind=kOutput, calls=%fused_computation.2.clone.1 | convolution fusion | flops 79691776 | bytes 2393088 | tf_op jit(solution)/shard_map/while/body/eval_jaxpr/dot_general | solution.py:40
  163.7 0.8 convolution_add_fusion.6
  164.9 1.7 convolution_add_fusion.5
  167.2 5.5 %collective-permute-done = bf16[256,32]{1,0:T(8,128)(2,1)S(1)} collective-permute-done((bf16[256,32]{1,0:T(8,128)(2,1)}, bf16[256,32]{1,0:T(8,128)(2,1)S(1)}, u32[]{:S(2)}, u32[]{:S(2)}) %collective-permute-start) | collective-permute-done | bytes 16416 | tf_op jit(solution)/shard_map/while/body/eval_jaxpr/ppermute | solution.py:16
  172.8 3.1 %multiply_convert_fusion.6 = bf16[4096,256]{1,0:T(8,128)(2,1)S(1)} fusion(bf16[4096,32]{1,0:T(8,128)(2,1)S(1)} %get-tuple-element.181, bf16[256,32]{1,0:T(8,128)(2,1)S(1)} %collective-permute-done, f32[256]{0:T(256)S(1)} %multiply_reduce_fusion.8, f32[4096]{0:T(1024)S(1)} %get-tuple-element.180), kind=kOutput, calls=%fused_computation.2.clone.1 | convolution fusion | flops 79691776 | bytes 2393088 | tf_op jit(solution)/shard_map/while/body/eval_jaxpr/dot_general | solution.py:40
  175.9 0.6 copy.21
  176.5 0.8 convolution_add_fusion.6
  177.8 1.7 convolution_add_fusion.5
  179.4 5.0 %fusion.4 = bf16[4096,128]{1,0:T(8,128)(2,1)} fusion(f32[4096,128]{1,0:T(8,128)S(1)} %get-tuple-element.46, bf16[256,128]{1,0:T(8,128)(2,1)} %copy-done.7, f32[256]{0:T(256)} %multiply_reduce_fusion.4, bf16[4096,32]{1,0:T(8,128)(2,1)S(1)} %get-tuple-element.189, bf16[256,32]{1,0:T(8,128)(2,1)} %copy-done.6, f32[4096]{0:T(1024)S(1)} %get-tuple-element.201), kind=kOutput, calls=%fused_computation.13 | convolution fusion | flops 349175808 | bytes 3507200 | tf_op jit(solution)/shard_map/dot_general | solution.py:79
  184.4 4.0 %all-to-all-start = ((bf16[16,256,128]{2,1,0:T(8,128)(2,1)}), bf16[16,256,128]{2,1,0:T(8,128)(2,1)S(1)}, u32[]{:S(2)}, u32[]{:S(2)}) async-start(bf16[16,256,128]{2,1,0:T(8,128)(2,1)} %bitcast.25), calls=%async_computation | async-start | bytes 2097152 | tf_op jit(solution)/shard_map/all_to_all | solution.py:26
  189.7 19.9 %all-to-all-done = bf16[16,256,128]{2,1,0:T(8,128)(2,1)S(1)} async-done(((bf16[16,256,128]{2,1,0:T(8,128)(2,1)}), bf16[16,256,128]{2,1,0:T(8,128)(2,1)S(1)}, u32[]{:S(2)}, u32[]{:S(2)}) %all-to-all-start) | async-done | bytes 1048608 | tf_op jit(solution)/shard_map/all_to_all | solution.py:26
  209.8 13.7 %all-reduce.1 = (f32[128]{0:T(128)S(1)}, f32[128]{0:T(128)S(1)}) all-reduce(f32[128]{0:T(128)S(1)} %multiply_reduce_fusion.6, f32[128]{0:T(128)S(1)} %multiply_reduce_fusion.3), channel_id=1, replica_groups=mesh['blk_0'=4,'blk_1'=2,'blk_2'=2,'wide_0'=2,'wide_1'=8] {'blk_0'}, use_global_device_ids=true, to_apply=%region_1.0 | all-reduce | flops 256 | bytes 2048 | tf_op jit(solution)/shard_map/psum | solution.py:31
  223.5 6.7 %all-reduce.4 = (f32[128]{0:T(128)S(1)}, f32[128]{0:T(128)S(1)}) all-reduce(f32[128]{0:T(128)S(1)} %get-tuple-element.93, f32[128]{0:T(128)S(1)} %get-tuple-element.94), channel_id=1, replica_groups=mesh['blk_0'=4,'blk_1'=2,'blk_2'=2,'wide_0'=2,'wide_1'=8] {'blk_1'}, use_global_device_ids=true, to_apply=%region_2.3 | all-reduce | flops 256 | bytes 2048 | tf_op jit(solution)/shard_map/psum | solution.py:31
  230.2 5.4 %all-reduce.3 = (f32[128]{0:T(128)S(1)}, f32[128]{0:T(128)S(1)}) all-reduce(f32[128]{0:T(128)S(1)} %get-tuple-element.99, f32[128]{0:T(128)S(1)} %get-tuple-element.100), channel_id=1, replica_groups=mesh['blk_0'=4,'blk_1'=2,'blk_2'=2,'wide_0'=2,'wide_1'=8] {'blk_2'}, use_global_device_ids=true, to_apply=%region_3.4 | all-reduce | flops 256 | bytes 2048 | tf_op jit(solution)/shard_map/psum | solution.py:31
  235.6 5.3 %all-reduce.2 = (f32[128]{0:T(128)S(1)}, f32[128]{0:T(128)S(1)}) all-reduce(f32[128]{0:T(128)S(1)} %get-tuple-element.97, f32[128]{0:T(128)S(1)} %get-tuple-element.98), channel_id=1, replica_groups=mesh['blk_0'=4,'blk_1'=2,'blk_2'=2,'wide_0'=2,'wide_1'=8] {'wide_0'}, use_global_device_ids=true, to_apply=%region_4.0 | all-reduce | flops 256 | bytes 2048 | tf_op jit(solution)/shard_map/psum | solution.py:31
  240.9 11.3 %all-reduce = (f32[128]{0:T(128)S(1)}, f32[128]{0:T(128)S(1)}) all-reduce(f32[128]{0:T(128)S(1)} %get-tuple-element.95, f32[128]{0:T(128)S(1)} %get-tuple-element.96), channel_id=1, replica_groups=mesh['blk_0'=4,'blk_1'=2,'blk_2'=2,'wide_0'=2,'wide_1'=8] {'wide_1'}, use_global_device_ids=true, to_apply=%region_5.0 | all-reduce | flops 256 | bytes 2048 | tf_op jit(solution)/shard_map/psum | solution.py:31
  252.2 0.7 multiply_reduce_fusion.2
  252.9 6.0 %psum.115 = f32[128]{0:T(128)S(1)} all-reduce(f32[128]{0:T(128)S(1)} %get-tuple-element.101), channel_id=1, replica_groups=mesh['blk_0'=4,'blk_1'=2,'blk_2'=2,'wide_0'=2,'wide_1'=8] {'blk_0'}, use_global_device_ids=true, to_apply=%region_20.0 | all-reduce | flops 128 | bytes 1024 | tf_op jit(solution)/shard_map/psum | solution.py:31
  258.9 4.0 %psum.116 = f32[128]{0:T(128)S(1)} all-reduce(f32[128]{0:T(128)S(1)} %psum.115), channel_id=1, replica_groups=mesh['blk_0'=4,'blk_1'=2,'blk_2'=2,'wide_0'=2,'wide_1'=8] {'blk_1'}, use_global_device_ids=true, to_apply=%region_21.0 | all-reduce | flops 128 | bytes 1024 | tf_op jit(solution)/shard_map/psum | solution.py:31
  263.0 10.0 %psum.117 = f32[128]{0:T(128)S(1)} all-reduce(f32[128]{0:T(128)S(1)} %psum.116), channel_id=1, replica_groups=mesh['blk_0'=4,'blk_1'=2,'blk_2'=2,'wide_0'=2,'wide_1'=8] {'blk_2'}, use_global_device_ids=true, to_apply=%region_22.0 | all-reduce | flops 128 | bytes 1024 | tf_op jit(solution)/shard_map/psum | solution.py:31
  272.9 5.3 %psum.118 = f32[128]{0:T(128)S(1)} all-reduce(f32[128]{0:T(128)S(1)} %psum.117), channel_id=1, replica_groups=mesh['blk_0'=4,'blk_1'=2,'blk_2'=2,'wide_0'=2,'wide_1'=8] {'wide_0'}, use_global_device_ids=true, to_apply=%region_23.0 | all-reduce | flops 128 | bytes 1024 | tf_op jit(solution)/shard_map/psum | solution.py:31
  278.2 11.4 %psum.119 = f32[128]{0:T(128)S(1)} all-reduce(f32[128]{0:T(128)S(1)} %psum.118), channel_id=1, replica_groups=mesh['blk_0'=4,'blk_1'=2,'blk_2'=2,'wide_0'=2,'wide_1'=8] {'wide_1'}, use_global_device_ids=true, to_apply=%region_24.0 | all-reduce | flops 128 | bytes 1024 | tf_op jit(solution)/shard_map/psum | solution.py:31
  289.6 0.7 multiply_add_fusion
  (93 shorter events, 9.2 us)
Async XLA Ops:
  7.2 83.0 %all-gather.2.cloned.1.call-start = ((), (), s32[]{:S(2)}) async-start(), calls=%async_computation.1 | async-start | bytes 1114112 | tf_op jit(solution)/shard_map/all_gather | solution.py:54
  8.8 50.7 %copy-start.4 = (bf16[256,128]{1,0:T(8,128)(2,1)S(1)}, bf16[256,128]{1,0:T(8,128)(2,1)}, u32[]{:S(2)}) copy-start(bf16[256,128]{1,0:T(8,128)(2,1)} %convert_element_type.38) | copy-start | bytes 196612
  8.8 55.2 %collective-permute-start.4 = (bf16[256,128]{1,0:T(8,128)(2,1)}, bf16[256,128]{1,0:T(8,128)(2,1)S(1)}, u32[]{:S(2)}, u32[]{:S(2)}) collective-permute-start(bf16[256,128]{1,0:T(8,128)(2,1)} %convert_element_type.38), channel_id=1, source_target_pairs={{0,128},{16,144},{32,160},{48,176},{64,192},{80,208},{96,224},{112... | collective-permute-start | bytes 196616 | tf_op jit(solution)/shard_map/ppermute | solution.py:16
  14.6 48.7 %collective-permute-start.3 = (bf16[256,32]{1,0:T(8,128)(2,1)}, bf16[256,32]{1,0:T(8,128)(2,1)S(1)}, u32[]{:S(2)}, u32[]{:S(2)}) collective-permute-start(bf16[256,32]{1,0:T(8,128)(2,1)} %get-tuple-element.156), channel_id=1, source_target_pairs={{0,128},{16,144},{32,160},{48,176},{64,192},{80,208},{96,224},{112... | collective-permute-start | bytes 49160 | tf_op jit(solution)/shard_map/ppermute | solution.py:16
  63.3 26.9 %copy-start.6 = (bf16[256,32]{1,0:T(8,128)(2,1)}, bf16[256,32]{1,0:T(8,128)(2,1)S(1)}, u32[]{:S(2)}) copy-start(bf16[256,32]{1,0:T(8,128)(2,1)S(1)} %collective-permute-done.3) | copy-start | bytes 49156
  64.0 26.2 %copy-start.7 = (bf16[256,128]{1,0:T(8,128)(2,1)}, bf16[256,128]{1,0:T(8,128)(2,1)S(1)}, u32[]{:S(2)}) copy-start(bf16[256,128]{1,0:T(8,128)(2,1)S(1)} %collective-permute-done.4) | copy-start | bytes 196612
  90.2 7.2 %collective-permute-start = (bf16[256,32]{1,0:T(8,128)(2,1)}, bf16[256,32]{1,0:T(8,128)(2,1)S(1)}, u32[]{:S(2)}, u32[]{:S(2)}) collective-permute-start(bf16[256,32]{1,0:T(8,128)(2,1)} %get-tuple-element.166), channel_id=1, source_target_pairs={{0,16},{16,32},{32,48},{48,64},{64,80},{80,96},{96,112},{112,128},... | collective-permute-start | bytes 49160 | tf_op jit(solution)/shard_map/while/body/eval_jaxpr/ppermute | solution.py:16
  94.8 7.2 %collective-permute-start.2 = (f32[256,128]{1,0:T(8,128)S(1)}, f32[256,128]{1,0:T(8,128)}, u32[]{:S(2)}, u32[]{:S(2)}) collective-permute-start(f32[256,128]{1,0:T(8,128)S(1)} %broadcast_select_fusion.2), channel_id=1, source_target_pairs={{0,16},{16,32},{32,48},{48,64},{64,80},{80,96},{96,112},{112,128},... | collective-permute-start | bytes 393224 | tf_op jit(solution)/shard_map/while/body/eval_jaxpr/ppermute | solution.py:16
  94.9 6.3 %collective-permute-start.1 = (bf16[256,128]{1,0:T(8,128)(2,1)S(1)}, bf16[256,128]{1,0:T(8,128)(2,1)S(1)}, u32[]{:S(2)}, u32[]{:S(2)}) collective-permute-start(bf16[256,128]{1,0:T(8,128)(2,1)S(1)} %get-tuple-element.167), channel_id=1, source_target_pairs={{0,16},{16,32},{32,48},{48,64},{64,80},{80,96},{96,112},{112,128},... | collective-permute-start | bytes 196616 | tf_op jit(solution)/shard_map/while/body/eval_jaxpr/ppermute | solution.py:16
  101.2 1.2 copy-start
  104.1 4.9 %collective-permute-start = (bf16[256,32]{1,0:T(8,128)(2,1)}, bf16[256,32]{1,0:T(8,128)(2,1)S(1)}, u32[]{:S(2)}, u32[]{:S(2)}) collective-permute-start(bf16[256,32]{1,0:T(8,128)(2,1)} %get-tuple-element.166), channel_id=1, source_target_pairs={{0,16},{16,32},{32,48},{48,64},{64,80},{80,96},{96,112},{112,128},... | collective-permute-start | bytes 49160 | tf_op jit(solution)/shard_map/while/body/eval_jaxpr/ppermute | solution.py:16
  105.6 8.1 %collective-permute-start.2 = (f32[256,128]{1,0:T(8,128)S(1)}, f32[256,128]{1,0:T(8,128)}, u32[]{:S(2)}, u32[]{:S(2)}) collective-permute-start(f32[256,128]{1,0:T(8,128)S(1)} %broadcast_select_fusion.2), channel_id=1, source_target_pairs={{0,16},{16,32},{32,48},{48,64},{64,80},{80,96},{96,112},{112,128},... | collective-permute-start | bytes 393224 | tf_op jit(solution)/shard_map/while/body/eval_jaxpr/ppermute | solution.py:16
  105.8 7.0 %collective-permute-start.1 = (bf16[256,128]{1,0:T(8,128)(2,1)S(1)}, bf16[256,128]{1,0:T(8,128)(2,1)S(1)}, u32[]{:S(2)}, u32[]{:S(2)}) collective-permute-start(bf16[256,128]{1,0:T(8,128)(2,1)S(1)} %get-tuple-element.167), channel_id=1, source_target_pairs={{0,16},{16,32},{32,48},{48,64},{64,80},{80,96},{96,112},{112,128},... | collective-permute-start | bytes 196616 | tf_op jit(solution)/shard_map/while/body/eval_jaxpr/ppermute | solution.py:16
  112.8 1.2 copy-start
  115.8 5.5 %collective-permute-start = (bf16[256,32]{1,0:T(8,128)(2,1)}, bf16[256,32]{1,0:T(8,128)(2,1)S(1)}, u32[]{:S(2)}, u32[]{:S(2)}) collective-permute-start(bf16[256,32]{1,0:T(8,128)(2,1)} %get-tuple-element.166), channel_id=1, source_target_pairs={{0,16},{16,32},{32,48},{48,64},{64,80},{80,96},{96,112},{112,128},... | collective-permute-start | bytes 49160 | tf_op jit(solution)/shard_map/while/body/eval_jaxpr/ppermute | solution.py:16
  116.3 9.6 %collective-permute-start.2 = (f32[256,128]{1,0:T(8,128)S(1)}, f32[256,128]{1,0:T(8,128)}, u32[]{:S(2)}, u32[]{:S(2)}) collective-permute-start(f32[256,128]{1,0:T(8,128)S(1)} %broadcast_select_fusion.2), channel_id=1, source_target_pairs={{0,16},{16,32},{32,48},{48,64},{64,80},{80,96},{96,112},{112,128},... | collective-permute-start | bytes 393224 | tf_op jit(solution)/shard_map/while/body/eval_jaxpr/ppermute | solution.py:16
  117.5 7.6 %collective-permute-start.1 = (bf16[256,128]{1,0:T(8,128)(2,1)S(1)}, bf16[256,128]{1,0:T(8,128)(2,1)S(1)}, u32[]{:S(2)}, u32[]{:S(2)}) collective-permute-start(bf16[256,128]{1,0:T(8,128)(2,1)S(1)} %get-tuple-element.167), channel_id=1, source_target_pairs={{0,16},{16,32},{32,48},{48,64},{64,80},{80,96},{96,112},{112,128},... | collective-permute-start | bytes 196616 | tf_op jit(solution)/shard_map/while/body/eval_jaxpr/ppermute | solution.py:16
  125.1 1.2 copy-start
  128.0 6.1 %collective-permute-start = (bf16[256,32]{1,0:T(8,128)(2,1)}, bf16[256,32]{1,0:T(8,128)(2,1)S(1)}, u32[]{:S(2)}, u32[]{:S(2)}) collective-permute-start(bf16[256,32]{1,0:T(8,128)(2,1)} %get-tuple-element.166), channel_id=1, source_target_pairs={{0,16},{16,32},{32,48},{48,64},{64,80},{80,96},{96,112},{112,128},... | collective-permute-start | bytes 49160 | tf_op jit(solution)/shard_map/while/body/eval_jaxpr/ppermute | solution.py:16
  128.1 10.6 %collective-permute-start.2 = (f32[256,128]{1,0:T(8,128)S(1)}, f32[256,128]{1,0:T(8,128)}, u32[]{:S(2)}, u32[]{:S(2)}) collective-permute-start(f32[256,128]{1,0:T(8,128)S(1)} %broadcast_select_fusion.2), channel_id=1, source_target_pairs={{0,16},{16,32},{32,48},{48,64},{64,80},{80,96},{96,112},{112,128},... | collective-permute-start | bytes 393224 | tf_op jit(solution)/shard_map/while/body/eval_jaxpr/ppermute | solution.py:16
  129.1 8.8 %collective-permute-start.1 = (bf16[256,128]{1,0:T(8,128)(2,1)S(1)}, bf16[256,128]{1,0:T(8,128)(2,1)S(1)}, u32[]{:S(2)}, u32[]{:S(2)}) collective-permute-start(bf16[256,128]{1,0:T(8,128)(2,1)S(1)} %get-tuple-element.167), channel_id=1, source_target_pairs={{0,16},{16,32},{32,48},{48,64},{64,80},{80,96},{96,112},{112,128},... | collective-permute-start | bytes 196616 | tf_op jit(solution)/shard_map/while/body/eval_jaxpr/ppermute | solution.py:16
  138.0 1.2 copy-start
  140.9 6.1 %collective-permute-start = (bf16[256,32]{1,0:T(8,128)(2,1)}, bf16[256,32]{1,0:T(8,128)(2,1)S(1)}, u32[]{:S(2)}, u32[]{:S(2)}) collective-permute-start(bf16[256,32]{1,0:T(8,128)(2,1)} %get-tuple-element.166), channel_id=1, source_target_pairs={{0,16},{16,32},{32,48},{48,64},{64,80},{80,96},{96,112},{112,128},... | collective-permute-start | bytes 49160 | tf_op jit(solution)/shard_map/while/body/eval_jaxpr/ppermute | solution.py:16
  141.0 10.6 %collective-permute-start.2 = (f32[256,128]{1,0:T(8,128)S(1)}, f32[256,128]{1,0:T(8,128)}, u32[]{:S(2)}, u32[]{:S(2)}) collective-permute-start(f32[256,128]{1,0:T(8,128)S(1)} %broadcast_select_fusion.2), channel_id=1, source_target_pairs={{0,16},{16,32},{32,48},{48,64},{64,80},{80,96},{96,112},{112,128},... | collective-permute-start | bytes 393224 | tf_op jit(solution)/shard_map/while/body/eval_jaxpr/ppermute | solution.py:16
  141.1 9.7 %collective-permute-start.1 = (bf16[256,128]{1,0:T(8,128)(2,1)S(1)}, bf16[256,128]{1,0:T(8,128)(2,1)S(1)}, u32[]{:S(2)}, u32[]{:S(2)}) collective-permute-start(bf16[256,128]{1,0:T(8,128)(2,1)S(1)} %get-tuple-element.167), channel_id=1, source_target_pairs={{0,16},{16,32},{32,48},{48,64},{64,80},{80,96},{96,112},{112,128},... | collective-permute-start | bytes 196616 | tf_op jit(solution)/shard_map/while/body/eval_jaxpr/ppermute | solution.py:16
  150.8 1.2 copy-start
  153.7 6.1 %collective-permute-start = (bf16[256,32]{1,0:T(8,128)(2,1)}, bf16[256,32]{1,0:T(8,128)(2,1)S(1)}, u32[]{:S(2)}, u32[]{:S(2)}) collective-permute-start(bf16[256,32]{1,0:T(8,128)(2,1)} %get-tuple-element.166), channel_id=1, source_target_pairs={{0,16},{16,32},{32,48},{48,64},{64,80},{80,96},{96,112},{112,128},... | collective-permute-start | bytes 49160 | tf_op jit(solution)/shard_map/while/body/eval_jaxpr/ppermute | solution.py:16
  153.9 10.6 %collective-permute-start.2 = (f32[256,128]{1,0:T(8,128)S(1)}, f32[256,128]{1,0:T(8,128)}, u32[]{:S(2)}, u32[]{:S(2)}) collective-permute-start(f32[256,128]{1,0:T(8,128)S(1)} %broadcast_select_fusion.2), channel_id=1, source_target_pairs={{0,16},{16,32},{32,48},{48,64},{64,80},{80,96},{96,112},{112,128},... | collective-permute-start | bytes 393224 | tf_op jit(solution)/shard_map/while/body/eval_jaxpr/ppermute | solution.py:16
  154.0 9.7 %collective-permute-start.1 = (bf16[256,128]{1,0:T(8,128)(2,1)S(1)}, bf16[256,128]{1,0:T(8,128)(2,1)S(1)}, u32[]{:S(2)}, u32[]{:S(2)}) collective-permute-start(bf16[256,128]{1,0:T(8,128)(2,1)S(1)} %get-tuple-element.167), channel_id=1, source_target_pairs={{0,16},{16,32},{32,48},{48,64},{64,80},{80,96},{96,112},{112,128},... | collective-permute-start | bytes 196616 | tf_op jit(solution)/shard_map/while/body/eval_jaxpr/ppermute | solution.py:16
  163.7 1.2 copy-start
  166.6 6.1 %collective-permute-start = (bf16[256,32]{1,0:T(8,128)(2,1)}, bf16[256,32]{1,0:T(8,128)(2,1)S(1)}, u32[]{:S(2)}, u32[]{:S(2)}) collective-permute-start(bf16[256,32]{1,0:T(8,128)(2,1)} %get-tuple-element.166), channel_id=1, source_target_pairs={{0,16},{16,32},{32,48},{48,64},{64,80},{80,96},{96,112},{112,128},... | collective-permute-start | bytes 49160 | tf_op jit(solution)/shard_map/while/body/eval_jaxpr/ppermute | solution.py:16
  166.7 10.6 %collective-permute-start.2 = (f32[256,128]{1,0:T(8,128)S(1)}, f32[256,128]{1,0:T(8,128)}, u32[]{:S(2)}, u32[]{:S(2)}) collective-permute-start(f32[256,128]{1,0:T(8,128)S(1)} %broadcast_select_fusion.2), channel_id=1, source_target_pairs={{0,16},{16,32},{32,48},{48,64},{64,80},{80,96},{96,112},{112,128},... | collective-permute-start | bytes 393224 | tf_op jit(solution)/shard_map/while/body/eval_jaxpr/ppermute | solution.py:16
  166.8 9.7 %collective-permute-start.1 = (bf16[256,128]{1,0:T(8,128)(2,1)S(1)}, bf16[256,128]{1,0:T(8,128)(2,1)S(1)}, u32[]{:S(2)}, u32[]{:S(2)}) collective-permute-start(bf16[256,128]{1,0:T(8,128)(2,1)S(1)} %get-tuple-element.167), channel_id=1, source_target_pairs={{0,16},{16,32},{32,48},{48,64},{64,80},{80,96},{96,112},{112,128},... | collective-permute-start | bytes 196616 | tf_op jit(solution)/shard_map/while/body/eval_jaxpr/ppermute | solution.py:16
  176.5 1.2 copy-start
  184.4 4.7 %copy-start.2 = (f32[256,128]{1,0:T(8,128)S(1)}, f32[256,128]{1,0:T(8,128)}, u32[]{:S(2)}) copy-start(f32[256,128]{1,0:T(8,128)} %param.12) | copy-start | bytes 393220
  184.4 25.4 %copy-start.1 = (f32[256,128]{1,0:T(8,128)S(1)}, f32[256,128]{1,0:T(8,128)}, u32[]{:S(2)}) copy-start(f32[256,128]{1,0:T(8,128)} %param.13) | copy-start | bytes 393220
  184.4 67.8 %copy-start.5 = (f32[256,128]{1,0:T(8,128)S(1)}, f32[256,128]{1,0:T(8,128)}, u32[]{:S(2)}) copy-start(f32[256,128]{1,0:T(8,128)} %param.11) | copy-start | bytes 393220
  184.4 25.2 %all-to-all-start = ((bf16[16,256,128]{2,1,0:T(8,128)(2,1)}), bf16[16,256,128]{2,1,0:T(8,128)(2,1)S(1)}, u32[]{:S(2)}, u32[]{:S(2)}) async-start(bf16[16,256,128]{2,1,0:T(8,128)(2,1)} %bitcast.25), calls=%async_computation | async-start | bytes 2097152 | tf_op jit(solution)/shard_map/all_to_all | solution.py:26
  189.2 20.6 %collective-permute-start.5 = (f32[256,128]{1,0:T(8,128)S(1)}, f32[256,128]{1,0:T(8,128)S(1)}, u32[]{:S(2)}, u32[]{:S(2)}) collective-permute-start(f32[256,128]{1,0:T(8,128)S(1)} %get-tuple-element.47), channel_id=1, source_target_pairs={{0,144},{16,160},{32,176},{48,192},{64,208},{80,224},{96,240},{112... | collective-permute-start | bytes 393224 | tf_op jit(solution)/shard_map/ppermute | solution.py:16
  252.9 37.4 %copy-start.3 = (f32[256,128]{1,0:T(8,128)}, f32[256,128]{1,0:T(8,128)S(1)}, u32[]{:S(2)}) copy-start(f32[256,128]{1,0:T(8,128)S(1)} %get-tuple-element.102) | copy-start | bytes 393220
Sparse Core Ops, SparseCore 0:
  11.2 78.9 all-gather.1
where the time goes:
time: 303 us; the launch traced here: 297 us
  blocking collectives  123 us (41%)
  waiting for transfers between devices  61.4 us (20%)
  matrix products  47.5 us (16%)
  starting transfers between devices  34.7 us (11%)
  between operations  14.8 us (5%)
  local copies, waits for them, and re-layouts  8.23 us (3%)
  other arithmetic  6.7 us (2%)
    psum x10, blocking collectives, over_axes(): return functools.reduce(lax.psum, axes, x)  79.1 us
    all_gather x1, blocking collectives, on_device(): lax.all_gather(scaled, WIDE, axis=0, tiled=True)  44.2 us
    ppermute x24, starting transfers between devices, shifted(): return lax.ppermute(x, axis, [(i, (i + by) % count) for i in range(count)])  30.7 us
    all_gather x1, waiting for transfers between devices, on_device(): lax.all_gather(low_dir, WIDE, axis=0, tiled=True)  26.2 us
    dot_general x7, matrix products, kernel_tile(): lax.dot_general(rows_x, cols_x, (((1,), (1,)), ((), ())), preferred_eleme...  21.6 us
    all_to_all x1, waiting for transfers between devices, sent_and_summed(): blocks = lax.all_to_all(cut_along(x, dim, count), axis, 0, 0, tiled=True)  19.9 us
    ppermute x24, waiting for transfers between devices, shifted(): return lax.ppermute(x, axis, [(i, (i + by) % count) for i in range(count)])  15.4 us
    dot_general x7, matrix products, paired_turn(): lax.dot_general(kernel_block, block_p, (((0,), (0,)), ((), ())), preferre...  11.7 us
  transfers between devices with their start and end apart: 26, of which 7 were waited for; matrix products, arithmetic and copies ran while one was open for 13% of the time, Pallas kernels for 0%

commit v1 on v0

v1 whole, which is shorter than its diff:
```python
import functools
import math

import jax
import jax.numpy as jnp
from jax import lax
from jax.experimental import pallas as pl
from jax.experimental.pallas import tpu as pltpu
from jax.sharding import Mesh
from jax.sharding import PartitionSpec as P

AXES = ("x", "yl", "c", "yh", "z")
ROWS = ("x", "yl")
PLANE = ("x", "yl", "c", "yh")
FEATURES = 32
SCALE = 5.0 / 3.0
ROOT3 = math.sqrt(3.0)
LOG2E = 1.4426950408889634
VMEM = pltpu.CompilerParams(vmem_limit_bytes=48 * 2**20)


def split3(v):
    one = v.astype(jnp.bfloat16).astype(jnp.float32)
    rest = v - one
    two = rest.astype(jnp.bfloat16).astype(jnp.float32)
    return one, two, (rest - two)


def augmented(x4, quarter, is_row):
    k = lax.broadcasted_iota(jnp.int32, (128, 128), 0)
    l = lax.broadcasted_iota(jnp.int32, (128, 128), 1)
    mine = k // FEATURES == quarter
    spread = mine & (l < 96) & (k % FEATURES == l % FEATURES)
    total = mine & (l >= 96) & (l < 102)
    wide = x4.astype(jnp.float32)
    square = wide * wide
    high = square.astype(jnp.bfloat16)
    low = (square - high.astype(jnp.float32)).astype(jnp.bfloat16)
    to = lambda m: jnp.where(m, 1.0, 0.0).astype(jnp.bfloat16)
    dot = functools.partial(jnp.dot, preferred_element_type=jnp.float32)
    v = dot(x4, to(spread)) + dot(high, to(total)) + dot(low, to(total))
    lane = lax.broadcasted_iota(jnp.int32, (1, 128), 1)
    if is_row:
        one, two, three = split3(v * SCALE)
        tail = jnp.where(lane == 96, one, jnp.where(lane == 97, two, three))
        tail = jnp.where(lane < 99, tail, jnp.where(lane < 102, 1.0, 0.0))
        out = jnp.where(lane < 96, v, tail)
    else:
        one, two, three = split3(v * jnp.where(lane < 96, -2.0 * SCALE, SCALE))
        first = (lane < 32) | (lane == 99)
        second = ((lane >= 32) & (lane < 64)) | (lane == 100)
        out = jnp.where(first, one, jnp.where(second, two, three))
        out = jnp.where((lane >= 96) & (lane < 99), 1.0, out)
        out = jnp.where(lane < 102, out, 0.0)
    return out.astype(jnp.bfloat16)


def rows_kernel(x_ref, out_ref):
    n = x_ref.shape[0]
    x4 = x_ref[...].reshape(n * 64, 128)
    for q in range(4):
        out_ref[:, q * 64 : (q + 1) * 64, :] = augmented(x4, q, True).reshape(n, 64, 128)


def matern(u):
    m = jnp.maximum(u, 1e-30)
    t = m * lax.rsqrt(m)
    return (((1.0 + m) + ROOT3 * t) * jnp.exp2((-ROOT3 * LOG2E) * t)).astype(jnp.bfloat16)


def tiles_kernel(n_bundles, has_sum, last, row_tile, *refs):
    rows_ref, bundles, refs = refs[0], refs[1 : 1 + n_bundles], refs[1 + n_bundles :]
    if has_sum:
        sum_ref, refs = refs[0], refs[1:]
    out_ref, cols_ref, dirs_ref, acc_ref = refs
    pieces = bundles[0].shape[0]
    for b, bundle in enumerate(bundles):
        here = slice(b * pieces, (b + 1) * pieces)
        dirs_ref[here] = bundle[:, :256, :]
        x4 = bundle[:, 256:, :].reshape(pieces * 64, 128)
        for q in range(4):
            cols_ref[here, q * 64 : (q + 1) * 64, :] = augmented(x4, q, False).reshape(pieces, 64, 128)
    count = rows_ref.shape[0]

    def turn(n, first):
        for i in range(count // row_tile):
            at = slice(i * row_tile, (i + 1) * row_tile)
            u = lax.dot_general(
                rows_ref[at, :], cols_ref[n], (((1,), (1,)), ((), ())), preferred_element_type=jnp.float32
            )
            part = jnp.dot(matern(u), dirs_ref[n], preferred_element_type=jnp.float32)
            if first is None:
                acc_ref[at, :] = acc_ref[at, :] + part
            elif first:
                acc_ref[at, :] = part
            else:
                acc_ref[at, :] = sum_ref[at, :] + part

    turn(0, not has_sum)

    def body(n, _):
        turn(n, None)
        return 0

    lax.fori_loop(1, n_bundles * pieces, body, 0)
    out_ref[...] = acc_ref[...].astype(out_ref.dtype)


def tiles(rows, bundles, so_far, last):
    pieces = bundles[0].shape[0]
    n = len(bundles) * pieces
    count = rows.shape[0]
    args = (rows, *bundles) + (() if so_far is None else (so_far,))
    whole = pl.BlockSpec(memory_space=pltpu.VMEM)
    return pl.pallas_call(
        functools.partial(tiles_kernel, len(bundles), so_far is not None, last, min(count, 1024)),
        out_shape=jax.ShapeDtypeStruct((count, 128), jnp.bfloat16 if last else jnp.float32),
        in_specs=[whole] * len(args),
        out_specs=whole,
        scratch_shapes=[
            pltpu.VMEM((n, 256, 128), jnp.bfloat16),
            pltpu.VMEM((n, 256, 128), jnp.bfloat16),
            pltpu.VMEM((count, 128), jnp.float32),
        ],
        compiler_params=VMEM,
        cost_estimate=pl.CostEstimate(
            flops=2 * count * n * 256 * 256 * 2, bytes_accessed=2 * count * 128 * 4, transcendentals=count * n * 512
        ),
    )(*args)


def image_kernel(parts_ref, noise_ref, dir_ref, res_ref, image_ref, sums_ref):
    image = jnp.sum(parts_ref[...].astype(jnp.float32), axis=0) + noise_ref[0, 0] * dir_ref[...]
    image_ref[...] = image
    res = res_ref[...]
    col = lambda v: jnp.sum(v, axis=0, keepdims=True)
    sums_ref[0:1, :] = col(res * res)
    sums_ref[1:2, :] = col(dir_ref[...] * image)
    sums_ref[2:3, :] = col(res * image)
    sums_ref[3:4, :] = col(image * image)
    sums_ref[4:8, :] = jnp.zeros((4, 128), jnp.float32)


def step_kernel(sums_ref, image_ref, sol_ref, res_ref, dir_ref, new_sol, new_res, new_dir):
    sums = jnp.sum(sums_ref[...], axis=0)
    old_norm, curvature, cross, image_sq = (sums[i : i + 1, :] for i in range(4))
    step = old_norm / curvature
    new_norm = jnp.maximum(old_norm - 2.0 * step * cross + step * step * image_sq, 0.0)
    direction = dir_ref[...]
    new_sol[...] = sol_ref[...] + step * direction
    residual = res_ref[...] - step * image_ref[...]
    new_res[...] = residual
    new_dir[...] = residual + (new_norm / old_norm) * direction


def turned(x, axis, by):
    count = lax.axis_size(axis)
    return lax.ppermute(x, axis, [(i, (i + by) % count) for i in range(count)])


def from_all(x, axes):
    count = lax.axis_size(axes)
    return lax.all_to_all(jnp.broadcast_to(x[None], (count,) + x.shape), axes, 0, 0, tiled=True)


def on_device(points, inv_length, noise_var, solution, residual, direction):
    scaled = (points.astype(jnp.float32) * inv_length).astype(jnp.bfloat16)
    x4 = jnp.concatenate([scaled[q * 64 : (q + 1) * 64] for q in range(4)], axis=1)
    packed = jnp.concatenate([direction.astype(jnp.bfloat16), x4], axis=0)[None]
    pair = jnp.concatenate([packed, turned(packed, "yh", 1)], axis=0)
    whole = pl.BlockSpec(memory_space=pltpu.VMEM)

    n_rows = lax.axis_size(ROWS)
    rows = pl.pallas_call(
        rows_kernel,
        out_shape=jax.ShapeDtypeStruct((n_rows, 256, 128), jnp.bfloat16),
        in_specs=[whole],
        out_specs=whole,
        compiler_params=VMEM,
    )(from_all(x4, ROWS)).reshape(n_rows * 256, 128)

    length = lax.axis_size("z")
    up = down = pair
    so_far = None
    here = [pair]
    for hop in range(length // 2 + 1):
        bundles = [b for h in here for b in (h, turned(h, "c", 1))]
        if hop < length // 2 - 1:
            up, down = turned(up, "z", 1), turned(down, "z", -1)
            here = [up, down]
        else:
            up = turned(up, "z", 1)
            here = [up]
        so_far = tiles(rows, bundles, so_far, hop == length // 2)
    parts = lax.all_to_all(so_far.reshape(n_rows, 256, 128), ROWS, 0, 0, tiled=True)
    f32 = jax.ShapeDtypeStruct(direction.shape, jnp.float32)
    image, sums = pl.pallas_call(
        image_kernel,
        out_shape=(f32, jax.ShapeDtypeStruct((8, 128), jnp.float32)),
        in_specs=[whole, pl.BlockSpec(memory_space=pltpu.SMEM), whole, whole],
        out_specs=(whole, whole),
        compiler_params=VMEM,
    )(parts, noise_var.reshape(1, 1), direction, residual)
    sums = jnp.sum(from_all(sums, PLANE), axis=0)
    sums = from_all(sums, ("z",))
    return pl.pallas_call(
        step_kernel,
        out_shape=(f32, f32, f32),
        in_specs=[whole] * 5,
        out_specs=(whole,) * 3,
        compiler_params=VMEM,
    )(sums, image, solution, residual, direction)


def solution(mesh):
    finer = Mesh(mesh.devices.reshape(4, 2, 2, 2, 8), AXES)
    placed = P(AXES, None)
    return jax.shard_map(
        on_device,
        mesh=finer,
        in_specs=(placed, P(), P(), placed, placed, placed),
        out_specs=(placed,) * 3,
        check_vma=False,
    )
```

time: 303 us -> 111 us (0.37); the launches traced: 297 us -> 111 us
  blocking collectives: 123 us -> 36.5 us
  waiting for transfers between devices: 61.4 us -> 10.6 us
  matrix products: 47.5 us -> 0 us
  Pallas kernels: 0 us -> 35.5 us
  between operations: 14.8 us -> 1.45 us
  starting transfers between devices: 34.7 us -> 24.7 us
  local copies, waits for them, and re-layouts: 8.23 us -> 1.75 us
  other arithmetic: 6.7 us -> 0.26 us
    psum x10 -> x0, blocking collectives: 79.1 us -> none  [over_axes(): return functools.reduce(lax.psum, axes, x)]
    dot_general x23 -> x0, matrix products: 47.5 us -> none  [the longest x7 21.6 us: kernel_tile(): lax.dot_general(rows_x, cols_x, (((1,), (1,)), ((), ())), preferred_eleme...]
    all_gather x1 -> x0, blocking collectives: 44.2 us -> none  [on_device(): lax.all_gather(scaled, WIDE, axis=0, tiled=True)]
    all_to_all x0 -> x3, blocking collectives: none -> 36.5 us  [from_all(): lax.all_to_all(jnp.broadcast_to(x[None], (count,) + x.shape), axes, 0, 0,...]
    pallas_call x0 -> x8, Pallas kernels: none -> 35.5 us  [the longest x5 33.9 us: tiles(): pl.pallas_call(functools.partial(tiles_kernel, len(bundles), so_far is no...]
    all_gather x1 -> x0, waiting for transfers between devices: 26.2 us -> none  [on_device(): lax.all_gather(low_dir, WIDE, axis=0, tiled=True)]
    ppermute x24 -> x16, waiting for transfers between devices: 15.4 us -> 1.87 us  [turned(): return lax.ppermute(x, axis, [(i, (i + by) % count) for i in range(count)])]
    all_to_all x1, waiting for transfers between devices: 19.9 us -> 8.7 us  [on_device(): lax.all_to_all(so_far.reshape(n_rows, 256, 128), ROWS, 0, 0, tiled=True)]
  transfers between devices with their start and end apart: 26 -> 17, of which waited for: 7 -> 2; matrix products, arithmetic and copies ran while one was open for 13% -> 0% of each run, Pallas kernels for 0% -> 27%
where the time goes in v1:
time: 111 us
  blocking collectives  36.5 us (33%)
  Pallas kernels  35.5 us (32%)
  starting transfers between devices  24.7 us (22%)
  waiting for transfers between devices  10.6 us (10%)
  local copies, waits for them, and re-layouts  1.75 us (2%)
  between operations  1.45 us (1%)
    all_to_all x3, blocking collectives, from_all(): lax.all_to_all(jnp.broadcast_to(x[None], (count,) + x.shape), axes, 0, 0,...  36.5 us
    pallas_call x5, Pallas kernels, tiles(): pl.pallas_call(functools.partial(tiles_kernel, len(bundles), so_far is no...  33.9 us
    ppermute x16, starting transfers between devices, turned(): return lax.ppermute(x, axis, [(i, (i + by) % count) for i in range(count)])  21.1 us
    all_to_all x1, waiting for transfers between devices, on_device(): lax.all_to_all(so_far.reshape(n_rows, 256, 128), ROWS, 0, 0, tiled=True)  8.7 us
    all_to_all x1, starting transfers between devices, on_device(): lax.all_to_all(so_far.reshape(n_rows, 256, 128), ROWS, 0, 0, tiled=True)  3.62 us
  transfers between devices with their start and end apart: 17, of which 2 were waited for; matrix products, arithmetic and copies ran while one was open for 0% of the time, Pallas kernels for 27%

profile of v1, /device:TPU:1, one launch (start us, length us, event | category | flops | bytes accessed | tf_op | source)
XLA Modules:
  0.0 110.7 jit_solution(6905433237083197970)
XLA Ops:
  0.6 0.0 copy-start.3
  0.6 0.8 copy.10
  1.5 0.0 copy-done.3
  1.5 0.0 copy-start
  1.5 0.9 copy-done
  2.4 0.1 maximum_bitcast_fusion
  2.5 3.8 %collective-permute-start = (bf16[1,320,128]{2,1,0:T(8,128)(2,1)S(1)}, bf16[1,320,128]{2,1,0:T(8,128)(2,1)S(1)}, u32[]{:S(2)}, u32[]{:S(2)}) collective-permute-start(bf16[1,320,128]{2,1,0:T(8,128)(2,1)S(1)} %maximum_bitcast_fusion), channel_id=1, source_target_pairs={{0,8},{8,0},{1,9},{9,1},{2,10},{10,2},{3,11},{11,3},{4,12},{12,4},... | collective-permute-start | bytes 245768 | tf_op jit(solution)/shard_map/ppermute | solution.py:158
  6.3 1.8 %collective-permute-done = bf16[1,320,128]{2,1,0:T(8,128)(2,1)S(1)} collective-permute-done((bf16[1,320,128]{2,1,0:T(8,128)(2,1)S(1)}, bf16[1,320,128]{2,1,0:T(8,128)(2,1)S(1)}, u32[]{:S(2)}, u32[]{:S(2)}) %collective-permute-start) | collective-permute-done | bytes 81952 | tf_op jit(solution)/shard_map/ppermute | solution.py:158
  8.2 3.7 %collective-permute-start.15 = (bf16[2,320,128]{2,1,0:T(8,128)(2,1)S(1)}, bf16[2,320,128]{2,1,0:T(8,128)(2,1)S(1)}, u32[]{:S(2)}, u32[]{:S(2)}) collective-permute-start(bf16[2,320,128]{2,1,0:T(8,128)(2,1)S(1)} %pad_maximum_fusion.refs_1_), channel_id=1, source_target_pairs={{0,16},{16,0},{1,17},{17,1},{2,18},{18,2},{3,19},{19,3},{4,20},{20... | collective-permute-start | bytes 491528 | tf_op jit(solution)/shard_map/ppermute | solution.py:158
  11.9 0.0 collective-permute-start.1
  11.9 3.8 %collective-permute-start.7 = (bf16[2,320,128]{2,1,0:T(8,128)(2,1)S(1)}, bf16[2,320,128]{2,1,0:T(8,128)(2,1)S(1)}, u32[]{:S(2)}, u32[]{:S(2)}) collective-permute-start(bf16[2,320,128]{2,1,0:T(8,128)(2,1)S(1)} %pad_maximum_fusion.refs_1_), channel_id=1, source_target_pairs={{0,7},{1,0},{2,1},{3,2},{4,3},{5,4},{6,5},{7,6},{8,15},{9,8},{10,9... | collective-permute-start | bytes 491528 | tf_op jit(solution)/shard_map/ppermute | solution.py:158
  15.7 0.1 pad_maximum_fusion.1
  15.8 10.2 %all_to_all.20.x_ref = bf16[8,64,128]{2,1,0:T(8,128)(2,1)S(1)} all-to-all(bf16[8,64,128]{2,1,0:T(8,128)(2,1)S(1)} %broadcast_in_dim.8), channel_id=1, replica_groups=mesh['x'=4,'yl'=2,'c'=2,'yh'=2,'z'=8] {'x','yl'}, dimensions={0} | all-to-all | bytes 262144 | tf_op jit(solution)/shard_map/all_to_all | solution.py:163
  26.1 0.7 shard_map.85
  26.8 0.0 collective-permute-done.1.refs_1_
  26.8 1.8 %collective-permute-start.13 = (bf16[2,320,128]{2,1,0:T(8,128)(2,1)S(1)}, bf16[2,320,128]{2,1,0:T(8,128)(2,1)S(1)}, u32[]{:S(2)}, u32[]{:S(2)}) collective-permute-start(bf16[2,320,128]{2,1,0:T(8,128)(2,1)S(1)} %collective-permute-done.1.refs_1_), channel_id=1, source_target_pairs={{0,16},{16,0},{1,17},{17,1},{2,18},{18,2},{3,19},{19,3},{4,20},{20... | collective-permute-start | bytes 491528 | tf_op jit(solution)/shard_map/ppermute | solution.py:158
  28.6 0.0 collective-permute-start.2
  28.6 0.0 collective-permute-done.7.refs_3_
  28.6 0.2 collective-permute-start.14
  28.8 2.8 %collective-permute-start.8 = (bf16[2,320,128]{2,1,0:T(8,128)(2,1)S(1)}, bf16[2,320,128]{2,1,0:T(8,128)(2,1)S(1)}, u32[]{:S(2)}, u32[]{:S(2)}) collective-permute-start(bf16[2,320,128]{2,1,0:T(8,128)(2,1)S(1)} %collective-permute-done.7.refs_3_), channel_id=1, source_target_pairs={{0,7},{1,0},{2,1},{3,2},{4,3},{5,4},{6,5},{7,6},{8,15},{9,8},{10,9... | collective-permute-start | bytes 491528 | tf_op jit(solution)/shard_map/ppermute | solution.py:158
  31.7 0.0 collective-permute-done.15.refs_2_
  31.7 4.2 %shard_map.86.refs_5_ = f32[2048,128]{1,0:T(8,128)S(1)} custom-call(bf16[2048,128]{1,0:T(8,128)(2,1)S(1)} %bitcast.6, bf16[2,320,128]{2,1,0:T(8,128)(2,1)S(1)} %pad_maximum_fusion.refs_1_, bf16[2,320,128]{2,1,0:T(8,128)(2,1)S(1)} %collective-permute-done.15.refs_2_), custom_call_target="tpu_custom_call" | custom-call | flops 2147483648 | bytes 2097152 | tf_op jit(solution)/shard_map/pallas_call | solution.py:115
  35.8 0.0 collective-permute-done.2.refs_1_
  35.8 0.6 collective-permute-start.11
  36.4 0.0 collective-permute-start.3
  36.5 0.0 collective-permute-done.8.refs_3_
  36.5 0.1 collective-permute-start.12
  36.6 0.0 collective-permute-done.13.refs_2_
  36.6 2.9 %collective-permute-start.9 = (bf16[2,320,128]{2,1,0:T(8,128)(2,1)S(1)}, bf16[2,320,128]{2,1,0:T(8,128)(2,1)S(1)}, u32[]{:S(2)}, u32[]{:S(2)}) collective-permute-start(bf16[2,320,128]{2,1,0:T(8,128)(2,1)S(1)} %collective-permute-done.8.refs_3_), channel_id=1, source_target_pairs={{0,7},{1,0},{2,1},{3,2},{4,3},{5,4},{6,5},{7,6},{8,15},{9,8},{10,9... | collective-permute-start | bytes 491528 | tf_op jit(solution)/shard_map/ppermute | solution.py:158
  39.5 0.0 collective-permute-done.14.refs_4_
  39.5 8.2 %shard_map.87.refs_5_ = f32[2048,128]{1,0:T(8,128)S(1)} custom-call(bf16[2048,128]{1,0:T(8,128)(2,1)S(1)} %bitcast.7, bf16[2,320,128]{2,1,0:T(8,128)(2,1)S(1)} %collective-permute-done.1.refs_1_, bf16[2,320,128]{2,1,0:T(8,128)(2,1)S(1)} %collective-permute-done.13.refs_2_, bf16[2,320,128]{2,1,0:T(8,128)(2,1)S(1)} %collective-permute-done.7.refs_3_, ...), custom_call_target="tpu_custom_call" | custom-call | flops 4294967296 | bytes 2097152 | tf_op jit(solution)/shard_map/pallas_call | solution.py:115
  47.7 0.0 collective-permute-done.3.refs_1_
  47.8 0.6 collective-permute-start.6
  48.4 0.0 collective-permute-start.4
  48.4 0.0 collective-permute-done.9.refs_3_
  48.4 0.2 collective-permute-start.10
  48.6 0.0 collective-permute-done.11.refs_2_
  48.6 0.0 collective-permute-done.12.refs_4_
  48.6 8.2 %shard_map.88.refs_5_ = f32[2048,128]{1,0:T(8,128)S(1)} custom-call(bf16[2048,128]{1,0:T(8,128)(2,1)S(1)} %bitcast.8, bf16[2,320,128]{2,1,0:T(8,128)(2,1)S(1)} %collective-permute-done.2.refs_1_, bf16[2,320,128]{2,1,0:T(8,128)(2,1)S(1)} %collective-permute-done.11.refs_2_, bf16[2,320,128]{2,1,0:T(8,128)(2,1)S(1)} %collective-permute-done.8.refs_3_, ...), custom_call_target="tpu_custom_call" | custom-call | flops 4294967296 | bytes 2097152 | tf_op jit(solution)/shard_map/pallas_call | solution.py:115
  56.8 0.0 collective-permute-done.4.refs_1_
  56.8 0.4 collective-permute-start.5
  57.2 0.0 collective-permute-done.6.refs_2_
  57.2 0.0 collective-permute-done.10.refs_4_
  57.2 8.2 %shard_map.89.refs_3_ = f32[2048,128]{1,0:T(8,128)S(1)} custom-call(bf16[2048,128]{1,0:T(8,128)(2,1)S(1)} %bitcast.9, bf16[2,320,128]{2,1,0:T(8,128)(2,1)S(1)} %collective-permute-done.3.refs_1_, bf16[2,320,128]{2,1,0:T(8,128)(2,1)S(1)} %collective-permute-done.6.refs_2_, bf16[2,320,128]{2,1,0:T(8,128)(2,1)S(1)} %collective-permute-done.9.refs_3_, ...), custom_call_target="tpu_custom_call" | custom-call | flops 4294967296 | bytes 2097152 | tf_op jit(solution)/shard_map/pallas_call | solution.py:115
  65.5 0.0 collective-permute-done.5.refs_2_
  65.5 5.0 %shard_map.90 = bf16[2048,128]{1,0:T(8,128)(2,1)} custom-call(bf16[2048,128]{1,0:T(8,128)(2,1)S(1)} %bitcast.10, bf16[2,320,128]{2,1,0:T(8,128)(2,1)S(1)} %collective-permute-done.4.refs_1_, bf16[2,320,128]{2,1,0:T(8,128)(2,1)S(1)} %collective-permute-done.5.refs_2_, f32[2048,128]{1,0:T(8,128)S(1)} %shard_map.89.refs_3_), custom_call_target="tpu_custom_call" | custom-call | flops 2147483648 | bytes 2097152 | tf_op jit(solution)/shard_map/pallas_call | solution.py:115
  70.5 0.0 copy-start.1
  70.5 3.6 %all-to-all-start.1 = ((bf16[8,256,128]{2,1,0:T(8,128)(2,1)}), bf16[8,256,128]{2,1,0:T(8,128)(2,1)S(1)}, u32[]{:S(2)}, u32[]{:S(2)}) async-start(bf16[8,256,128]{2,1,0:T(8,128)(2,1)} %bitcast.2), calls=%async_computation.1 | async-start | bytes 1048576 | tf_op jit(solution)/shard_map/all_to_all | solution.py:195
  74.8 8.7 %all-to-all-done.1.parts_ref = bf16[8,256,128]{2,1,0:T(8,128)(2,1)S(1)} async-done(((bf16[8,256,128]{2,1,0:T(8,128)(2,1)}), bf16[8,256,128]{2,1,0:T(8,128)(2,1)S(1)}, u32[]{:S(2)}, u32[]{:S(2)}) %all-to-all-start.1) | async-done | bytes 524320 | tf_op jit(solution)/shard_map/all_to_all | solution.py:195
  83.5 0.0 copy-done.1
  83.5 0.1 shard_map.91
  83.6 13.6 %all_to_all.21 = f32[32,8,128]{2,1,0:T(8,128)S(1)} all-to-all(f32[32,8,128]{2,1,0:T(8,128)S(1)} %broadcast_in_dim.10), channel_id=1, replica_groups=mesh['x'=4,'yl'=2,'c'=2,'yh'=2,'z'=8] {'x','yl','c','yh'}, dimensions={0} | all-to-all | bytes 262144 | tf_op jit(solution)/shard_map/all_to_all | solution.py:163
  97.3 0.0 copy-start.2
  97.3 12.6 %all_to_all.22.sums_ref = f32[8,8,128]{2,1,0:T(8,128)S(1)} all-to-all(f32[8,8,128]{2,1,0:T(8,128)S(1)} %broadcast_in_dim.11), channel_id=1, replica_groups=mesh['x'=4,'yl'=2,'c'=2,'yh'=2,'z'=8] {'z'}, dimensions={0} | all-to-all | bytes 65536 | tf_op jit(solution)/shard_map/all_to_all | solution.py:163
  109.9 0.0 copy-done.2
  109.9 0.8 shard_map.92
  (8 shorter events, 0.1 us)
Async XLA Ops:
  0.6 0.9 copy-start.3
  1.5 0.9 copy-start
  2.5 5.7 %collective-permute-start = (bf16[1,320,128]{2,1,0:T(8,128)(2,1)S(1)}, bf16[1,320,128]{2,1,0:T(8,128)(2,1)S(1)}, u32[]{:S(2)}, u32[]{:S(2)}) collective-permute-start(bf16[1,320,128]{2,1,0:T(8,128)(2,1)S(1)} %maximum_bitcast_fusion), channel_id=1, source_target_pairs={{0,8},{8,0},{1,9},{9,1},{2,10},{10,2},{3,11},{11,3},{4,12},{12,4},... | collective-permute-start | bytes 245768 | tf_op jit(solution)/shard_map/ppermute | solution.py:158
  8.2 23.5 %collective-permute-start.15 = (bf16[2,320,128]{2,1,0:T(8,128)(2,1)S(1)}, bf16[2,320,128]{2,1,0:T(8,128)(2,1)S(1)}, u32[]{:S(2)}, u32[]{:S(2)}) collective-permute-start(bf16[2,320,128]{2,1,0:T(8,128)(2,1)S(1)} %pad_maximum_fusion.refs_1_), channel_id=1, source_target_pairs={{0,16},{16,0},{1,17},{17,1},{2,18},{18,2},{3,19},{19,3},{4,20},{20... | collective-permute-start | bytes 491528 | tf_op jit(solution)/shard_map/ppermute | solution.py:158
  11.9 14.9 %collective-permute-start.1 = (bf16[2,320,128]{2,1,0:T(8,128)(2,1)S(1)}, bf16[2,320,128]{2,1,0:T(8,128)(2,1)S(1)}, u32[]{:S(2)}, u32[]{:S(2)}) collective-permute-start(bf16[2,320,128]{2,1,0:T(8,128)(2,1)S(1)} %pad_maximum_fusion.refs_1_), channel_id=1, source_target_pairs={{0,1},{1,2},{2,3},{3,4},{4,5},{5,6},{6,7},{7,0},{8,9},{9,10},{10,1... | collective-permute-start | bytes 491528 | tf_op jit(solution)/shard_map/ppermute | solution.py:158
  11.9 16.7 %collective-permute-start.7 = (bf16[2,320,128]{2,1,0:T(8,128)(2,1)S(1)}, bf16[2,320,128]{2,1,0:T(8,128)(2,1)S(1)}, u32[]{:S(2)}, u32[]{:S(2)}) collective-permute-start(bf16[2,320,128]{2,1,0:T(8,128)(2,1)S(1)} %pad_maximum_fusion.refs_1_), channel_id=1, source_target_pairs={{0,7},{1,0},{2,1},{3,2},{4,3},{5,4},{6,5},{7,6},{8,15},{9,8},{10,9... | collective-permute-start | bytes 491528 | tf_op jit(solution)/shard_map/ppermute | solution.py:158
  26.8 9.8 %collective-permute-start.13 = (bf16[2,320,128]{2,1,0:T(8,128)(2,1)S(1)}, bf16[2,320,128]{2,1,0:T(8,128)(2,1)S(1)}, u32[]{:S(2)}, u32[]{:S(2)}) collective-permute-start(bf16[2,320,128]{2,1,0:T(8,128)(2,1)S(1)} %collective-permute-done.1.refs_1_), channel_id=1, source_target_pairs={{0,16},{16,0},{1,17},{17,1},{2,18},{18,2},{3,19},{19,3},{4,20},{20... | collective-permute-start | bytes 491528 | tf_op jit(solution)/shard_map/ppermute | solution.py:158
  28.6 7.2 %collective-permute-start.2 = (bf16[2,320,128]{2,1,0:T(8,128)(2,1)S(1)}, bf16[2,320,128]{2,1,0:T(8,128)(2,1)S(1)}, u32[]{:S(2)}, u32[]{:S(2)}) collective-permute-start(bf16[2,320,128]{2,1,0:T(8,128)(2,1)S(1)} %collective-permute-done.1.refs_1_), channel_id=1, source_target_pairs={{0,1},{1,2},{2,3},{3,4},{4,5},{5,6},{6,7},{7,0},{8,9},{9,10},{10,1... | collective-permute-start | bytes 491528 | tf_op jit(solution)/shard_map/ppermute | solution.py:158
  28.6 10.9 %collective-permute-start.14 = (bf16[2,320,128]{2,1,0:T(8,128)(2,1)S(1)}, bf16[2,320,128]{2,1,0:T(8,128)(2,1)S(1)}, u32[]{:S(2)}, u32[]{:S(2)}) collective-permute-start(bf16[2,320,128]{2,1,0:T(8,128)(2,1)S(1)} %collective-permute-done.7.refs_3_), channel_id=1, source_target_pairs={{0,16},{16,0},{1,17},{17,1},{2,18},{18,2},{3,19},{19,3},{4,20},{20... | collective-permute-start | bytes 491528 | tf_op jit(solution)/shard_map/ppermute | solution.py:158
  28.8 7.6 %collective-permute-start.8 = (bf16[2,320,128]{2,1,0:T(8,128)(2,1)S(1)}, bf16[2,320,128]{2,1,0:T(8,128)(2,1)S(1)}, u32[]{:S(2)}, u32[]{:S(2)}) collective-permute-start(bf16[2,320,128]{2,1,0:T(8,128)(2,1)S(1)} %collective-permute-done.7.refs_3_), channel_id=1, source_target_pairs={{0,7},{1,0},{2,1},{3,2},{4,3},{5,4},{6,5},{7,6},{8,15},{9,8},{10,9... | collective-permute-start | bytes 491528 | tf_op jit(solution)/shard_map/ppermute | solution.py:158
  35.8 12.7 %collective-permute-start.11 = (bf16[2,320,128]{2,1,0:T(8,128)(2,1)S(1)}, bf16[2,320,128]{2,1,0:T(8,128)(2,1)S(1)}, u32[]{:S(2)}, u32[]{:S(2)}) collective-permute-start(bf16[2,320,128]{2,1,0:T(8,128)(2,1)S(1)} %collective-permute-done.2.refs_1_), channel_id=1, source_target_pairs={{0,16},{16,0},{1,17},{17,1},{2,18},{18,2},{3,19},{19,3},{4,20},{20... | collective-permute-start | bytes 491528 | tf_op jit(solution)/shard_map/ppermute | solution.py:158
  36.4 11.3 %collective-permute-start.3 = (bf16[2,320,128]{2,1,0:T(8,128)(2,1)S(1)}, bf16[2,320,128]{2,1,0:T(8,128)(2,1)S(1)}, u32[]{:S(2)}, u32[]{:S(2)}) collective-permute-start(bf16[2,320,128]{2,1,0:T(8,128)(2,1)S(1)} %collective-permute-done.2.refs_1_), channel_id=1, source_target_pairs={{0,1},{1,2},{2,3},{3,4},{4,5},{5,6},{6,7},{7,0},{8,9},{9,10},{10,1... | collective-permute-start | bytes 491528 | tf_op jit(solution)/shard_map/ppermute | solution.py:158
  36.5 12.1 %collective-permute-start.12 = (bf16[2,320,128]{2,1,0:T(8,128)(2,1)S(1)}, bf16[2,320,128]{2,1,0:T(8,128)(2,1)S(1)}, u32[]{:S(2)}, u32[]{:S(2)}) collective-permute-start(bf16[2,320,128]{2,1,0:T(8,128)(2,1)S(1)} %collective-permute-done.8.refs_3_), channel_id=1, source_target_pairs={{0,16},{16,0},{1,17},{17,1},{2,18},{18,2},{3,19},{19,3},{4,20},{20... | collective-permute-start | bytes 491528 | tf_op jit(solution)/shard_map/ppermute | solution.py:158
  36.6 11.8 %collective-permute-start.9 = (bf16[2,320,128]{2,1,0:T(8,128)(2,1)S(1)}, bf16[2,320,128]{2,1,0:T(8,128)(2,1)S(1)}, u32[]{:S(2)}, u32[]{:S(2)}) collective-permute-start(bf16[2,320,128]{2,1,0:T(8,128)(2,1)S(1)} %collective-permute-done.8.refs_3_), channel_id=1, source_target_pairs={{0,7},{1,0},{2,1},{3,2},{4,3},{5,4},{6,5},{7,6},{8,15},{9,8},{10,9... | collective-permute-start | bytes 491528 | tf_op jit(solution)/shard_map/ppermute | solution.py:158
  47.8 9.5 %collective-permute-start.6 = (bf16[2,320,128]{2,1,0:T(8,128)(2,1)S(1)}, bf16[2,320,128]{2,1,0:T(8,128)(2,1)S(1)}, u32[]{:S(2)}, u32[]{:S(2)}) collective-permute-start(bf16[2,320,128]{2,1,0:T(8,128)(2,1)S(1)} %collective-permute-done.3.refs_1_), channel_id=1, source_target_pairs={{0,16},{16,0},{1,17},{17,1},{2,18},{18,2},{3,19},{19,3},{4,20},{20... | collective-permute-start | bytes 491528 | tf_op jit(solution)/shard_map/ppermute | solution.py:158
  48.4 8.5 %collective-permute-start.4 = (bf16[2,320,128]{2,1,0:T(8,128)(2,1)S(1)}, bf16[2,320,128]{2,1,0:T(8,128)(2,1)S(1)}, u32[]{:S(2)}, u32[]{:S(2)}) collective-permute-start(bf16[2,320,128]{2,1,0:T(8,128)(2,1)S(1)} %collective-permute-done.3.refs_1_), channel_id=1, source_target_pairs={{0,1},{1,2},{2,3},{3,4},{4,5},{5,6},{6,7},{7,0},{8,9},{9,10},{10,1... | collective-permute-start | bytes 491528 | tf_op jit(solution)/shard_map/ppermute | solution.py:158
  48.4 8.9 %collective-permute-start.10 = (bf16[2,320,128]{2,1,0:T(8,128)(2,1)S(1)}, bf16[2,320,128]{2,1,0:T(8,128)(2,1)S(1)}, u32[]{:S(2)}, u32[]{:S(2)}) collective-permute-start(bf16[2,320,128]{2,1,0:T(8,128)(2,1)S(1)} %collective-permute-done.9.refs_3_), channel_id=1, source_target_pairs={{0,16},{16,0},{1,17},{17,1},{2,18},{18,2},{3,19},{19,3},{4,20},{20... | collective-permute-start | bytes 491528 | tf_op jit(solution)/shard_map/ppermute | solution.py:158
  56.8 8.7 %collective-permute-start.5 = (bf16[2,320,128]{2,1,0:T(8,128)(2,1)S(1)}, bf16[2,320,128]{2,1,0:T(8,128)(2,1)S(1)}, u32[]{:S(2)}, u32[]{:S(2)}) collective-permute-start(bf16[2,320,128]{2,1,0:T(8,128)(2,1)S(1)} %collective-permute-done.4.refs_1_), channel_id=1, source_target_pairs={{0,16},{16,0},{1,17},{17,1},{2,18},{18,2},{3,19},{19,3},{4,20},{20... | collective-permute-start | bytes 491528 | tf_op jit(solution)/shard_map/ppermute | solution.py:158
  70.5 13.0 %copy-start.1 = (f32[256,128]{1,0:T(8,128)S(1)}, f32[256,128]{1,0:T(8,128)}, u32[]{:S(2)}) copy-start(f32[256,128]{1,0:T(8,128)} %res_ref.3) | copy-start | bytes 393220
  70.5 13.0 %all-to-all-start.1 = ((bf16[8,256,128]{2,1,0:T(8,128)(2,1)}), bf16[8,256,128]{2,1,0:T(8,128)(2,1)S(1)}, u32[]{:S(2)}, u32[]{:S(2)}) async-start(bf16[8,256,128]{2,1,0:T(8,128)(2,1)} %bitcast.2), calls=%async_computation.1 | async-start | bytes 1048576 | tf_op jit(solution)/shard_map/all_to_all | solution.py:195
  97.3 12.6 %copy-start.2 = (f32[256,128]{1,0:T(8,128)S(1)}, f32[256,128]{1,0:T(8,128)}, u32[]{:S(2)}) copy-start(f32[256,128]{1,0:T(8,128)} %sol_ref.1) | copy-start | bytes 393220

commit v2 on v1

--- a/solution.py
+++ b/solution.py
@@ -9,9 +9,11 @@
 from jax.sharding import Mesh
 from jax.sharding import PartitionSpec as P
 
-AXES = ("x", "yl", "c", "yh", "z")
-ROWS = ("x", "yl")
-PLANE = ("x", "yl", "c", "yh")
+AXES = ("xh", "xl", "yl", "c", "yh", "zh", "zm", "zl")
+ROWS = ("xh", "yh", "zm")
+CUBE = ("xl", "yl", "zl")
+PLANE = ("xh", "xl", "yl", "c", "yh")
+DEPTH = ("zh", "zm", "zl")
 FEATURES = 32
 SCALE = 5.0 / 3.0
 ROOT3 = math.sqrt(3.0)
@@ -68,52 +70,58 @@
     return (((1.0 + m) + ROOT3 * t) * jnp.exp2((-ROOT3 * LOG2E) * t)).astype(jnp.bfloat16)
 
 
-def tiles_kernel(n_bundles, has_sum, last, row_tile, *refs):
+def tiles_kernel(n_bundles, has_sum, tile, unroll, *refs):
     rows_ref, bundles, refs = refs[0], refs[1 : 1 + n_bundles], refs[1 + n_bundles :]
     if has_sum:
         sum_ref, refs = refs[0], refs[1:]
-    out_ref, cols_ref, dirs_ref, acc_ref = refs
+    out_ref, cols_ref, dirs_ref, acc_ref, ahead_ref = refs
     pieces = bundles[0].shape[0]
     for b, bundle in enumerate(bundles):
         here = slice(b * pieces, (b + 1) * pieces)
         dirs_ref[here] = bundle[:, :256, :]
-        x4 = bundle[:, 256:, :].reshape(pieces * 64, 128)
-        for q in range(4):
-            cols_ref[here, q * 64 : (q + 1) * 64, :] = augmented(x4, q, False).reshape(pieces, 64, 128)
-    count = rows_ref.shape[0]
-
-    def turn(n, first):
-        for i in range(count // row_tile):
-            at = slice(i * row_tile, (i + 1) * row_tile)
-            u = lax.dot_general(
-                rows_ref[at, :], cols_ref[n], (((1,), (1,)), ((), ())), preferred_element_type=jnp.float32
+
+        def quarter(q, _):
+            x4 = bundle[:, 256:, :].reshape(pieces * 64, 128)
+            cols_ref[here, pl.ds(pl.multiple_of(q * 64, 64), 64), :] = augmented(x4, q, False).reshape(pieces, 64, 128)
+            return 0
+
+        lax.fori_loop(0, 4, quarter, 0)
+    per_piece = rows_ref.shape[0] // tile
+    total = n_bundles * pieces * per_piece
+    acc_ref[...] = sum_ref[...] if has_sum else jnp.zeros_like(acc_ref)
+
+    def at(k):
+        return pl.ds(pl.multiple_of((k % per_piece) * tile, tile), tile)
+
+    def distances(k, slot):
+        ahead_ref[slot] = lax.dot_general(
+            rows_ref[at(k), :], cols_ref[k // per_piece], (((1,), (1,)), ((), ())), preferred_element_type=jnp.float32
+        )
+
+    distances(0, 0)
+
+    def body(turn, _):
+        for s in range(unroll):
+            k = turn * unroll + s
+            distances(jnp.minimum(k + 1, total - 1), (s + 1) % 2)
+            acc_ref[at(k), :] += jnp.dot(
+                matern(ahead_ref[s % 2]), dirs_ref[k // per_piece], preferred_element_type=jnp.float32
             )
-            part = jnp.dot(matern(u), dirs_ref[n], preferred_element_type=jnp.float32)
-            if first is None:
-                acc_ref[at, :] = acc_ref[at, :] + part
-            elif first:
-                acc_ref[at, :] = part
-            else:
-                acc_ref[at, :] = sum_ref[at, :] + part
-
-    turn(0, not has_sum)
-
-    def body(n, _):
-        turn(n, None)
         return 0
 
-    lax.fori_loop(1, n_bundles * pieces, body, 0)
+    lax.fori_loop(0, total // unroll, body, 0)
     out_ref[...] = acc_ref[...].astype(out_ref.dtype)
 
 
-def tiles(rows, bundles, so_far, last):
+def tiles(rows, bundles, so_far, last=False):
     pieces = bundles[0].shape[0]
     n = len(bundles) * pieces
     count = rows.shape[0]
+    tile = 1024
     args = (rows, *bundles) + (() if so_far is None else (so_far,))
     whole = pl.BlockSpec(memory_space=pltpu.VMEM)
     return pl.pallas_call(
-        functools.partial(tiles_kernel, len(bundles), so_far is not None, last, min(count, 1024)),
+        functools.partial(tiles_kernel, len(bundles), so_far is not None, tile, 2),
         out_shape=jax.ShapeDtypeStruct((count, 128), jnp.bfloat16 if last else jnp.float32),
         in_specs=[whole] * len(args),
         out_specs=whole,
@@ -121,10 +129,11 @@
             pltpu.VMEM((n, 256, 128), jnp.bfloat16),
             pltpu.VMEM((n, 256, 128), jnp.bfloat16),
             pltpu.VMEM((count, 128), jnp.float32),
+            pltpu.VMEM((2, tile, 256), jnp.float32),
         ],
         compiler_params=VMEM,
         cost_estimate=pl.CostEstimate(
-            flops=2 * count * n * 256 * 256 * 2, bytes_accessed=2 * count * 128 * 4, transcendentals=count * n * 512
+            flops=count * n * 256 * 256, bytes_accessed=0, transcendentals=0
         ),
     )(*args)
 
@@ -138,7 +147,6 @@
     sums_ref[1:2, :] = col(dir_ref[...] * image)
     sums_ref[2:3, :] = col(res * image)
     sums_ref[3:4, :] = col(image * image)
-    sums_ref[4:8, :] = jnp.zeros((4, 128), jnp.float32)
 
 
 def step_kernel(sums_ref, image_ref, sol_ref, res_ref, dir_ref, new_sol, new_res, new_dir):
@@ -158,6 +166,11 @@
     return lax.ppermute(x, axis, [(i, (i + by) % count) for i in range(count)])
 
 
+def mirrored(x, axes):
+    count = lax.axis_size(axes)
+    return lax.ppermute(x, axes, [(i, count - 1 - i) for i in range(count)])
+
+
 def from_all(x, axes):
     count = lax.axis_size(axes)
     return lax.all_to_all(jnp.broadcast_to(x[None], (count,) + x.shape), axes, 0, 0, tiled=True)
@@ -167,7 +180,7 @@
     scaled = (points.astype(jnp.float32) * inv_length).astype(jnp.bfloat16)
     x4 = jnp.concatenate([scaled[q * 64 : (q + 1) * 64] for q in range(4)], axis=1)
     packed = jnp.concatenate([direction.astype(jnp.bfloat16), x4], axis=0)[None]
-    pair = jnp.concatenate([packed, turned(packed, "yh", 1)], axis=0)
+    pair = jnp.concatenate([packed, mirrored(packed, DEPTH)], axis=0)
     whole = pl.BlockSpec(memory_space=pltpu.VMEM)
 
     n_rows = lax.axis_size(ROWS)
@@ -179,30 +192,36 @@
         compiler_params=VMEM,
     )(from_all(x4, ROWS)).reshape(n_rows * 256, 128)
 
-    length = lax.axis_size("z")
-    up = down = pair
-    so_far = None
-    here = [pair]
-    for hop in range(length // 2 + 1):
-        bundles = [b for h in here for b in (h, turned(h, "c", 1))]
-        if hop < length // 2 - 1:
-            up, down = turned(up, "z", 1), turned(down, "z", -1)
-            here = [up, down]
-        else:
-            up = turned(up, "z", 1)
-            here = [up]
-        so_far = tiles(rows, bundles, so_far, hop == length // 2)
+    def after(x, done):
+        return lax.optimization_barrier((x, done))[0]
+
+    own = after(pair, rows)
+    near = [turned(own, a, 1) for a in CUBE]
+    so_far = tiles(rows, [own, turned(own, "c", 1)], None)
+    near = after(near, so_far)
+    other = [turned(b, "c", 1) for b in near]
+    far = [turned(near[(i + 1) % 3], a, 1) for i, a in enumerate(CUBE)]
+    so_far = tiles(rows, near, so_far)
+    so_far = tiles(rows, other, so_far)
+    far = after(far, so_far)
+    opposite = turned(far[0], CUBE[2], 1)
+    other = [turned(b, "c", 1) for b in far]
+    so_far = tiles(rows, far, so_far)
+    opposite = after(opposite, so_far)
+    opposite = [opposite, turned(opposite, "c", 1)]
+    so_far = tiles(rows, other, so_far)
+    so_far = tiles(rows, opposite, so_far, True)
     parts = lax.all_to_all(so_far.reshape(n_rows, 256, 128), ROWS, 0, 0, tiled=True)
     f32 = jax.ShapeDtypeStruct(direction.shape, jnp.float32)
     image, sums = pl.pallas_call(
         image_kernel,
-        out_shape=(f32, jax.ShapeDtypeStruct((8, 128), jnp.float32)),
+        out_shape=(f32, jax.ShapeDtypeStruct((4, 128), jnp.float32)),
         in_specs=[whole, pl.BlockSpec(memory_space=pltpu.SMEM), whole, whole],
         out_specs=(whole, whole),
         compiler_params=VMEM,
     )(parts, noise_var.reshape(1, 1), direction, residual)
     sums = jnp.sum(from_all(sums, PLANE), axis=0)
-    sums = from_all(sums, ("z",))
+    sums = from_all(sums, DEPTH)
     return pl.pallas_call(
         step_kernel,
         out_shape=(f32, f32, f32),
@@ -213,7 +232,7 @@
 
 
 def solution(mesh):
-    finer = Mesh(mesh.devices.reshape(4, 2, 2, 2, 8), AXES)
+    finer = Mesh(mesh.devices.reshape((2,) * 8), AXES)
     placed = P(AXES, None)
     return jax.shard_map(
         on_device,

time: 111 us -> 126 us (1.14)
  blocking collectives: 36.5 us -> 24.2 us
  waiting for transfers between devices: 10.6 us -> 21.7 us
  Pallas kernels: 35.5 us -> 44.1 us
  starting transfers between devices: 24.7 us -> 32.6 us
    all_to_all x3 -> x2, blocking collectives: 36.5 us -> 24.2 us  [from_all(): lax.all_to_all(jnp.broadcast_to(x[None], (count,) + x.shape), axes, 0, 0,...]
    all_to_all x0 -> x1, starting transfers between devices: none -> 10.3 us  [from_all(): lax.all_to_all(jnp.broadcast_to(x[None], (count,) + x.shape), axes, 0, 0,...]
    ppermute x16 -> x15, starting transfers between devices: 21.1 us -> 11.7 us  [turned(): return lax.ppermute(x, axis, [(i, (i + by) % count) for i in range(count)])]
    all_to_all x1, waiting for transfers between devices: 8.7 us -> 17.8 us  [on_device(): lax.all_to_all(so_far.reshape(n_rows, 256, 128), ROWS, 0, 0, tiled=True)]
    pallas_call x5 -> x6, Pallas kernels: 33.9 us -> 42.5 us  [tiles(): pl.pallas_call(functools.partial(tiles_kernel, len(bundles), so_far is no...]
    ppermute x0 -> x1, starting transfers between devices: none -> 5.02 us  [mirrored(): return lax.ppermute(x, axes, [(i, count - 1 - i) for i in range(count)])]
    ppermute x0 -> x1, waiting for transfers between devices: none -> 3.04 us  [mirrored(): return lax.ppermute(x, axes, [(i, count - 1 - i) for i in range(count)])]
    all_to_all x1, starting transfers between devices: 3.62 us -> 5.58 us  [on_device(): lax.all_to_all(so_far.reshape(n_rows, 256, 128), ROWS, 0, 0, tiled=True)]
  transfers between devices with their start and end apart: 17 -> 18, of which waited for: 2 -> 3; matrix products, arithmetic and copies ran while one was open for 0% -> 0% of each run, Pallas kernels for 27% -> 29%
where the time goes in v2:
time: 126 us
  Pallas kernels  44.1 us (35%)
  starting transfers between devices  32.6 us (26%)
  blocking collectives  24.2 us (19%)
  waiting for transfers between devices  21.7 us (17%)
  local copies, waits for them, and re-layouts  1.56 us (1%)
  between operations  1.52 us (1%)
    pallas_call x6, Pallas kernels, tiles(): pl.pallas_call(functools.partial(tiles_kernel, len(bundles), so_far is no...  42.5 us
    all_to_all x2, blocking collectives, from_all(): lax.all_to_all(jnp.broadcast_to(x[None], (count,) + x.shape), axes, 0, 0,...  24.2 us
    all_to_all x1, waiting for transfers between devices, on_device(): lax.all_to_all(so_far.reshape(n_rows, 256, 128), ROWS, 0, 0, tiled=True)  17.8 us
    ppermute x15, starting transfers between devices, turned(): return lax.ppermute(x, axis, [(i, (i + by) % count) for i in range(count)])  11.7 us
    all_to_all x1, starting transfers between devices, from_all(): lax.all_to_all(jnp.broadcast_to(x[None], (count,) + x.shape), axes, 0, 0,...  10.3 us
    all_to_all x1, starting transfers between devices, on_device(): lax.all_to_all(so_far.reshape(n_rows, 256, 128), ROWS, 0, 0, tiled=True)  5.58 us
    ppermute x1, starting transfers between devices, mirrored(): return lax.ppermute(x, axes, [(i, count - 1 - i) for i in range(count)])  5.02 us
    ppermute x1, waiting for transfers between devices, mirrored(): return lax.ppermute(x, axes, [(i, count - 1 - i) for i in range(count)])  3.04 us
  transfers between devices with their start and end apart: 18, of which 3 were waited for; matrix products, arithmetic and copies ran while one was open for 0% of the time, Pallas kernels for 29%

profile of v2, /device:TPU:1, one launch (start us, length us, event | category | flops | bytes accessed | tf_op | source)
XLA Modules:
  0.0 125.9 jit_solution(6596463381019818228)
XLA Ops:
  0.6 0.0 copy-start.3
  0.6 0.8 copy.11
  1.5 0.0 copy-done.3
  1.5 0.1 pad_maximum_fusion.1
  1.6 0.7 broadcast_in_dim.8
  2.3 0.0 copy-start
  2.3 10.3 %all-to-all-start = ((bf16[8,64,128]{2,1,0:T(8,128)(2,1)}), bf16[8,64,128]{2,1,0:T(8,128)(2,1)S(1)}, u32[]{:S(2)}, u32[]{:S(2)}) async-start(bf16[8,64,128]{2,1,0:T(8,128)(2,1)} %broadcast_in_dim.8), calls=%async_computation | async-start | bytes 262144 | tf_op jit(solution)/shard_map/all_to_all | solution.py:176
  12.6 0.0 copy-done
  12.6 0.1 maximum_bitcast_fusion
  12.7 5.0 %collective-permute-start = (bf16[1,320,128]{2,1,0:T(8,128)(2,1)S(1)}, bf16[1,320,128]{2,1,0:T(8,128)(2,1)S(1)}, u32[]{:S(2)}, u32[]{:S(2)}) collective-permute-start(bf16[1,320,128]{2,1,0:T(8,128)(2,1)S(1)} %maximum_bitcast_fusion), channel_id=1, source_target_pairs={{0,7},{1,6},{2,5},{3,4},{4,3},{5,2},{6,1},{7,0},{8,15},{9,14},{10,... | collective-permute-start | bytes 245768 | tf_op jit(solution)/shard_map/ppermute | solution.py:171
  17.8 3.0 %collective-permute-done = bf16[1,320,128]{2,1,0:T(8,128)(2,1)S(1)} collective-permute-done((bf16[1,320,128]{2,1,0:T(8,128)(2,1)S(1)}, bf16[1,320,128]{2,1,0:T(8,128)(2,1)S(1)}, u32[]{:S(2)}, u32[]{:S(2)}) %collective-permute-start) | collective-permute-done | bytes 81952 | tf_op jit(solution)/shard_map/ppermute | solution.py:171
  20.8 0.8 all-to-all-done.x_ref
  21.6 0.7 shard_map.85
  22.3 2.8 %collective-permute-start.4 = (bf16[2,320,128]{2,1,0:T(8,128)(2,1)S(1)}, bf16[2,320,128]{2,1,0:T(8,128)(2,1)S(1)}, u32[]{:S(2)}, u32[]{:S(2)}) collective-permute-start(bf16[2,320,128]{2,1,0:T(8,128)(2,1)S(1)} %pad_maximum_fusion.refs_1_), channel_id=1, source_target_pairs={{0,16},{16,0},{1,17},{17,1},{2,18},{18,2},{3,19},{19,3},{4,20},{20... | collective-permute-start | bytes 491528 | tf_op jit(solution)/shard_map/ppermute | solution.py:166
  25.2 0.3 collective-permute-start.1
  25.5 0.4 collective-permute-start.2
  25.9 1.0 collective-permute-start.3
  26.9 0.0 collective-permute-done.4.refs_2_
  26.9 5.3 %shard_map.86.refs_4_ = f32[2048,128]{1,0:T(8,128)S(1)} custom-call(bf16[2048,128]{1,0:T(8,128)(2,1)S(1)} %bitcast.6, bf16[2,320,128]{2,1,0:T(8,128)(2,1)S(1)} %pad_maximum_fusion.refs_1_, bf16[2,320,128]{2,1,0:T(8,128)(2,1)S(1)} %collective-permute-done.4.refs_2_), custom_call_target="tpu_custom_call" | custom-call | flops 536870912 | tf_op jit(solution)/shard_map/pallas_call | solution.py:123
  32.2 0.0 collective-permute-done.1.refs_1_
  32.2 0.0 collective-permute-done.2.refs_2_
  32.2 0.0 collective-permute-done.3.refs_3_
  32.2 1.0 collective-permute-start.10
  33.2 0.1 collective-permute-start.8
  33.3 0.4 collective-permute-start.9
  33.8 1.2 collective-permute-start.5
  34.9 1.1 collective-permute-start.6
  36.0 0.0 collective-permute-done.10.refs_3_
  36.0 0.5 collective-permute-start.7
  36.5 7.8 %shard_map.87.refs_4_ = f32[2048,128]{1,0:T(8,128)S(1)} custom-call(bf16[2048,128]{1,0:T(8,128)(2,1)S(1)} %bitcast.7, bf16[2,320,128]{2,1,0:T(8,128)(2,1)S(1)} %collective-permute-done.1.refs_1_, bf16[2,320,128]{2,1,0:T(8,128)(2,1)S(1)} %collective-permute-done.2.refs_2_, bf16[2,320,128]{2,1,0:T(8,128)(2,1)S(1)} %collective-permute-done.3.refs_3_, ...), custom_call_target="tpu_custom_call" | custom-call | flops 805306368 | tf_op jit(solution)/shard_map/pallas_call | solution.py:123
  44.3 0.0 collective-permute-done.8.refs_1_
  44.3 0.0 collective-permute-done.9.refs_2_
  44.3 7.8 %shard_map.88.refs_4_ = f32[2048,128]{1,0:T(8,128)S(1)} custom-call(bf16[2048,128]{1,0:T(8,128)(2,1)S(1)} %bitcast.8, bf16[2,320,128]{2,1,0:T(8,128)(2,1)S(1)} %collective-permute-done.8.refs_1_, bf16[2,320,128]{2,1,0:T(8,128)(2,1)S(1)} %collective-permute-done.9.refs_2_, bf16[2,320,128]{2,1,0:T(8,128)(2,1)S(1)} %collective-permute-done.10.refs_3_, ...), custom_call_target="tpu_custom_call" | custom-call | flops 805306368 | tf_op jit(solution)/shard_map/pallas_call | solution.py:123
  52.1 0.0 collective-permute-done.5.refs_1_
  52.1 0.0 collective-permute-done.6.refs_2_
  52.1 0.0 collective-permute-done.7.refs_3_
  52.1 1.1 collective-permute-start.11
  53.2 1.2 collective-permute-start.13
  54.4 0.0 collective-permute-start.14
  54.4 0.5 collective-permute-start.15
  54.9 7.8 %shard_map.89.refs_4_ = f32[2048,128]{1,0:T(8,128)S(1)} custom-call(bf16[2048,128]{1,0:T(8,128)(2,1)S(1)} %bitcast.9, bf16[2,320,128]{2,1,0:T(8,128)(2,1)S(1)} %collective-permute-done.5.refs_1_, bf16[2,320,128]{2,1,0:T(8,128)(2,1)S(1)} %collective-permute-done.6.refs_2_, bf16[2,320,128]{2,1,0:T(8,128)(2,1)S(1)} %collective-permute-done.7.refs_3_, ...), custom_call_target="tpu_custom_call" | custom-call | flops 805306368 | tf_op jit(solution)/shard_map/pallas_call | solution.py:123
  62.7 0.0 collective-permute-done.11.refs_1_
  62.7 0.1 collective-permute-start.12
  62.8 0.0 collective-permute-done.13.refs_1_
  62.8 0.0 collective-permute-done.14.refs_2_
  62.8 0.0 collective-permute-done.15.refs_3_
  62.8 7.8 %shard_map.90.refs_3_ = f32[2048,128]{1,0:T(8,128)S(1)} custom-call(bf16[2048,128]{1,0:T(8,128)(2,1)S(1)} %bitcast.10, bf16[2,320,128]{2,1,0:T(8,128)(2,1)S(1)} %collective-permute-done.13.refs_1_, bf16[2,320,128]{2,1,0:T(8,128)(2,1)S(1)} %collective-permute-done.14.refs_2_, bf16[2,320,128]{2,1,0:T(8,128)(2,1)S(1)} %collective-permute-done.15.refs_3_, ...), custom_call_target="tpu_custom_call" | custom-call | flops 805306368 | tf_op jit(solution)/shard_map/pallas_call | solution.py:123
  70.6 0.0 collective-permute-done.12.refs_2_
  70.6 6.1 %shard_map.91 = bf16[2048,128]{1,0:T(8,128)(2,1)} custom-call(bf16[2048,128]{1,0:T(8,128)(2,1)S(1)} %bitcast.11, bf16[2,320,128]{2,1,0:T(8,128)(2,1)S(1)} %collective-permute-done.11.refs_1_, bf16[2,320,128]{2,1,0:T(8,128)(2,1)S(1)} %collective-permute-done.12.refs_2_, f32[2048,128]{1,0:T(8,128)S(1)} %shard_map.90.refs_3_), custom_call_target="tpu_custom_call" | custom-call | flops 536870912 | tf_op jit(solution)/shard_map/pallas_call | solution.py:123
  76.8 0.0 copy-start.1
  76.8 5.6 %all-to-all-start.1 = ((bf16[8,256,128]{2,1,0:T(8,128)(2,1)}), bf16[8,256,128]{2,1,0:T(8,128)(2,1)S(1)}, u32[]{:S(2)}, u32[]{:S(2)}) async-start(bf16[8,256,128]{2,1,0:T(8,128)(2,1)} %bitcast.2), calls=%async_computation.1 | async-start | bytes 1048576 | tf_op jit(solution)/shard_map/all_to_all | solution.py:214
  83.0 17.8 %all-to-all-done.1.parts_ref = bf16[8,256,128]{2,1,0:T(8,128)(2,1)S(1)} async-done(((bf16[8,256,128]{2,1,0:T(8,128)(2,1)}), bf16[8,256,128]{2,1,0:T(8,128)(2,1)S(1)}, u32[]{:S(2)}, u32[]{:S(2)}) %all-to-all-start.1) | async-done | bytes 524320 | tf_op jit(solution)/shard_map/all_to_all | solution.py:214
  100.8 0.0 copy-done.1
  100.8 0.1 shard_map.92
  100.9 0.0 copy-start.2
  100.9 11.9 %all_to_all.20 = f32[32,4,128]{2,1,0:T(4,128)S(1)} all-to-all(f32[32,4,128]{2,1,0:T(4,128)S(1)} %broadcast_in_dim.10), channel_id=1, replica_groups=mesh['xh'=2,'xl'=2,'yl'=2,'c'=2,'yh'=2,'zh'=2,'zm'=2,'zl'=2] {'xh','xl',..., dimensions={0} | all-to-all | bytes 131072 | tf_op jit(solution)/shard_map/all_to_all | solution.py:176
  112.9 12.3 %all_to_all.21.sums_ref = f32[8,4,128]{2,1,0:T(4,128)S(1)} all-to-all(f32[8,4,128]{2,1,0:T(4,128)S(1)} %broadcast_in_dim.11), channel_id=1, replica_groups=mesh['xh'=2,'xl'=2,'yl'=2,'c'=2,'yh'=2,'zh'=2,'zm'=2,'zl'=2] {'zh','zm',..., dimensions={0} | all-to-all | bytes 32768 | tf_op jit(solution)/shard_map/all_to_all | solution.py:176
  125.1 0.0 copy-done.2
  125.1 0.8 shard_map.93
  (7 shorter events, 0.1 us)
Async XLA Ops:
  0.6 0.9 copy-start.3
  2.3 10.3 %copy-start = (f32[256,128]{1,0:T(8,128)S(1)}, f32[256,128]{1,0:T(8,128)}, u32[]{:S(2)}) copy-start(f32[256,128]{1,0:T(8,128)} %dir_ref.3) | copy-start | bytes 393220
  2.3 19.3 %all-to-all-start = ((bf16[8,64,128]{2,1,0:T(8,128)(2,1)}), bf16[8,64,128]{2,1,0:T(8,128)(2,1)S(1)}, u32[]{:S(2)}, u32[]{:S(2)}) async-start(bf16[8,64,128]{2,1,0:T(8,128)(2,1)} %broadcast_in_dim.8), calls=%async_computation | async-start | bytes 262144 | tf_op jit(solution)/shard_map/all_to_all | solution.py:176
  12.7 8.1 %collective-permute-start = (bf16[1,320,128]{2,1,0:T(8,128)(2,1)S(1)}, bf16[1,320,128]{2,1,0:T(8,128)(2,1)S(1)}, u32[]{:S(2)}, u32[]{:S(2)}) collective-permute-start(bf16[1,320,128]{2,1,0:T(8,128)(2,1)S(1)} %maximum_bitcast_fusion), channel_id=1, source_target_pairs={{0,7},{1,6},{2,5},{3,4},{4,3},{5,2},{6,1},{7,0},{8,15},{9,14},{10,... | collective-permute-start | bytes 245768 | tf_op jit(solution)/shard_map/ppermute | solution.py:171
  22.3 4.6 %collective-permute-start.4 = (bf16[2,320,128]{2,1,0:T(8,128)(2,1)S(1)}, bf16[2,320,128]{2,1,0:T(8,128)(2,1)S(1)}, u32[]{:S(2)}, u32[]{:S(2)}) collective-permute-start(bf16[2,320,128]{2,1,0:T(8,128)(2,1)S(1)} %pad_maximum_fusion.refs_1_), channel_id=1, source_target_pairs={{0,16},{16,0},{1,17},{17,1},{2,18},{18,2},{3,19},{19,3},{4,20},{20... | collective-permute-start | bytes 491528 | tf_op jit(solution)/shard_map/ppermute | solution.py:166
  25.2 7.0 %collective-permute-start.1 = (bf16[2,320,128]{2,1,0:T(8,128)(2,1)S(1)}, bf16[2,320,128]{2,1,0:T(8,128)(2,1)S(1)}, u32[]{:S(2)}, u32[]{:S(2)}) collective-permute-start(bf16[2,320,128]{2,1,0:T(8,128)(2,1)S(1)} %pad_maximum_fusion.refs_1_), channel_id=1, source_target_pairs={{0,64},{64,0},{1,65},{65,1},{2,66},{66,2},{3,67},{67,3},{4,68},{68... | collective-permute-start | bytes 491528 | tf_op jit(solution)/shard_map/ppermute | solution.py:166
  25.5 6.7 %collective-permute-start.2 = (bf16[2,320,128]{2,1,0:T(8,128)(2,1)S(1)}, bf16[2,320,128]{2,1,0:T(8,128)(2,1)S(1)}, u32[]{:S(2)}, u32[]{:S(2)}) collective-permute-start(bf16[2,320,128]{2,1,0:T(8,128)(2,1)S(1)} %pad_maximum_fusion.refs_1_), channel_id=1, source_target_pairs={{0,32},{32,0},{1,33},{33,1},{2,34},{34,2},{3,35},{35,3},{4,36},{36... | collective-permute-start | bytes 491528 | tf_op jit(solution)/shard_map/ppermute | solution.py:166
  25.9 6.3 %collective-permute-start.3 = (bf16[2,320,128]{2,1,0:T(8,128)(2,1)S(1)}, bf16[2,320,128]{2,1,0:T(8,128)(2,1)S(1)}, u32[]{:S(2)}, u32[]{:S(2)}) collective-permute-start(bf16[2,320,128]{2,1,0:T(8,128)(2,1)S(1)} %pad_maximum_fusion.refs_1_), channel_id=1, source_target_pairs={{0,1},{1,0},{2,3},{3,2},{4,5},{5,4},{6,7},{7,6},{8,9},{9,8},{10,11... | collective-permute-start | bytes 491528 | tf_op jit(solution)/shard_map/ppermute | solution.py:166
  32.2 3.8 %collective-permute-start.10 = (bf16[2,320,128]{2,1,0:T(8,128)(2,1)S(1)}, bf16[2,320,128]{2,1,0:T(8,128)(2,1)S(1)}, u32[]{:S(2)}, u32[]{:S(2)}) collective-permute-start(bf16[2,320,128]{2,1,0:T(8,128)(2,1)S(1)} %collective-permute-done.3.refs_3_), channel_id=1, source_target_pairs={{0,16},{16,0},{1,17},{17,1},{2,18},{18,2},{3,19},{19,3},{4,20},{20... | collective-permute-start | bytes 491528 | tf_op jit(solution)/shard_map/ppermute | solution.py:166
  33.2 11.0 %collective-permute-start.8 = (bf16[2,320,128]{2,1,0:T(8,128)(2,1)S(1)}, bf16[2,320,128]{2,1,0:T(8,128)(2,1)S(1)}, u32[]{:S(2)}, u32[]{:S(2)}) collective-permute-start(bf16[2,320,128]{2,1,0:T(8,128)(2,1)S(1)} %collective-permute-done.1.refs_1_), channel_id=1, source_target_pairs={{0,16},{16,0},{1,17},{17,1},{2,18},{18,2},{3,19},{19,3},{4,20},{20... | collective-permute-start | bytes 491528 | tf_op jit(solution)/shard_map/ppermute | solution.py:166
  33.3 10.9 %collective-permute-start.9 = (bf16[2,320,128]{2,1,0:T(8,128)(2,1)S(1)}, bf16[2,320,128]{2,1,0:T(8,128)(2,1)S(1)}, u32[]{:S(2)}, u32[]{:S(2)}) collective-permute-start(bf16[2,320,128]{2,1,0:T(8,128)(2,1)S(1)} %collective-permute-done.2.refs_2_), channel_id=1, source_target_pairs={{0,16},{16,0},{1,17},{17,1},{2,18},{18,2},{3,19},{19,3},{4,20},{20... | collective-permute-start | bytes 491528 | tf_op jit(solution)/shard_map/ppermute | solution.py:166
  33.8 18.3 %collective-permute-start.5 = (bf16[2,320,128]{2,1,0:T(8,128)(2,1)S(1)}, bf16[2,320,128]{2,1,0:T(8,128)(2,1)S(1)}, u32[]{:S(2)}, u32[]{:S(2)}) collective-permute-start(bf16[2,320,128]{2,1,0:T(8,128)(2,1)S(1)} %collective-permute-done.2.refs_2_), channel_id=1, source_target_pairs={{0,64},{64,0},{1,65},{65,1},{2,66},{66,2},{3,67},{67,3},{4,68},{68... | collective-permute-start | bytes 491528 | tf_op jit(solution)/shard_map/ppermute | solution.py:166
  34.9 17.2 %collective-permute-start.6 = (bf16[2,320,128]{2,1,0:T(8,128)(2,1)S(1)}, bf16[2,320,128]{2,1,0:T(8,128)(2,1)S(1)}, u32[]{:S(2)}, u32[]{:S(2)}) collective-permute-start(bf16[2,320,128]{2,1,0:T(8,128)(2,1)S(1)} %collective-permute-done.3.refs_3_), channel_id=1, source_target_pairs={{0,32},{32,0},{1,33},{33,1},{2,34},{34,2},{3,35},{35,3},{4,36},{36... | collective-permute-start | bytes 491528 | tf_op jit(solution)/shard_map/ppermute | solution.py:166
  36.0 16.1 %collective-permute-start.7 = (bf16[2,320,128]{2,1,0:T(8,128)(2,1)S(1)}, bf16[2,320,128]{2,1,0:T(8,128)(2,1)S(1)}, u32[]{:S(2)}, u32[]{:S(2)}) collective-permute-start(bf16[2,320,128]{2,1,0:T(8,128)(2,1)S(1)} %collective-permute-done.1.refs_1_), channel_id=1, source_target_pairs={{0,1},{1,0},{2,3},{3,2},{4,5},{5,4},{6,7},{7,6},{8,9},{9,8},{10,11... | collective-permute-start | bytes 491528 | tf_op jit(solution)/shard_map/ppermute | solution.py:166
  52.1 10.6 %collective-permute-start.11 = (bf16[2,320,128]{2,1,0:T(8,128)(2,1)S(1)}, bf16[2,320,128]{2,1,0:T(8,128)(2,1)S(1)}, u32[]{:S(2)}, u32[]{:S(2)}) collective-permute-start(bf16[2,320,128]{2,1,0:T(8,128)(2,1)S(1)} %collective-permute-done.5.refs_1_), channel_id=1, source_target_pairs={{0,1},{1,0},{2,3},{3,2},{4,5},{5,4},{6,7},{7,6},{8,9},{9,8},{10,11... | collective-permute-start | bytes 491528 | tf_op jit(solution)/shard_map/ppermute | solution.py:166
  53.2 9.6 %collective-permute-start.13 = (bf16[2,320,128]{2,1,0:T(8,128)(2,1)S(1)}, bf16[2,320,128]{2,1,0:T(8,128)(2,1)S(1)}, u32[]{:S(2)}, u32[]{:S(2)}) collective-permute-start(bf16[2,320,128]{2,1,0:T(8,128)(2,1)S(1)} %collective-permute-done.5.refs_1_), channel_id=1, source_target_pairs={{0,16},{16,0},{1,17},{17,1},{2,18},{18,2},{3,19},{19,3},{4,20},{20... | collective-permute-start | bytes 491528 | tf_op jit(solution)/shard_map/ppermute | solution.py:166
  54.4 8.4 %collective-permute-start.14 = (bf16[2,320,128]{2,1,0:T(8,128)(2,1)S(1)}, bf16[2,320,128]{2,1,0:T(8,128)(2,1)S(1)}, u32[]{:S(2)}, u32[]{:S(2)}) collective-permute-start(bf16[2,320,128]{2,1,0:T(8,128)(2,1)S(1)} %collective-permute-done.6.refs_2_), channel_id=1, source_target_pairs={{0,16},{16,0},{1,17},{17,1},{2,18},{18,2},{3,19},{19,3},{4,20},{20... | collective-permute-start | bytes 491528 | tf_op jit(solution)/shard_map/ppermute | solution.py:166
  54.4 8.4 %collective-permute-start.15 = (bf16[2,320,128]{2,1,0:T(8,128)(2,1)S(1)}, bf16[2,320,128]{2,1,0:T(8,128)(2,1)S(1)}, u32[]{:S(2)}, u32[]{:S(2)}) collective-permute-start(bf16[2,320,128]{2,1,0:T(8,128)(2,1)S(1)} %collective-permute-done.7.refs_3_), channel_id=1, source_target_pairs={{0,16},{16,0},{1,17},{17,1},{2,18},{18,2},{3,19},{19,3},{4,20},{20... | collective-permute-start | bytes 491528 | tf_op jit(solution)/shard_map/ppermute | solution.py:166
  62.7 7.9 %collective-permute-start.12 = (bf16[2,320,128]{2,1,0:T(8,128)(2,1)S(1)}, bf16[2,320,128]{2,1,0:T(8,128)(2,1)S(1)}, u32[]{:S(2)}, u32[]{:S(2)}) collective-permute-start(bf16[2,320,128]{2,1,0:T(8,128)(2,1)S(1)} %collective-permute-done.11.refs_1_), channel_id=1, source_target_pairs={{0,16},{16,0},{1,17},{17,1},{2,18},{18,2},{3,19},{19,3},{4,20},{20... | collective-permute-start | bytes 491528 | tf_op jit(solution)/shard_map/ppermute | solution.py:166
  76.8 24.0 %copy-start.1 = (f32[256,128]{1,0:T(8,128)S(1)}, f32[256,128]{1,0:T(8,128)}, u32[]{:S(2)}) copy-start(f32[256,128]{1,0:T(8,128)} %res_ref.3) | copy-start | bytes 393220
  76.8 24.0 %all-to-all-start.1 = ((bf16[8,256,128]{2,1,0:T(8,128)(2,1)}), bf16[8,256,128]{2,1,0:T(8,128)(2,1)S(1)}, u32[]{:S(2)}, u32[]{:S(2)}) async-start(bf16[8,256,128]{2,1,0:T(8,128)(2,1)} %bitcast.2), calls=%async_computation.1 | async-start | bytes 1048576 | tf_op jit(solution)/shard_map/all_to_all | solution.py:214
  100.9 24.2 %copy-start.2 = (f32[256,128]{1,0:T(8,128)S(1)}, f32[256,128]{1,0:T(8,128)}, u32[]{:S(2)}) copy-start(f32[256,128]{1,0:T(8,128)} %sol_ref.1) | copy-start | bytes 393220

commit v3 on v2

v3 whole, which is shorter than its diff:
```python
import functools
import math

import jax
import jax.numpy as jnp
from jax import lax
from jax.experimental import pallas as pl
from jax.experimental.pallas import tpu as pltpu
from jax.sharding import Mesh
from jax.sharding import PartitionSpec as P

AXES = ("xh", "xl", "yl", "c", "yh", "zh", "zm", "zl")
ROWS = ("xh", "xl", "yl")
NEAR = ("zl", "yh", "zm")
PLANE = ("xh", "xl", "yl", "c", "yh")
DEPTH = ("zh", "zm", "zl")
FEATURES = 32
LOG2E = 1.4426950408889634
VMEM = pltpu.CompilerParams(vmem_limit_bytes=48 * 2**20)


def split3(v):
    one = v.astype(jnp.bfloat16).astype(jnp.float32)
    rest = v - one
    two = rest.astype(jnp.bfloat16).astype(jnp.float32)
    return one, two, rest - two


def prep_kernel(points_ref, inv_ref, dir_ref, row_ref, packed_ref):
    count = points_ref.shape[1]
    square = (FEATURES, FEATURES)
    diagonal = lax.broadcasted_iota(jnp.int32, square, 0) == lax.broadcasted_iota(jnp.int32, square, 1)
    inverse = jnp.sum(jnp.where(diagonal, inv_ref[...], 0.0), axis=1, keepdims=True)
    x = (points_ref[...].astype(jnp.float32) * inverse).astype(jnp.bfloat16).astype(jnp.float32)
    parts = split3(jnp.sum(x * x, axis=0, keepdims=True))
    place = lax.broadcasted_iota(jnp.int32, (FEATURES, count), 0)

    def operand(front, squares_at, ones_at):
        tail = jnp.where((place >= ones_at) & (place < ones_at + 3), 1.0, 0.0)
        for i, part in enumerate(parts):
            tail = jnp.where(place == squares_at + i, part, tail)
        half = count // 2
        stacked = jnp.concatenate([front[:, :half], tail[:, :half], front[:, half:], tail[:, half:]], axis=0)
        return stacked.T.astype(jnp.bfloat16)

    row_ref[...] = operand(x, 0, 3)
    packed_ref[0, :256, :] = dir_ref[...].astype(jnp.bfloat16)
    packed_ref[0, 256:, :] = operand(-2.0 * x, 3, 0)


def rows_kernel(x_ref, out_ref):
    lane = lax.broadcasted_iota(jnp.int32, (1, 128), 1)
    for j in range(x_ref.shape[0]):
        v = x_ref[j].astype(jnp.float32)
        r = pltpu.roll(v, 64, 1)
        out_ref[j, :128, :] = jnp.where(lane < 64, v, r).astype(jnp.bfloat16)
        out_ref[j, 128:, :] = jnp.where(lane < 64, r, v).astype(jnp.bfloat16)


def matern(d):
    m = jnp.maximum(d, 1e-30)
    t = m * lax.rsqrt(m)
    return (((m + 0.6) + (3.0 / math.sqrt(5.0)) * t) * jnp.exp2((-math.sqrt(5.0) * LOG2E) * t)).astype(jnp.bfloat16)


def tiles_kernel(n_bundles, has_sum, *refs):
    rows_ref, bundles, refs = refs[0], refs[1 : 1 + n_bundles], refs[1 + n_bundles :]
    if has_sum:
        sum_ref, refs = refs[0], refs[1:]
    out_ref, cols_ref, dirs_ref, acc_ref, ahead_ref = refs
    pieces = bundles[0].shape[0]
    total = n_bundles * pieces
    lane = lax.broadcasted_iota(jnp.int32, (1, 128), 1)
    first = jnp.where(lane < 64, 1.0, 0.0).astype(jnp.bfloat16)
    second = jnp.where(lane < 64, 0.0, 1.0).astype(jnp.bfloat16)
    for n in range(total):
        bundle = bundles[n // pieces]
        dirs_ref[n] = bundle[n % pieces, :256, :]
        both = bundle[n % pieces, 256:, :]
        cols_ref[n, :128, :] = both * first
        cols_ref[n, 128:, :] = both * second
    acc_ref[...] = sum_ref[...] if has_sum else jnp.zeros_like(acc_ref)

    def distances(n, slot):
        ahead_ref[slot] = lax.dot_general(
            rows_ref[...], cols_ref[n], (((1,), (1,)), ((), ())), preferred_element_type=jnp.float32
        )

    distances(0, 0)

    def body(turn, _):
        for s in range(2):
            n = turn * 2 + s
            distances(jnp.minimum(n + 1, total - 1), 1 - s)
            acc_ref[...] += jnp.dot(matern(ahead_ref[s]), dirs_ref[n], preferred_element_type=jnp.float32)
        return 0

    lax.fori_loop(0, total // 2, body, 0)
    out_ref[...] = acc_ref[...].astype(out_ref.dtype)


def tiles(rows, bundles, so_far, last=False):
    pieces = bundles[0].shape[0]
    n = len(bundles) * pieces
    count = rows.shape[0]
    args = (rows, *bundles) + (() if so_far is None else (so_far,))
    whole = pl.BlockSpec(memory_space=pltpu.VMEM)
    return pl.pallas_call(
        functools.partial(tiles_kernel, len(bundles), so_far is not None),
        out_shape=jax.ShapeDtypeStruct((count, 128), jnp.bfloat16 if last else jnp.float32),
        in_specs=[whole] * len(args),
        out_specs=whole,
        scratch_shapes=[
            pltpu.VMEM((n, 256, 128), jnp.bfloat16),
            pltpu.VMEM((n, 256, 128), jnp.bfloat16),
            pltpu.VMEM((count, 128), jnp.float32),
            pltpu.VMEM((2, count, 256), jnp.float32),
        ],
        compiler_params=VMEM,
        cost_estimate=pl.CostEstimate(flops=count * n * 256 * 256, bytes_accessed=0, transcendentals=0),
    )(*args)


def image_kernel(parts_ref, noise_ref, dir_ref, res_ref, image_ref, sums_ref):
    image = (5.0 / 3.0) * jnp.sum(parts_ref[...].astype(jnp.float32), axis=0) + noise_ref[0, 0] * dir_ref[...]
    image_ref[...] = image
    res = res_ref[...]
    col = lambda v: jnp.sum(v, axis=0, keepdims=True)
    sums_ref[0:1, :] = col(res * res)
    sums_ref[1:2, :] = col(dir_ref[...] * image)
    sums_ref[2:3, :] = col(res * image)
    sums_ref[3:4, :] = col(image * image)


def step_kernel(sums_ref, image_ref, sol_ref, res_ref, dir_ref, new_sol, new_res, new_dir):
    sums = jnp.sum(sums_ref[...], axis=0)
    old_norm, curvature, cross, image_sq = (sums[i : i + 1, :] for i in range(4))
    step = old_norm / curvature
    new_norm = jnp.maximum(old_norm - 2.0 * step * cross + step * step * image_sq, 0.0)
    direction = dir_ref[...]
    new_sol[...] = sol_ref[...] + step * direction
    residual = res_ref[...] - step * image_ref[...]
    new_res[...] = residual
    new_dir[...] = residual + (new_norm / old_norm) * direction


def turned(x, axis, by):
    count = lax.axis_size(axis)
    return lax.ppermute(x, axis, [(i, (i + by) % count) for i in range(count)])


def mirrored(x, axes):
    count = lax.axis_size(axes)
    return lax.ppermute(x, axes, [(i, count - 1 - i) for i in range(count)])


def from_all(x, axes):
    count = lax.axis_size(axes)
    return lax.all_to_all(jnp.broadcast_to(x[None], (count,) + x.shape), axes, 0, 0, tiled=True)


def on_device(points, inv_length, noise_var, solution, residual, direction):
    whole = pl.BlockSpec(memory_space=pltpu.VMEM)

    def after(x, done):
        return lax.optimization_barrier((x, done))[0]

    row, packed = pl.pallas_call(
        prep_kernel,
        out_shape=(
            jax.ShapeDtypeStruct((128, 128), jnp.bfloat16),
            jax.ShapeDtypeStruct((1, 384, 128), jnp.bfloat16),
        ),
        in_specs=[whole] * 3,
        out_specs=(whole,) * 2,
        compiler_params=VMEM,
    )(points.T, inv_length.reshape(1, FEATURES), direction)

    mirror = mirrored(packed, DEPTH)
    n_rows = lax.axis_size(ROWS)
    rows = pl.pallas_call(
        rows_kernel,
        out_shape=jax.ShapeDtypeStruct((n_rows, 256, 128), jnp.bfloat16),
        in_specs=[whole],
        out_specs=whole,
        compiler_params=VMEM,
    )(from_all(row, ROWS)).reshape(n_rows * 256, 128)
    pair = jnp.concatenate([packed, mirror], axis=0)
    own = after(pair, rows)
    near = [turned(own, a, 1) for a in NEAR]
    so_far = tiles(rows, [own, turned(own, "c", 1)], None)
    near = after(near, so_far)
    other = [turned(b, "c", 1) for b in near]
    far = [turned(near[(i + 1) % 3], a, 1) for i, a in enumerate(NEAR)]
    so_far = tiles(rows, near, so_far)
    so_far = tiles(rows, other, so_far)
    far = after(far, so_far)
    opposite = turned(far[0], NEAR[2], 1)
    other = [turned(b, "c", 1) for b in far]
    so_far = tiles(rows, far, so_far)
    opposite = after(opposite, so_far)
    opposite = [opposite, turned(opposite, "c", 1)]
    so_far = tiles(rows, other, so_far)
    so_far = tiles(rows, opposite, so_far, True)
    parts = lax.all_to_all(so_far.reshape(n_rows, 256, 128), ROWS, 0, 0, tiled=True)
    f32 = jax.ShapeDtypeStruct(direction.shape, jnp.float32)
    image, sums = pl.pallas_call(
        image_kernel,
        out_shape=(f32, jax.ShapeDtypeStruct((4, 128), jnp.float32)),
        in_specs=[whole, pl.BlockSpec(memory_space=pltpu.SMEM), whole, whole],
        out_specs=(whole, whole),
        compiler_params=VMEM,
    )(parts, noise_var.reshape(1, 1), direction, residual)
    sums = jnp.sum(from_all(sums, PLANE), axis=0)
    sums = from_all(sums, DEPTH)
    return pl.pallas_call(
        step_kernel,
        out_shape=(f32, f32, f32),
        in_specs=[whole] * 5,
        out_specs=(whole,) * 3,
        compiler_params=VMEM,
    )(sums, image, solution, residual, direction)


def solution(mesh):
    finer = Mesh(mesh.devices.reshape((2,) * 8), AXES)
    placed = P(AXES, None)
    return jax.shard_map(
        on_device,
        mesh=finer,
        in_specs=(placed, P(), P(), placed, placed, placed),
        out_specs=(placed,) * 3,
        check_vma=False,
    )
```

time: 126 us -> 114 us (0.905)
  Pallas kernels: 44.1 us -> 29.7 us
  starting transfers between devices: 32.6 us -> 28.7 us
  waiting for transfers between devices: 21.7 us -> 24 us
  blocking collectives: 24.2 us -> 26.3 us
  local copies, waits for them, and re-layouts: 1.56 us -> 3.04 us
    pallas_call x6, Pallas kernels: 42.5 us -> 28.4 us  [tiles(): pl.pallas_call(functools.partial(tiles_kernel, len(bundles), so_far is no...]
    ppermute x15, waiting for transfers between devices: 0.04 us -> 10.5 us  [turned(): return lax.ppermute(x, axis, [(i, (i + by) % count) for i in range(count)])]
    all_to_all x1, waiting for transfers between devices: 17.8 us -> 8.67 us  [on_device(): lax.all_to_all(so_far.reshape(n_rows, 256, 128), ROWS, 0, 0, tiled=True)]
    all_to_all x1, starting transfers between devices: 10.3 us -> 5.86 us  [from_all(): lax.all_to_all(jnp.broadcast_to(x[None], (count,) + x.shape), axes, 0, 0,...]
    all_to_all x2, blocking collectives: 24.2 us -> 26.3 us  [from_all(): lax.all_to_all(jnp.broadcast_to(x[None], (count,) + x.shape), axes, 0, 0,...]
    ppermute x1, waiting for transfers between devices: 3.04 us -> 4.9 us  [mirrored(): return lax.ppermute(x, axes, [(i, count - 1 - i) for i in range(count)])]
    unnamed x9 -> x12, local copies, waits for them, and re-layouts: 0.86 us -> 2.28 us
  transfers between devices with their start and end apart: 18 -> 18, of which waited for: 3 -> 5; matrix products, arithmetic and copies ran while one was open for 0% -> 0% of each run, Pallas kernels for 29% -> 21%
where the time goes in v3:
time: 114 us; the launch traced here: 113 us
  Pallas kernels  29.7 us (26%)
  starting transfers between devices  28.7 us (25%)
  blocking collectives  26.3 us (23%)
  waiting for transfers between devices  24 us (21%)
  local copies, waits for them, and re-layouts  3.04 us (3%)
  between operations  1.46 us (1%)
    pallas_call x6, Pallas kernels, tiles(): pl.pallas_call(functools.partial(tiles_kernel, len(bundles), so_far is no...  28.4 us
    all_to_all x2, blocking collectives, from_all(): lax.all_to_all(jnp.broadcast_to(x[None], (count,) + x.shape), axes, 0, 0,...  26.3 us
    ppermute x15, starting transfers between devices, turned(): return lax.ppermute(x, axis, [(i, (i + by) % count) for i in range(count)])  12.2 us
    ppermute x15, waiting for transfers between devices, turned(): return lax.ppermute(x, axis, [(i, (i + by) % count) for i in range(count)])  10.5 us
    all_to_all x1, waiting for transfers between devices, on_device(): lax.all_to_all(so_far.reshape(n_rows, 256, 128), ROWS, 0, 0, tiled=True)  8.67 us
    all_to_all x1, starting transfers between devices, from_all(): lax.all_to_all(jnp.broadcast_to(x[None], (count,) + x.shape), axes, 0, 0,...  5.86 us
    ppermute x1, starting transfers between devices, mirrored(): return lax.ppermute(x, axes, [(i, count - 1 - i) for i in range(count)])  5.58 us
    all_to_all x1, starting transfers between devices, on_device(): lax.all_to_all(so_far.reshape(n_rows, 256, 128), ROWS, 0, 0, tiled=True)  5.12 us
  transfers between devices with their start and end apart: 18, of which 5 were waited for; matrix products, arithmetic and copies ran while one was open for 0% of the time, Pallas kernels for 21%

profile of v3, /device:TPU:1, one launch (start us, length us, event | category | flops | bytes accessed | tf_op | source)
XLA Modules:
  0.0 113.2 jit_solution(7066275049703070746)
XLA Ops:
  0.6 0.0 copy-start.5
  0.6 0.6 copy-done.5
  1.3 0.0 copy-start
  1.3 0.9 copy-done
  2.2 0.0 copy-start.4
  2.2 0.7 copy-done.4
  2.9 0.2 shard_map.85
  3.1 0.7 broadcast_in_dim.6
  3.8 5.9 %all-to-all-start = ((bf16[8,128,128]{2,1,0:T(8,128)(2,1)}), bf16[8,128,128]{2,1,0:T(8,128)(2,1)S(1)}, u32[]{:S(2)}, u32[]{:S(2)}) async-start(bf16[8,128,128]{2,1,0:T(8,128)(2,1)} %broadcast_in_dim.6), calls=%async_computation | async-start | bytes 524288 | tf_op jit(solution)/shard_map/all_to_all | solution.py:159
  9.7 5.6 %collective-permute-start = (bf16[1,384,128]{2,1,0:T(8,128)(2,1)S(1)}, bf16[1,384,128]{2,1,0:T(8,128)(2,1)S(1)}, u32[]{:S(2)}, u32[]{:S(2)}) collective-permute-start(bf16[1,384,128]{2,1,0:T(8,128)(2,1)S(1)} %get-tuple-element.16), channel_id=1, source_target_pairs={{0,7},{1,6},{2,5},{3,4},{4,3},{5,2},{6,1},{7,0},{8,15},{9,14},{10,... | collective-permute-start | bytes 294920 | tf_op jit(solution)/shard_map/ppermute | solution.py:154
  15.3 4.9 %collective-permute-done = bf16[1,384,128]{2,1,0:T(8,128)(2,1)S(1)} collective-permute-done((bf16[1,384,128]{2,1,0:T(8,128)(2,1)S(1)}, bf16[1,384,128]{2,1,0:T(8,128)(2,1)S(1)}, u32[]{:S(2)}, u32[]{:S(2)}) %collective-permute-start) | collective-permute-done | bytes 98336 | tf_op jit(solution)/shard_map/ppermute | solution.py:154
  20.2 0.0 all-to-all-done.x_ref
  20.2 0.1 shard_map.86
  20.4 1.0 collective-permute-start.4
  21.4 0.0 collective-permute-start.1
  21.4 2.6 %collective-permute-start.2 = (bf16[2,384,128]{2,1,0:T(8,128)(2,1)S(1)}, bf16[2,384,128]{2,1,0:T(8,128)(2,1)S(1)}, u32[]{:S(2)}, u32[]{:S(2)}) collective-permute-start(bf16[2,384,128]{2,1,0:T(8,128)(2,1)S(1)} %pad_maximum_fusion.refs_1_), channel_id=1, source_target_pairs={{0,8},{8,0},{1,9},{9,1},{2,10},{10,2},{3,11},{11,3},{4,12},{12,4},... | collective-permute-start | bytes 589832 | tf_op jit(solution)/shard_map/ppermute | solution.py:149
  24.0 1.9 %collective-permute-start.3 = (bf16[2,384,128]{2,1,0:T(8,128)(2,1)S(1)}, bf16[2,384,128]{2,1,0:T(8,128)(2,1)S(1)}, u32[]{:S(2)}, u32[]{:S(2)}) collective-permute-start(bf16[2,384,128]{2,1,0:T(8,128)(2,1)S(1)} %pad_maximum_fusion.refs_1_), channel_id=1, source_target_pairs={{0,2},{2,0},{1,3},{3,1},{4,6},{6,4},{5,7},{7,5},{8,10},{10,8},{9,1... | collective-permute-start | bytes 589832 | tf_op jit(solution)/shard_map/ppermute | solution.py:149
  25.9 0.0 collective-permute-done.4.refs_2_
  25.9 3.6 %shard_map.87.refs_4_ = f32[2048,128]{1,0:T(8,128)S(1)} custom-call(bf16[2048,128]{1,0:T(8,128)(2,1)S(1)} %bitcast.6, bf16[2,384,128]{2,1,0:T(8,128)(2,1)S(1)} %pad_maximum_fusion.refs_1_, bf16[2,384,128]{2,1,0:T(8,128)(2,1)S(1)} %collective-permute-done.4.refs_2_), custom_call_target="tpu_custom_call" | custom-call | flops 536870912 | tf_op jit(solution)/shard_map/pallas_call | solution.py:108
  29.5 0.0 collective-permute-done.1.refs_1_
  29.6 0.0 collective-permute-done.2.refs_2_
  29.6 5.6 %collective-permute-done.3.refs_3_ = bf16[2,384,128]{2,1,0:T(8,128)(2,1)S(1)} collective-permute-done((bf16[2,384,128]{2,1,0:T(8,128)(2,1)S(1)}, bf16[2,384,128]{2,1,0:T(8,128)(2,1)S(1)}, u32[]{:S(2)}, u32[]{:S(2)}) %collective-permute-start.3) | collective-permute-done | bytes 196640 | tf_op jit(solution)/shard_map/ppermute | solution.py:149
  35.2 1.3 %collective-permute-start.10 = (bf16[2,384,128]{2,1,0:T(8,128)(2,1)S(1)}, bf16[2,384,128]{2,1,0:T(8,128)(2,1)S(1)}, u32[]{:S(2)}, u32[]{:S(2)}) collective-permute-start(bf16[2,384,128]{2,1,0:T(8,128)(2,1)S(1)} %collective-permute-done.3.refs_3_), channel_id=1, source_target_pairs={{0,16},{16,0},{1,17},{17,1},{2,18},{18,2},{3,19},{19,3},{4,20},{20... | collective-permute-start | bytes 589832 | tf_op jit(solution)/shard_map/ppermute | solution.py:149
  36.5 0.0 collective-permute-start.8
  36.5 0.5 collective-permute-start.9
  37.0 0.0 collective-permute-start.5
  37.0 0.3 collective-permute-start.6
  37.4 0.2 collective-permute-done.10.refs_3_
  37.6 1.7 %collective-permute-start.7 = (bf16[2,384,128]{2,1,0:T(8,128)(2,1)S(1)}, bf16[2,384,128]{2,1,0:T(8,128)(2,1)S(1)}, u32[]{:S(2)}, u32[]{:S(2)}) collective-permute-start(bf16[2,384,128]{2,1,0:T(8,128)(2,1)S(1)} %collective-permute-done.1.refs_1_), channel_id=1, source_target_pairs={{0,2},{2,0},{1,3},{3,1},{4,6},{6,4},{5,7},{7,5},{8,10},{10,8},{9,1... | collective-permute-start | bytes 589832 | tf_op jit(solution)/shard_map/ppermute | solution.py:149
  39.3 5.1 %shard_map.88.refs_4_ = f32[2048,128]{1,0:T(8,128)S(1)} custom-call(bf16[2048,128]{1,0:T(8,128)(2,1)S(1)} %bitcast.7, bf16[2,384,128]{2,1,0:T(8,128)(2,1)S(1)} %collective-permute-done.1.refs_1_, bf16[2,384,128]{2,1,0:T(8,128)(2,1)S(1)} %collective-permute-done.2.refs_2_, bf16[2,384,128]{2,1,0:T(8,128)(2,1)S(1)} %collective-permute-done.3.refs_3_, ...), custom_call_target="tpu_custom_call" | custom-call | flops 805306368 | tf_op jit(solution)/shard_map/pallas_call | solution.py:108
  44.4 0.0 collective-permute-done.8.refs_1_
  44.4 0.0 collective-permute-done.9.refs_2_
  44.4 5.1 %shard_map.89.refs_4_ = f32[2048,128]{1,0:T(8,128)S(1)} custom-call(bf16[2048,128]{1,0:T(8,128)(2,1)S(1)} %bitcast.8, bf16[2,384,128]{2,1,0:T(8,128)(2,1)S(1)} %collective-permute-done.8.refs_1_, bf16[2,384,128]{2,1,0:T(8,128)(2,1)S(1)} %collective-permute-done.9.refs_2_, bf16[2,384,128]{2,1,0:T(8,128)(2,1)S(1)} %collective-permute-done.10.refs_3_, ...), custom_call_target="tpu_custom_call" | custom-call | flops 805306368 | tf_op jit(solution)/shard_map/pallas_call | solution.py:108
  49.5 0.0 collective-permute-done.5.refs_1_
  49.5 0.0 collective-permute-done.6.refs_2_
  49.6 0.0 collective-permute-done.7.refs_3_
  49.6 0.8 collective-permute-start.11
  50.3 0.9 collective-permute-start.13
  51.3 0.0 collective-permute-start.14
  51.3 0.5 collective-permute-start.15
  51.8 5.1 %shard_map.90.refs_4_ = f32[2048,128]{1,0:T(8,128)S(1)} custom-call(bf16[2048,128]{1,0:T(8,128)(2,1)S(1)} %bitcast.9, bf16[2,384,128]{2,1,0:T(8,128)(2,1)S(1)} %collective-permute-done.5.refs_1_, bf16[2,384,128]{2,1,0:T(8,128)(2,1)S(1)} %collective-permute-done.6.refs_2_, bf16[2,384,128]{2,1,0:T(8,128)(2,1)S(1)} %collective-permute-done.7.refs_3_, ...), custom_call_target="tpu_custom_call" | custom-call | flops 805306368 | tf_op jit(solution)/shard_map/pallas_call | solution.py:108
  56.9 4.6 %collective-permute-done.11.refs_1_ = bf16[2,384,128]{2,1,0:T(8,128)(2,1)S(1)} collective-permute-done((bf16[2,384,128]{2,1,0:T(8,128)(2,1)S(1)}, bf16[2,384,128]{2,1,0:T(8,128)(2,1)S(1)}, u32[]{:S(2)}, u32[]{:S(2)}) %collective-permute-start.11) | collective-permute-done | bytes 196640 | tf_op jit(solution)/shard_map/ppermute | solution.py:149
  61.5 0.5 collective-permute-start.12
  62.0 0.0 collective-permute-done.13.refs_1_
  62.0 0.0 collective-permute-done.14.refs_2_
  62.0 0.0 collective-permute-done.15.refs_3_
  62.0 5.1 %shard_map.91.refs_3_ = f32[2048,128]{1,0:T(8,128)S(1)} custom-call(bf16[2048,128]{1,0:T(8,128)(2,1)S(1)} %bitcast.10, bf16[2,384,128]{2,1,0:T(8,128)(2,1)S(1)} %collective-permute-done.13.refs_1_, bf16[2,384,128]{2,1,0:T(8,128)(2,1)S(1)} %collective-permute-done.14.refs_2_, bf16[2,384,128]{2,1,0:T(8,128)(2,1)S(1)} %collective-permute-done.15.refs_3_, ...), custom_call_target="tpu_custom_call" | custom-call | flops 805306368 | tf_op jit(solution)/shard_map/pallas_call | solution.py:108
  67.1 0.0 collective-permute-done.12.refs_2_
  67.2 4.4 %shard_map.92 = bf16[2048,128]{1,0:T(8,128)(2,1)} custom-call(bf16[2048,128]{1,0:T(8,128)(2,1)S(1)} %bitcast.11, bf16[2,384,128]{2,1,0:T(8,128)(2,1)S(1)} %collective-permute-done.11.refs_1_, bf16[2,384,128]{2,1,0:T(8,128)(2,1)S(1)} %collective-permute-done.12.refs_2_, f32[2048,128]{1,0:T(8,128)S(1)} %shard_map.91.refs_3_), custom_call_target="tpu_custom_call" | custom-call | flops 536870912 | tf_op jit(solution)/shard_map/pallas_call | solution.py:108
  71.5 0.0 copy-start.1
  71.5 0.0 copy-start.2
  71.5 5.1 %all-to-all-start.1 = ((bf16[8,256,128]{2,1,0:T(8,128)(2,1)}), bf16[8,256,128]{2,1,0:T(8,128)(2,1)S(1)}, u32[]{:S(2)}, u32[]{:S(2)}) async-start(bf16[8,256,128]{2,1,0:T(8,128)(2,1)} %bitcast.3), calls=%async_computation.1 | async-start | bytes 1048576 | tf_op jit(solution)/shard_map/all_to_all | solution.py:205
  77.3 8.7 %all-to-all-done.1.parts_ref = bf16[8,256,128]{2,1,0:T(8,128)(2,1)S(1)} async-done(((bf16[8,256,128]{2,1,0:T(8,128)(2,1)}), bf16[8,256,128]{2,1,0:T(8,128)(2,1)S(1)}, u32[]{:S(2)}, u32[]{:S(2)}) %all-to-all-start.1) | async-done | bytes 524320 | tf_op jit(solution)/shard_map/all_to_all | solution.py:205
  86.0 0.0 copy-done.1
  86.0 0.0 copy-done.2
  86.0 0.1 shard_map.93
  86.1 0.0 copy-start.3
  86.1 13.5 %all_to_all.20 = f32[32,4,128]{2,1,0:T(4,128)S(1)} all-to-all(f32[32,4,128]{2,1,0:T(4,128)S(1)} %broadcast_in_dim.7), channel_id=1, replica_groups=mesh['xh'=2,'xl'=2,'yl'=2,'c'=2,'yh'=2,'zh'=2,'zm'=2,'zl'=2] {'xh','xl',..., dimensions={0} | all-to-all | bytes 131072 | tf_op jit(solution)/shard_map/all_to_all | solution.py:159
  99.7 12.8 %all_to_all.21.sums_ref = f32[8,4,128]{2,1,0:T(4,128)S(1)} all-to-all(f32[8,4,128]{2,1,0:T(4,128)S(1)} %broadcast_in_dim.8), channel_id=1, replica_groups=mesh['xh'=2,'xl'=2,'yl'=2,'c'=2,'yh'=2,'zh'=2,'zm'=2,'zl'=2] {'zh','zm',..., dimensions={0} | all-to-all | bytes 32768 | tf_op jit(solution)/shard_map/all_to_all | solution.py:159
  112.5 0.0 copy-done.3
  112.5 0.8 shard_map.94
  (4 shorter events, 0.1 us)
Async XLA Ops:
  0.6 0.7 copy-start.5
  1.3 0.9 copy-start
  2.2 0.7 copy-start.4
  3.8 16.4 %all-to-all-start = ((bf16[8,128,128]{2,1,0:T(8,128)(2,1)}), bf16[8,128,128]{2,1,0:T(8,128)(2,1)S(1)}, u32[]{:S(2)}, u32[]{:S(2)}) async-start(bf16[8,128,128]{2,1,0:T(8,128)(2,1)} %broadcast_in_dim.6), calls=%async_computation | async-start | bytes 524288 | tf_op jit(solution)/shard_map/all_to_all | solution.py:159
  9.7 10.5 %collective-permute-start = (bf16[1,384,128]{2,1,0:T(8,128)(2,1)S(1)}, bf16[1,384,128]{2,1,0:T(8,128)(2,1)S(1)}, u32[]{:S(2)}, u32[]{:S(2)}) collective-permute-start(bf16[1,384,128]{2,1,0:T(8,128)(2,1)S(1)} %get-tuple-element.16), channel_id=1, source_target_pairs={{0,7},{1,6},{2,5},{3,4},{4,3},{5,2},{6,1},{7,0},{8,15},{9,14},{10,... | collective-permute-start | bytes 294920 | tf_op jit(solution)/shard_map/ppermute | solution.py:154
  20.4 5.6 %collective-permute-start.4 = (bf16[2,384,128]{2,1,0:T(8,128)(2,1)S(1)}, bf16[2,384,128]{2,1,0:T(8,128)(2,1)S(1)}, u32[]{:S(2)}, u32[]{:S(2)}) collective-permute-start(bf16[2,384,128]{2,1,0:T(8,128)(2,1)S(1)} %pad_maximum_fusion.refs_1_), channel_id=1, source_target_pairs={{0,16},{16,0},{1,17},{17,1},{2,18},{18,2},{3,19},{19,3},{4,20},{20... | collective-permute-start | bytes 589832 | tf_op jit(solution)/shard_map/ppermute | solution.py:149
  21.4 8.1 %collective-permute-start.1 = (bf16[2,384,128]{2,1,0:T(8,128)(2,1)S(1)}, bf16[2,384,128]{2,1,0:T(8,128)(2,1)S(1)}, u32[]{:S(2)}, u32[]{:S(2)}) collective-permute-start(bf16[2,384,128]{2,1,0:T(8,128)(2,1)S(1)} %pad_maximum_fusion.refs_1_), channel_id=1, source_target_pairs={{0,1},{1,0},{2,3},{3,2},{4,5},{5,4},{6,7},{7,6},{8,9},{9,8},{10,11... | collective-permute-start | bytes 589832 | tf_op jit(solution)/shard_map/ppermute | solution.py:149
  21.4 8.1 %collective-permute-start.2 = (bf16[2,384,128]{2,1,0:T(8,128)(2,1)S(1)}, bf16[2,384,128]{2,1,0:T(8,128)(2,1)S(1)}, u32[]{:S(2)}, u32[]{:S(2)}) collective-permute-start(bf16[2,384,128]{2,1,0:T(8,128)(2,1)S(1)} %pad_maximum_fusion.refs_1_), channel_id=1, source_target_pairs={{0,8},{8,0},{1,9},{9,1},{2,10},{10,2},{3,11},{11,3},{4,12},{12,4},... | collective-permute-start | bytes 589832 | tf_op jit(solution)/shard_map/ppermute | solution.py:149
  24.0 11.2 %collective-permute-start.3 = (bf16[2,384,128]{2,1,0:T(8,128)(2,1)S(1)}, bf16[2,384,128]{2,1,0:T(8,128)(2,1)S(1)}, u32[]{:S(2)}, u32[]{:S(2)}) collective-permute-start(bf16[2,384,128]{2,1,0:T(8,128)(2,1)S(1)} %pad_maximum_fusion.refs_1_), channel_id=1, source_target_pairs={{0,2},{2,0},{1,3},{3,1},{4,6},{6,4},{5,7},{7,5},{8,10},{10,8},{9,1... | collective-permute-start | bytes 589832 | tf_op jit(solution)/shard_map/ppermute | solution.py:149
  35.2 2.4 %collective-permute-start.10 = (bf16[2,384,128]{2,1,0:T(8,128)(2,1)S(1)}, bf16[2,384,128]{2,1,0:T(8,128)(2,1)S(1)}, u32[]{:S(2)}, u32[]{:S(2)}) collective-permute-start(bf16[2,384,128]{2,1,0:T(8,128)(2,1)S(1)} %collective-permute-done.3.refs_3_), channel_id=1, source_target_pairs={{0,16},{16,0},{1,17},{17,1},{2,18},{18,2},{3,19},{19,3},{4,20},{20... | collective-permute-start | bytes 589832 | tf_op jit(solution)/shard_map/ppermute | solution.py:149
  36.5 7.9 %collective-permute-start.8 = (bf16[2,384,128]{2,1,0:T(8,128)(2,1)S(1)}, bf16[2,384,128]{2,1,0:T(8,128)(2,1)S(1)}, u32[]{:S(2)}, u32[]{:S(2)}) collective-permute-start(bf16[2,384,128]{2,1,0:T(8,128)(2,1)S(1)} %collective-permute-done.1.refs_1_), channel_id=1, source_target_pairs={{0,16},{16,0},{1,17},{17,1},{2,18},{18,2},{3,19},{19,3},{4,20},{20... | collective-permute-start | bytes 589832 | tf_op jit(solution)/shard_map/ppermute | solution.py:149
  36.5 7.9 %collective-permute-start.9 = (bf16[2,384,128]{2,1,0:T(8,128)(2,1)S(1)}, bf16[2,384,128]{2,1,0:T(8,128)(2,1)S(1)}, u32[]{:S(2)}, u32[]{:S(2)}) collective-permute-start(bf16[2,384,128]{2,1,0:T(8,128)(2,1)S(1)} %collective-permute-done.2.refs_2_), channel_id=1, source_target_pairs={{0,16},{16,0},{1,17},{17,1},{2,18},{18,2},{3,19},{19,3},{4,20},{20... | collective-permute-start | bytes 589832 | tf_op jit(solution)/shard_map/ppermute | solution.py:149
  37.0 12.5 %collective-permute-start.5 = (bf16[2,384,128]{2,1,0:T(8,128)(2,1)S(1)}, bf16[2,384,128]{2,1,0:T(8,128)(2,1)S(1)}, u32[]{:S(2)}, u32[]{:S(2)}) collective-permute-start(bf16[2,384,128]{2,1,0:T(8,128)(2,1)S(1)} %collective-permute-done.2.refs_2_), channel_id=1, source_target_pairs={{0,1},{1,0},{2,3},{3,2},{4,5},{5,4},{6,7},{7,6},{8,9},{9,8},{10,11... | collective-permute-start | bytes 589832 | tf_op jit(solution)/shard_map/ppermute | solution.py:149
  37.0 12.5 %collective-permute-start.6 = (bf16[2,384,128]{2,1,0:T(8,128)(2,1)S(1)}, bf16[2,384,128]{2,1,0:T(8,128)(2,1)S(1)}, u32[]{:S(2)}, u32[]{:S(2)}) collective-permute-start(bf16[2,384,128]{2,1,0:T(8,128)(2,1)S(1)} %collective-permute-done.3.refs_3_), channel_id=1, source_target_pairs={{0,8},{8,0},{1,9},{9,1},{2,10},{10,2},{3,11},{11,3},{4,12},{12,4},... | collective-permute-start | bytes 589832 | tf_op jit(solution)/shard_map/ppermute | solution.py:149
  37.6 12.0 %collective-permute-start.7 = (bf16[2,384,128]{2,1,0:T(8,128)(2,1)S(1)}, bf16[2,384,128]{2,1,0:T(8,128)(2,1)S(1)}, u32[]{:S(2)}, u32[]{:S(2)}) collective-permute-start(bf16[2,384,128]{2,1,0:T(8,128)(2,1)S(1)} %collective-permute-done.1.refs_1_), channel_id=1, source_target_pairs={{0,2},{2,0},{1,3},{3,1},{4,6},{6,4},{5,7},{7,5},{8,10},{10,8},{9,1... | collective-permute-start | bytes 589832 | tf_op jit(solution)/shard_map/ppermute | solution.py:149
  49.6 11.9 %collective-permute-start.11 = (bf16[2,384,128]{2,1,0:T(8,128)(2,1)S(1)}, bf16[2,384,128]{2,1,0:T(8,128)(2,1)S(1)}, u32[]{:S(2)}, u32[]{:S(2)}) collective-permute-start(bf16[2,384,128]{2,1,0:T(8,128)(2,1)S(1)} %collective-permute-done.5.refs_1_), channel_id=1, source_target_pairs={{0,2},{2,0},{1,3},{3,1},{4,6},{6,4},{5,7},{7,5},{8,10},{10,8},{9,1... | collective-permute-start | bytes 589832 | tf_op jit(solution)/shard_map/ppermute | solution.py:149
  50.3 11.7 %collective-permute-start.13 = (bf16[2,384,128]{2,1,0:T(8,128)(2,1)S(1)}, bf16[2,384,128]{2,1,0:T(8,128)(2,1)S(1)}, u32[]{:S(2)}, u32[]{:S(2)}) collective-permute-start(bf16[2,384,128]{2,1,0:T(8,128)(2,1)S(1)} %collective-permute-done.5.refs_1_), channel_id=1, source_target_pairs={{0,16},{16,0},{1,17},{17,1},{2,18},{18,2},{3,19},{19,3},{4,20},{20... | collective-permute-start | bytes 589832 | tf_op jit(solution)/shard_map/ppermute | solution.py:149
  51.3 10.7 %collective-permute-start.14 = (bf16[2,384,128]{2,1,0:T(8,128)(2,1)S(1)}, bf16[2,384,128]{2,1,0:T(8,128)(2,1)S(1)}, u32[]{:S(2)}, u32[]{:S(2)}) collective-permute-start(bf16[2,384,128]{2,1,0:T(8,128)(2,1)S(1)} %collective-permute-done.6.refs_2_), channel_id=1, source_target_pairs={{0,16},{16,0},{1,17},{17,1},{2,18},{18,2},{3,19},{19,3},{4,20},{20... | collective-permute-start | bytes 589832 | tf_op jit(solution)/shard_map/ppermute | solution.py:149
  51.3 10.7 %collective-permute-start.15 = (bf16[2,384,128]{2,1,0:T(8,128)(2,1)S(1)}, bf16[2,384,128]{2,1,0:T(8,128)(2,1)S(1)}, u32[]{:S(2)}, u32[]{:S(2)}) collective-permute-start(bf16[2,384,128]{2,1,0:T(8,128)(2,1)S(1)} %collective-permute-done.7.refs_3_), channel_id=1, source_target_pairs={{0,16},{16,0},{1,17},{17,1},{2,18},{18,2},{3,19},{19,3},{4,20},{20... | collective-permute-start | bytes 589832 | tf_op jit(solution)/shard_map/ppermute | solution.py:149
  61.5 5.6 %collective-permute-start.12 = (bf16[2,384,128]{2,1,0:T(8,128)(2,1)S(1)}, bf16[2,384,128]{2,1,0:T(8,128)(2,1)S(1)}, u32[]{:S(2)}, u32[]{:S(2)}) collective-permute-start(bf16[2,384,128]{2,1,0:T(8,128)(2,1)S(1)} %collective-permute-done.11.refs_1_), channel_id=1, source_target_pairs={{0,16},{16,0},{1,17},{17,1},{2,18},{18,2},{3,19},{19,3},{4,20},{20... | collective-permute-start | bytes 589832 | tf_op jit(solution)/shard_map/ppermute | solution.py:149
  71.5 14.4 %copy-start.1 = (f32[256,128]{1,0:T(8,128)S(1)}, f32[256,128]{1,0:T(8,128)}, u32[]{:S(2)}) copy-start(f32[256,128]{1,0:T(8,128)} %dir_ref.5) | copy-start | bytes 393220
  71.5 14.4 %copy-start.2 = (f32[256,128]{1,0:T(8,128)S(1)}, f32[256,128]{1,0:T(8,128)}, u32[]{:S(2)}) copy-start(f32[256,128]{1,0:T(8,128)} %res_ref.3) | copy-start | bytes 393220
  71.5 14.4 %all-to-all-start.1 = ((bf16[8,256,128]{2,1,0:T(8,128)(2,1)}), bf16[8,256,128]{2,1,0:T(8,128)(2,1)S(1)}, u32[]{:S(2)}, u32[]{:S(2)}) async-start(bf16[8,256,128]{2,1,0:T(8,128)(2,1)} %bitcast.3), calls=%async_computation.1 | async-start | bytes 1048576 | tf_op jit(solution)/shard_map/all_to_all | solution.py:205
  86.1 26.3 %copy-start.3 = (f32[256,128]{1,0:T(8,128)S(1)}, f32[256,128]{1,0:T(8,128)}, u32[]{:S(2)}) copy-start(f32[256,128]{1,0:T(8,128)} %sol_ref.1) | copy-start | bytes 393220

commit v4 on v3

--- a/solution.py
+++ b/solution.py
@@ -11,7 +11,6 @@
 
 AXES = ("xh", "xl", "yl", "c", "yh", "zh", "zm", "zl")
 ROWS = ("xh", "xl", "yl")
-NEAR = ("zl", "yh", "zm")
 PLANE = ("xh", "xl", "yl", "c", "yh")
 DEPTH = ("zh", "zm", "zl")
 FEATURES = 32
@@ -63,7 +62,7 @@
     return (((m + 0.6) + (3.0 / math.sqrt(5.0)) * t) * jnp.exp2((-math.sqrt(5.0) * LOG2E) * t)).astype(jnp.bfloat16)
 
 
-def tiles_kernel(n_bundles, has_sum, *refs):
+def tiles_kernel(n_bundles, has_sum, tile, *refs):
     rows_ref, bundles, refs = refs[0], refs[1 : 1 + n_bundles], refs[1 + n_bundles :]
     if has_sum:
         sum_ref, refs = refs[0], refs[1:]
@@ -81,21 +80,28 @@
         cols_ref[n, 128:, :] = both * second
     acc_ref[...] = sum_ref[...] if has_sum else jnp.zeros_like(acc_ref)
 
-    def distances(n, slot):
+    per_piece = rows_ref.shape[0] // tile
+
+    def at(k):
+        return pl.ds(pl.multiple_of((k % per_piece) * tile, tile), tile)
+
+    def distances(k, slot):
         ahead_ref[slot] = lax.dot_general(
-            rows_ref[...], cols_ref[n], (((1,), (1,)), ((), ())), preferred_element_type=jnp.float32
+            rows_ref[at(k), :], cols_ref[k // per_piece], (((1,), (1,)), ((), ())), preferred_element_type=jnp.float32
         )
 
     distances(0, 0)
 
     def body(turn, _):
         for s in range(2):
-            n = turn * 2 + s
-            distances(jnp.minimum(n + 1, total - 1), 1 - s)
-            acc_ref[...] += jnp.dot(matern(ahead_ref[s]), dirs_ref[n], preferred_element_type=jnp.float32)
+            k = turn * 2 + s
+            distances(jnp.minimum(k + 1, total * per_piece - 1), 1 - s)
+            acc_ref[at(k), :] += jnp.dot(
+                matern(ahead_ref[s]), dirs_ref[k // per_piece], preferred_element_type=jnp.float32
+            )
         return 0
 
-    lax.fori_loop(0, total // 2, body, 0)
+    lax.fori_loop(0, total * per_piece // 2, body, 0)
     out_ref[...] = acc_ref[...].astype(out_ref.dtype)
 
 
@@ -103,10 +109,11 @@
     pieces = bundles[0].shape[0]
     n = len(bundles) * pieces
     count = rows.shape[0]
+    tile = count if n > 4 else count // 2
     args = (rows, *bundles) + (() if so_far is None else (so_far,))
     whole = pl.BlockSpec(memory_space=pltpu.VMEM)
     return pl.pallas_call(
-        functools.partial(tiles_kernel, len(bundles), so_far is not None),
+        functools.partial(tiles_kernel, len(bundles), so_far is not None, tile),
         out_shape=jax.ShapeDtypeStruct((count, 128), jnp.bfloat16 if last else jnp.float32),
         in_specs=[whole] * len(args),
         out_specs=whole,
@@ -114,7 +121,7 @@
             pltpu.VMEM((n, 256, 128), jnp.bfloat16),
             pltpu.VMEM((n, 256, 128), jnp.bfloat16),
             pltpu.VMEM((count, 128), jnp.float32),
-            pltpu.VMEM((2, count, 256), jnp.float32),
+            pltpu.VMEM((2, tile, 256), jnp.float32),
         ],
         compiler_params=VMEM,
         cost_estimate=pl.CostEstimate(flops=count * n * 256 * 256, bytes_accessed=0, transcendentals=0),
@@ -185,23 +192,36 @@
         out_specs=whole,
         compiler_params=VMEM,
     )(from_all(row, ROWS)).reshape(n_rows * 256, 128)
+    def core(x):
+        return turned(x, "c", 1)
+
+    packed_here = after(packed, rows)
+    so_far = tiles(rows, [packed_here, core(packed)], None)
+    mirror = after(mirror, so_far)
     pair = jnp.concatenate([packed, mirror], axis=0)
-    own = after(pair, rows)
-    near = [turned(own, a, 1) for a in NEAR]
-    so_far = tiles(rows, [own, turned(own, "c", 1)], None)
-    near = after(near, so_far)
-    other = [turned(b, "c", 1) for b in near]
-    far = [turned(near[(i + 1) % 3], a, 1) for i, a in enumerate(NEAR)]
-    so_far = tiles(rows, near, so_far)
-    so_far = tiles(rows, other, so_far)
-    far = after(far, so_far)
-    opposite = turned(far[0], NEAR[2], 1)
-    other = [turned(b, "c", 1) for b in far]
-    so_far = tiles(rows, far, so_far)
-    opposite = after(opposite, so_far)
-    opposite = [opposite, turned(opposite, "c", 1)]
-    so_far = tiles(rows, other, so_far)
-    so_far = tiles(rows, opposite, so_far, True)
+    zl, yh, zm = (turned(pair, a, 1) for a in ("zl", "yh", "zm"))
+    so_far = tiles(rows, [mirror, core(mirror)], so_far)
+
+    zl, yh = after((zl, yh), so_far)
+    zl_core, yh_core, zl_yh = core(zl), core(yh), turned(zl, "yh", 1)
+    so_far = tiles(rows, [zl, yh], so_far)
+
+    zm = after(zm, so_far)
+    zm_core, zm_zl, zm_yh = core(zm), turned(zm, "zl", 1), turned(zm, "yh", 1)
+    so_far = tiles(rows, [zl_core, yh_core, zm], so_far)
+
+    zl_yh, zm_yh = after((zl_yh, zm_yh), so_far)
+    zl_yh_core, all_three = core(zl_yh), turned(zm_yh, "zl", 1)
+    so_far = tiles(rows, [zl_yh, zm_core], so_far)
+
+    zm_zl, zm_yh = after((zm_zl, zm_yh), so_far)
+    zm_zl_core, zm_yh_core = core(zm_zl), core(zm_yh)
+    so_far = tiles(rows, [zm_zl, zm_yh], so_far)
+
+    all_three = after(all_three, so_far)
+    all_three_core = core(all_three)
+    so_far = tiles(rows, [zl_yh_core, zm_zl_core, zm_yh_core], so_far)
+    so_far = tiles(rows, [all_three, all_three_core], so_far, True)
     parts = lax.all_to_all(so_far.reshape(n_rows, 256, 128), ROWS, 0, 0, tiled=True)
     f32 = jax.ShapeDtypeStruct(direction.shape, jnp.float32)
     image, sums = pl.pallas_call(

time: 114 us -> 109 us (0.956)
  waiting for transfers between devices: 24 us -> 16.6 us
  Pallas kernels: 29.7 us -> 31.9 us
  starting transfers between devices: 28.7 us -> 30.2 us
    ppermute x15 -> x16, waiting for transfers between devices: 10.5 us -> 5.25 us  [turned(): return lax.ppermute(x, axis, [(i, (i + by) % count) for i in range(count)])]
    ppermute x15 -> x16, starting transfers between devices: 12.2 us -> 14.5 us  [turned(): return lax.ppermute(x, axis, [(i, (i + by) % count) for i in range(count)])]
    pallas_call x6 -> x8, Pallas kernels: 28.4 us -> 30.7 us  [tiles(): pl.pallas_call(functools.partial(tiles_kernel, len(bundles), so_far is no...]
    ppermute x1, waiting for transfers between devices: 4.9 us -> 2.85 us  [mirrored(): return lax.ppermute(x, axes, [(i, count - 1 - i) for i in range(count)])]
    unnamed x12 -> x13, local copies, waits for them, and re-layouts: 2.28 us -> 2.29 us
  transfers between devices with their start and end apart: 18 -> 19, of which waited for: 5 -> 4; matrix products, arithmetic and copies ran while one was open for 0% -> 0% of each run, Pallas kernels for 21% -> 24%
where the time goes in v4:
time: 109 us
  Pallas kernels  31.9 us (29%)
  starting transfers between devices  30.2 us (28%)
  blocking collectives  25.5 us (23%)
  waiting for transfers between devices  16.6 us (15%)
  local copies, waits for them, and re-layouts  3.06 us (3%)
  between operations  1.48 us (1%)
    pallas_call x8, Pallas kernels, tiles(): pl.pallas_call(functools.partial(tiles_kernel, len(bundles), so_far is no...  30.7 us
    all_to_all x2, blocking collectives, from_all(): lax.all_to_all(jnp.broadcast_to(x[None], (count,) + x.shape), axes, 0, 0,...  25.5 us
    ppermute x16, starting transfers between devices, turned(): return lax.ppermute(x, axis, [(i, (i + by) % count) for i in range(count)])  14.5 us
    all_to_all x1, waiting for transfers between devices, on_device(): lax.all_to_all(so_far.reshape(n_rows, 256, 128), ROWS, 0, 0, tiled=True)  8.53 us
    all_to_all x1, starting transfers between devices, from_all(): lax.all_to_all(jnp.broadcast_to(x[None], (count,) + x.shape), axes, 0, 0,...  5.86 us
    ppermute x1, starting transfers between devices, mirrored(): return lax.ppermute(x, axes, [(i, count - 1 - i) for i in range(count)])  5.59 us
    ppermute x16, waiting for transfers between devices, turned(): return lax.ppermute(x, axis, [(i, (i + by) % count) for i in range(count)])  5.25 us
    all_to_all x1, starting transfers between devices, on_device(): lax.all_to_all(so_far.reshape(n_rows, 256, 128), ROWS, 0, 0, tiled=True)  4.25 us
  transfers between devices with their start and end apart: 19, of which 4 were waited for; matrix products, arithmetic and copies ran while one was open for 0% of the time, Pallas kernels for 24%

profile of v4, /device:TPU:1, one launch (start us, length us, event | category | flops | bytes accessed | tf_op | source)
XLA Modules:
  0.0 108.8 jit_solution(13776172107293882903)
XLA Ops:
  0.6 0.0 copy-start.5
  0.6 0.6 copy-done.5
  1.3 0.0 copy-start
  1.3 0.9 copy-done
  2.2 0.0 copy-start.4
  2.2 0.7 copy-done.4
  2.9 0.2 shard_map.85
  3.1 0.7 broadcast_in_dim.6
  3.8 5.9 %all-to-all-start = ((bf16[8,128,128]{2,1,0:T(8,128)(2,1)}), bf16[8,128,128]{2,1,0:T(8,128)(2,1)S(1)}, u32[]{:S(2)}, u32[]{:S(2)}) async-start(bf16[8,128,128]{2,1,0:T(8,128)(2,1)} %broadcast_in_dim.6), calls=%async_computation | async-start | bytes 524288 | tf_op jit(solution)/shard_map/all_to_all | solution.py:166
  9.7 1.0 collective-permute-start.1
  10.7 5.6 %collective-permute-start = (bf16[1,384,128]{2,1,0:T(8,128)(2,1)S(1)}, bf16[1,384,128]{2,1,0:T(8,128)(2,1)S(1)}, u32[]{:S(2)}, u32[]{:S(2)}) collective-permute-start(bf16[1,384,128]{2,1,0:T(8,128)(2,1)S(1)} %get-tuple-element.19.refs_1_), channel_id=1, source_target_pairs={{0,7},{1,6},{2,5},{3,4},{4,3},{5,2},{6,1},{7,0},{8,15},{9,14},{10,... | collective-permute-start | bytes 294920 | tf_op jit(solution)/shard_map/ppermute | solution.py:161
  16.3 0.0 all-to-all-done.x_ref
  16.3 0.1 shard_map.86
  16.4 0.0 collective-permute-done.1.refs_2_
  16.4 2.1 %shard_map.87.refs_3_ = f32[2048,128]{1,0:T(8,128)S(1)} custom-call(bf16[2048,128]{1,0:T(8,128)(2,1)S(1)} %bitcast.6, bf16[1,384,128]{2,1,0:T(8,128)(2,1)S(1)} %get-tuple-element.19.refs_1_, bf16[1,384,128]{2,1,0:T(8,128)(2,1)S(1)} %collective-permute-done.1.refs_2_), custom_call_target="tpu_custom_call" | custom-call | flops 268435456 | tf_op jit(solution)/shard_map/pallas_call | solution.py:115
  18.6 2.8 %collective-permute-done.refs_1_ = bf16[1,384,128]{2,1,0:T(8,128)(2,1)S(1)} collective-permute-done((bf16[1,384,128]{2,1,0:T(8,128)(2,1)S(1)}, bf16[1,384,128]{2,1,0:T(8,128)(2,1)S(1)}, u32[]{:S(2)}, u32[]{:S(2)}) %collective-permute-start) | collective-permute-done | bytes 98336 | tf_op jit(solution)/shard_map/ppermute | solution.py:161
  21.4 0.1 collective-permute-start.2
  21.5 2.7 %collective-permute-start.3 = (bf16[2,384,128]{2,1,0:T(8,128)(2,1)S(1)}, bf16[2,384,128]{2,1,0:T(8,128)(2,1)S(1)}, u32[]{:S(2)}, u32[]{:S(2)}) collective-permute-start(bf16[2,384,128]{2,1,0:T(8,128)(2,1)S(1)} %constant_dynamic-update-slice_fusion), channel_id=1, source_target_pairs={{0,8},{8,0},{1,9},{9,1},{2,10},{10,2},{3,11},{11,3},{4,12},{12,4},... | collective-permute-start | bytes 589832 | tf_op jit(solution)/shard_map/ppermute | solution.py:156
  24.2 1.0 collective-permute-start.4
  25.2 2.9 %collective-permute-start.6 = (bf16[2,384,128]{2,1,0:T(8,128)(2,1)S(1)}, bf16[2,384,128]{2,1,0:T(8,128)(2,1)S(1)}, u32[]{:S(2)}, u32[]{:S(2)}) collective-permute-start(bf16[2,384,128]{2,1,0:T(8,128)(2,1)S(1)} %constant_dynamic-update-slice_fusion), channel_id=1, source_target_pairs={{0,2},{2,0},{1,3},{3,1},{4,6},{6,4},{5,7},{7,5},{8,10},{10,8},{9,1... | collective-permute-start | bytes 589832 | tf_op jit(solution)/shard_map/ppermute | solution.py:156
  28.1 0.0 collective-permute-done.4.refs_2_
  28.1 2.1 %shard_map.88.refs_3_ = f32[2048,128]{1,0:T(8,128)S(1)} custom-call(bf16[2048,128]{1,0:T(8,128)(2,1)S(1)} %bitcast.7, bf16[1,384,128]{2,1,0:T(8,128)(2,1)S(1)} %collective-permute-done.refs_1_, bf16[1,384,128]{2,1,0:T(8,128)(2,1)S(1)} %collective-permute-done.4.refs_2_, f32[2048,128]{1,0:T(8,128)S(1)} %shard_map.87.refs_3_), custom_call_target="tpu_custom_call" | custom-call | flops 268435456 | tf_op jit(solution)/shard_map/pallas_call | solution.py:115
  30.2 0.0 collective-permute-done.2.refs_1_
  30.3 0.0 collective-permute-done.3.refs_2_
  30.3 0.4 collective-permute-start.8
  30.6 0.2 collective-permute-start.9
  30.9 3.8 %shard_map.89.refs_4_ = f32[2048,128]{1,0:T(8,128)S(1)} custom-call(bf16[2048,128]{1,0:T(8,128)(2,1)S(1)} %bitcast.8, bf16[2,384,128]{2,1,0:T(8,128)(2,1)S(1)} %collective-permute-done.2.refs_1_, bf16[2,384,128]{2,1,0:T(8,128)(2,1)S(1)} %collective-permute-done.3.refs_2_, f32[2048,128]{1,0:T(8,128)S(1)} %shard_map.88.refs_3_), custom_call_target="tpu_custom_call" | custom-call | flops 536870912 | tf_op jit(solution)/shard_map/pallas_call | solution.py:115
  34.7 2.9 %collective-permute-done.6.refs_3_ = bf16[2,384,128]{2,1,0:T(8,128)(2,1)S(1)} collective-permute-done((bf16[2,384,128]{2,1,0:T(8,128)(2,1)S(1)}, bf16[2,384,128]{2,1,0:T(8,128)(2,1)S(1)}, u32[]{:S(2)}, u32[]{:S(2)}) %collective-permute-start.6) | collective-permute-done | bytes 196640 | tf_op jit(solution)/shard_map/ppermute | solution.py:156
  37.6 0.4 collective-permute-start.7
  37.9 2.6 %collective-permute-start.5 = (bf16[2,384,128]{2,1,0:T(8,128)(2,1)S(1)}, bf16[2,384,128]{2,1,0:T(8,128)(2,1)S(1)}, u32[]{:S(2)}, u32[]{:S(2)}) collective-permute-start(bf16[2,384,128]{2,1,0:T(8,128)(2,1)S(1)} %collective-permute-done.2.refs_1_), channel_id=1, source_target_pairs={{0,8},{8,0},{1,9},{9,1},{2,10},{10,2},{3,11},{11,3},{4,12},{12,4},... | collective-permute-start | bytes 589832 | tf_op jit(solution)/shard_map/ppermute | solution.py:156
  40.6 1.1 %collective-permute-start.12 = (bf16[2,384,128]{2,1,0:T(8,128)(2,1)S(1)}, bf16[2,384,128]{2,1,0:T(8,128)(2,1)S(1)}, u32[]{:S(2)}, u32[]{:S(2)}) collective-permute-start(bf16[2,384,128]{2,1,0:T(8,128)(2,1)S(1)} %collective-permute-done.6.refs_3_), channel_id=1, source_target_pairs={{0,16},{16,0},{1,17},{17,1},{2,18},{18,2},{3,19},{19,3},{4,20},{20... | collective-permute-start | bytes 589832 | tf_op jit(solution)/shard_map/ppermute | solution.py:156
  41.7 0.0 collective-permute-done.8.refs_1_
  41.7 0.0 collective-permute-start.11
  41.7 0.0 collective-permute-done.9.refs_2_
  41.7 5.1 %shard_map.90.refs_3_ = f32[2048,128]{1,0:T(8,128)S(1)} custom-call(bf16[2048,128]{1,0:T(8,128)(2,1)S(1)} %bitcast.9, bf16[2,384,128]{2,1,0:T(8,128)(2,1)S(1)} %collective-permute-done.8.refs_1_, bf16[2,384,128]{2,1,0:T(8,128)(2,1)S(1)} %collective-permute-done.9.refs_2_, bf16[2,384,128]{2,1,0:T(8,128)(2,1)S(1)} %collective-permute-done.6.refs_3_, ...), custom_call_target="tpu_custom_call" | custom-call | flops 805306368 | tf_op jit(solution)/shard_map/pallas_call | solution.py:115
  46.8 0.0 collective-permute-done.7.refs_2_
  46.8 2.3 %collective-permute-done.5.refs_1_ = bf16[2,384,128]{2,1,0:T(8,128)(2,1)S(1)} collective-permute-done((bf16[2,384,128]{2,1,0:T(8,128)(2,1)S(1)}, bf16[2,384,128]{2,1,0:T(8,128)(2,1)S(1)}, u32[]{:S(2)}, u32[]{:S(2)}) %collective-permute-start.5) | collective-permute-done | bytes 196640 | tf_op jit(solution)/shard_map/ppermute | solution.py:156
  49.2 0.0 collective-permute-start.10
  49.2 0.0 collective-permute-done.12.refs_2_
  49.2 3.8 %shard_map.91.refs_3_ = f32[2048,128]{1,0:T(8,128)S(1)} custom-call(bf16[2048,128]{1,0:T(8,128)(2,1)S(1)} %bitcast.10, bf16[2,384,128]{2,1,0:T(8,128)(2,1)S(1)} %collective-permute-done.5.refs_1_, bf16[2,384,128]{2,1,0:T(8,128)(2,1)S(1)} %collective-permute-done.12.refs_2_, f32[2048,128]{1,0:T(8,128)S(1)} %shard_map.90.refs_3_), custom_call_target="tpu_custom_call" | custom-call | flops 536870912 | tf_op jit(solution)/shard_map/pallas_call | solution.py:115
  53.0 0.0 collective-permute-done.11.refs_1_
  53.0 1.5 %collective-permute-start.15 = (bf16[2,384,128]{2,1,0:T(8,128)(2,1)S(1)}, bf16[2,384,128]{2,1,0:T(8,128)(2,1)S(1)}, u32[]{:S(2)}, u32[]{:S(2)}) collective-permute-start(bf16[2,384,128]{2,1,0:T(8,128)(2,1)S(1)} %collective-permute-done.11.refs_1_), channel_id=1, source_target_pairs={{0,16},{16,0},{1,17},{17,1},{2,18},{18,2},{3,19},{19,3},{4,20},{20... | collective-permute-start | bytes 589832 | tf_op jit(solution)/shard_map/ppermute | solution.py:156
  54.6 0.1 collective-permute-start.16
  54.7 0.4 collective-permute-start.14
  55.1 3.8 %shard_map.92.refs_4_ = f32[2048,128]{1,0:T(8,128)S(1)} custom-call(bf16[2048,128]{1,0:T(8,128)(2,1)S(1)} %bitcast.11, bf16[2,384,128]{2,1,0:T(8,128)(2,1)S(1)} %collective-permute-done.11.refs_1_, bf16[2,384,128]{2,1,0:T(8,128)(2,1)S(1)} %collective-permute-done.7.refs_2_, f32[2048,128]{1,0:T(8,128)S(1)} %shard_map.91.refs_3_), custom_call_target="tpu_custom_call" | custom-call | flops 536870912 | tf_op jit(solution)/shard_map/pallas_call | solution.py:115
  58.9 0.0 collective-permute-done.10.refs_1_
  58.9 0.2 collective-permute-start.13
  59.1 0.0 collective-permute-done.15.refs_2_
  59.1 0.0 collective-permute-done.16.refs_3_
  59.1 0.0 collective-permute-done.14.refs_1_
  59.1 5.1 %shard_map.93.refs_3_ = f32[2048,128]{1,0:T(8,128)S(1)} custom-call(bf16[2048,128]{1,0:T(8,128)(2,1)S(1)} %bitcast.12, bf16[2,384,128]{2,1,0:T(8,128)(2,1)S(1)} %collective-permute-done.14.refs_1_, bf16[2,384,128]{2,1,0:T(8,128)(2,1)S(1)} %collective-permute-done.15.refs_2_, bf16[2,384,128]{2,1,0:T(8,128)(2,1)S(1)} %collective-permute-done.16.refs_3_, ...), custom_call_target="tpu_custom_call" | custom-call | flops 805306368 | tf_op jit(solution)/shard_map/pallas_call | solution.py:115
  64.3 0.0 collective-permute-done.13.refs_2_
  64.3 4.6 %shard_map.94 = bf16[2048,128]{1,0:T(8,128)(2,1)} custom-call(bf16[2048,128]{1,0:T(8,128)(2,1)S(1)} %bitcast.13, bf16[2,384,128]{2,1,0:T(8,128)(2,1)S(1)} %collective-permute-done.10.refs_1_, bf16[2,384,128]{2,1,0:T(8,128)(2,1)S(1)} %collective-permute-done.13.refs_2_, f32[2048,128]{1,0:T(8,128)S(1)} %shard_map.93.refs_3_), custom_call_target="tpu_custom_call" | custom-call | flops 536870912 | tf_op jit(solution)/shard_map/pallas_call | solution.py:115
  68.9 0.0 copy-start.1
  68.9 4.3 %all-to-all-start.1 = ((bf16[8,256,128]{2,1,0:T(8,128)(2,1)}), bf16[8,256,128]{2,1,0:T(8,128)(2,1)S(1)}, u32[]{:S(2)}, u32[]{:S(2)}) async-start(bf16[8,256,128]{2,1,0:T(8,128)(2,1)} %bitcast.3), calls=%async_computation.1 | async-start | bytes 1048576 | tf_op jit(solution)/shard_map/all_to_all | solution.py:225
  73.8 8.5 %all-to-all-done.1.parts_ref = bf16[8,256,128]{2,1,0:T(8,128)(2,1)S(1)} async-done(((bf16[8,256,128]{2,1,0:T(8,128)(2,1)}), bf16[8,256,128]{2,1,0:T(8,128)(2,1)S(1)}, u32[]{:S(2)}, u32[]{:S(2)}) %all-to-all-start.1) | async-done | bytes 524320 | tf_op jit(solution)/shard_map/all_to_all | solution.py:225
  82.3 0.0 copy-done.1
  82.3 0.0 copy-done.2
  82.4 0.1 shard_map.95
  82.5 0.0 copy-start.3
  82.5 13.5 %all_to_all.20 = f32[32,4,128]{2,1,0:T(4,128)S(1)} all-to-all(f32[32,4,128]{2,1,0:T(4,128)S(1)} %broadcast_in_dim.7), channel_id=1, replica_groups=mesh['xh'=2,'xl'=2,'yl'=2,'c'=2,'yh'=2,'zh'=2,'zm'=2,'zl'=2] {'xh','xl',..., dimensions={0} | all-to-all | bytes 131072 | tf_op jit(solution)/shard_map/all_to_all | solution.py:166
  96.0 12.0 %all_to_all.21.sums_ref = f32[8,4,128]{2,1,0:T(4,128)S(1)} all-to-all(f32[8,4,128]{2,1,0:T(4,128)S(1)} %broadcast_in_dim.8), channel_id=1, replica_groups=mesh['xh'=2,'xl'=2,'yl'=2,'c'=2,'yh'=2,'zh'=2,'zm'=2,'zl'=2] {'zh','zm',..., dimensions={0} | all-to-all | bytes 32768 | tf_op jit(solution)/shard_map/all_to_all | solution.py:166
  108.0 0.0 copy-done.3
  108.0 0.8 shard_map.96
  (6 shorter events, 0.1 us)
Async XLA Ops:
  0.6 0.7 copy-start.5
  1.3 0.9 copy-start
  2.2 0.7 copy-start.4
  3.8 12.4 %all-to-all-start = ((bf16[8,128,128]{2,1,0:T(8,128)(2,1)}), bf16[8,128,128]{2,1,0:T(8,128)(2,1)S(1)}, u32[]{:S(2)}, u32[]{:S(2)}) async-start(bf16[8,128,128]{2,1,0:T(8,128)(2,1)} %broadcast_in_dim.6), calls=%async_computation | async-start | bytes 524288 | tf_op jit(solution)/shard_map/all_to_all | solution.py:166
  9.7 6.7 %collective-permute-start.1 = (bf16[1,384,128]{2,1,0:T(8,128)(2,1)S(1)}, bf16[1,384,128]{2,1,0:T(8,128)(2,1)S(1)}, u32[]{:S(2)}, u32[]{:S(2)}) collective-permute-start(bf16[1,384,128]{2,1,0:T(8,128)(2,1)S(1)} %get-tuple-element.19.refs_1_), channel_id=1, source_target_pairs={{0,16},{16,0},{1,17},{17,1},{2,18},{18,2},{3,19},{19,3},{4,20},{20... | collective-permute-start | bytes 294920 | tf_op jit(solution)/shard_map/ppermute | solution.py:156
  10.7 10.8 %collective-permute-start = (bf16[1,384,128]{2,1,0:T(8,128)(2,1)S(1)}, bf16[1,384,128]{2,1,0:T(8,128)(2,1)S(1)}, u32[]{:S(2)}, u32[]{:S(2)}) collective-permute-start(bf16[1,384,128]{2,1,0:T(8,128)(2,1)S(1)} %get-tuple-element.19.refs_1_), channel_id=1, source_target_pairs={{0,7},{1,6},{2,5},{3,4},{4,3},{5,2},{6,1},{7,0},{8,15},{9,14},{10,... | collective-permute-start | bytes 294920 | tf_op jit(solution)/shard_map/ppermute | solution.py:161
  21.4 8.8 %collective-permute-start.2 = (bf16[2,384,128]{2,1,0:T(8,128)(2,1)S(1)}, bf16[2,384,128]{2,1,0:T(8,128)(2,1)S(1)}, u32[]{:S(2)}, u32[]{:S(2)}) collective-permute-start(bf16[2,384,128]{2,1,0:T(8,128)(2,1)S(1)} %constant_dynamic-update-slice_fusion), channel_id=1, source_target_pairs={{0,1},{1,0},{2,3},{3,2},{4,5},{5,4},{6,7},{7,6},{8,9},{9,8},{10,11... | collective-permute-start | bytes 589832 | tf_op jit(solution)/shard_map/ppermute | solution.py:156
  21.5 8.7 %collective-permute-start.3 = (bf16[2,384,128]{2,1,0:T(8,128)(2,1)S(1)}, bf16[2,384,128]{2,1,0:T(8,128)(2,1)S(1)}, u32[]{:S(2)}, u32[]{:S(2)}) collective-permute-start(bf16[2,384,128]{2,1,0:T(8,128)(2,1)S(1)} %constant_dynamic-update-slice_fusion), channel_id=1, source_target_pairs={{0,8},{8,0},{1,9},{9,1},{2,10},{10,2},{3,11},{11,3},{4,12},{12,4},... | collective-permute-start | bytes 589832 | tf_op jit(solution)/shard_map/ppermute | solution.py:156
  24.2 3.9 %collective-permute-start.4 = (bf16[1,384,128]{2,1,0:T(8,128)(2,1)S(1)}, bf16[1,384,128]{2,1,0:T(8,128)(2,1)S(1)}, u32[]{:S(2)}, u32[]{:S(2)}) collective-permute-start(bf16[1,384,128]{2,1,0:T(8,128)(2,1)S(1)} %collective-permute-done.refs_1_), channel_id=1, source_target_pairs={{0,16},{16,0},{1,17},{17,1},{2,18},{18,2},{3,19},{19,3},{4,20},{20... | collective-permute-start | bytes 294920 | tf_op jit(solution)/shard_map/ppermute | solution.py:156
  25.2 12.4 %collective-permute-start.6 = (bf16[2,384,128]{2,1,0:T(8,128)(2,1)S(1)}, bf16[2,384,128]{2,1,0:T(8,128)(2,1)S(1)}, u32[]{:S(2)}, u32[]{:S(2)}) collective-permute-start(bf16[2,384,128]{2,1,0:T(8,128)(2,1)S(1)} %constant_dynamic-update-slice_fusion), channel_id=1, source_target_pairs={{0,2},{2,0},{1,3},{3,1},{4,6},{6,4},{5,7},{7,5},{8,10},{10,8},{9,1... | collective-permute-start | bytes 589832 | tf_op jit(solution)/shard_map/ppermute | solution.py:156
  30.3 11.4 %collective-permute-start.8 = (bf16[2,384,128]{2,1,0:T(8,128)(2,1)S(1)}, bf16[2,384,128]{2,1,0:T(8,128)(2,1)S(1)}, u32[]{:S(2)}, u32[]{:S(2)}) collective-permute-start(bf16[2,384,128]{2,1,0:T(8,128)(2,1)S(1)} %collective-permute-done.2.refs_1_), channel_id=1, source_target_pairs={{0,16},{16,0},{1,17},{17,1},{2,18},{18,2},{3,19},{19,3},{4,20},{20... | collective-permute-start | bytes 589832 | tf_op jit(solution)/shard_map/ppermute | solution.py:156
  30.6 11.1 %collective-permute-start.9 = (bf16[2,384,128]{2,1,0:T(8,128)(2,1)S(1)}, bf16[2,384,128]{2,1,0:T(8,128)(2,1)S(1)}, u32[]{:S(2)}, u32[]{:S(2)}) collective-permute-start(bf16[2,384,128]{2,1,0:T(8,128)(2,1)S(1)} %collective-permute-done.3.refs_2_), channel_id=1, source_target_pairs={{0,16},{16,0},{1,17},{17,1},{2,18},{18,2},{3,19},{19,3},{4,20},{20... | collective-permute-start | bytes 589832 | tf_op jit(solution)/shard_map/ppermute | solution.py:156
  37.6 9.3 %collective-permute-start.7 = (bf16[2,384,128]{2,1,0:T(8,128)(2,1)S(1)}, bf16[2,384,128]{2,1,0:T(8,128)(2,1)S(1)}, u32[]{:S(2)}, u32[]{:S(2)}) collective-permute-start(bf16[2,384,128]{2,1,0:T(8,128)(2,1)S(1)} %collective-permute-done.6.refs_3_), channel_id=1, source_target_pairs={{0,8},{8,0},{1,9},{9,1},{2,10},{10,2},{3,11},{11,3},{4,12},{12,4},... | collective-permute-start | bytes 589832 | tf_op jit(solution)/shard_map/ppermute | solution.py:156
  37.9 11.2 %collective-permute-start.5 = (bf16[2,384,128]{2,1,0:T(8,128)(2,1)S(1)}, bf16[2,384,128]{2,1,0:T(8,128)(2,1)S(1)}, u32[]{:S(2)}, u32[]{:S(2)}) collective-permute-start(bf16[2,384,128]{2,1,0:T(8,128)(2,1)S(1)} %collective-permute-done.2.refs_1_), channel_id=1, source_target_pairs={{0,8},{8,0},{1,9},{9,1},{2,10},{10,2},{3,11},{11,3},{4,12},{12,4},... | collective-permute-start | bytes 589832 | tf_op jit(solution)/shard_map/ppermute | solution.py:156
  40.6 8.6 %collective-permute-start.12 = (bf16[2,384,128]{2,1,0:T(8,128)(2,1)S(1)}, bf16[2,384,128]{2,1,0:T(8,128)(2,1)S(1)}, u32[]{:S(2)}, u32[]{:S(2)}) collective-permute-start(bf16[2,384,128]{2,1,0:T(8,128)(2,1)S(1)} %collective-permute-done.6.refs_3_), channel_id=1, source_target_pairs={{0,16},{16,0},{1,17},{17,1},{2,18},{18,2},{3,19},{19,3},{4,20},{20... | collective-permute-start | bytes 589832 | tf_op jit(solution)/shard_map/ppermute | solution.py:156
  41.7 11.3 %collective-permute-start.11 = (bf16[2,384,128]{2,1,0:T(8,128)(2,1)S(1)}, bf16[2,384,128]{2,1,0:T(8,128)(2,1)S(1)}, u32[]{:S(2)}, u32[]{:S(2)}) collective-permute-start(bf16[2,384,128]{2,1,0:T(8,128)(2,1)S(1)} %collective-permute-done.6.refs_3_), channel_id=1, source_target_pairs={{0,1},{1,0},{2,3},{3,2},{4,5},{5,4},{6,7},{7,6},{8,9},{9,8},{10,11... | collective-permute-start | bytes 589832 | tf_op jit(solution)/shard_map/ppermute | solution.py:156
  49.2 9.8 %collective-permute-start.10 = (bf16[2,384,128]{2,1,0:T(8,128)(2,1)S(1)}, bf16[2,384,128]{2,1,0:T(8,128)(2,1)S(1)}, u32[]{:S(2)}, u32[]{:S(2)}) collective-permute-start(bf16[2,384,128]{2,1,0:T(8,128)(2,1)S(1)} %collective-permute-done.7.refs_2_), channel_id=1, source_target_pairs={{0,1},{1,0},{2,3},{3,2},{4,5},{5,4},{6,7},{7,6},{8,9},{9,8},{10,11... | collective-permute-start | bytes 589832 | tf_op jit(solution)/shard_map/ppermute | solution.py:156
  53.0 6.1 %collective-permute-start.15 = (bf16[2,384,128]{2,1,0:T(8,128)(2,1)S(1)}, bf16[2,384,128]{2,1,0:T(8,128)(2,1)S(1)}, u32[]{:S(2)}, u32[]{:S(2)}) collective-permute-start(bf16[2,384,128]{2,1,0:T(8,128)(2,1)S(1)} %collective-permute-done.11.refs_1_), channel_id=1, source_target_pairs={{0,16},{16,0},{1,17},{17,1},{2,18},{18,2},{3,19},{19,3},{4,20},{20... | collective-permute-start | bytes 589832 | tf_op jit(solution)/shard_map/ppermute | solution.py:156
  54.6 4.6 %collective-permute-start.16 = (bf16[2,384,128]{2,1,0:T(8,128)(2,1)S(1)}, bf16[2,384,128]{2,1,0:T(8,128)(2,1)S(1)}, u32[]{:S(2)}, u32[]{:S(2)}) collective-permute-start(bf16[2,384,128]{2,1,0:T(8,128)(2,1)S(1)} %collective-permute-done.7.refs_2_), channel_id=1, source_target_pairs={{0,16},{16,0},{1,17},{17,1},{2,18},{18,2},{3,19},{19,3},{4,20},{20... | collective-permute-start | bytes 589832 | tf_op jit(solution)/shard_map/ppermute | solution.py:156
  54.7 4.5 %collective-permute-start.14 = (bf16[2,384,128]{2,1,0:T(8,128)(2,1)S(1)}, bf16[2,384,128]{2,1,0:T(8,128)(2,1)S(1)}, u32[]{:S(2)}, u32[]{:S(2)}) collective-permute-start(bf16[2,384,128]{2,1,0:T(8,128)(2,1)S(1)} %collective-permute-done.5.refs_1_), channel_id=1, source_target_pairs={{0,16},{16,0},{1,17},{17,1},{2,18},{18,2},{3,19},{19,3},{4,20},{20... | collective-permute-start | bytes 589832 | tf_op jit(solution)/shard_map/ppermute | solution.py:156
  58.9 5.3 %collective-permute-start.13 = (bf16[2,384,128]{2,1,0:T(8,128)(2,1)S(1)}, bf16[2,384,128]{2,1,0:T(8,128)(2,1)S(1)}, u32[]{:S(2)}, u32[]{:S(2)}) collective-permute-start(bf16[2,384,128]{2,1,0:T(8,128)(2,1)S(1)} %collective-permute-done.10.refs_1_), channel_id=1, source_target_pairs={{0,16},{16,0},{1,17},{17,1},{2,18},{18,2},{3,19},{19,3},{4,20},{20... | collective-permute-start | bytes 589832 | tf_op jit(solution)/shard_map/ppermute | solution.py:156
  68.9 13.4 %copy-start.1 = (f32[256,128]{1,0:T(8,128)S(1)}, f32[256,128]{1,0:T(8,128)}, u32[]{:S(2)}) copy-start(f32[256,128]{1,0:T(8,128)} %dir_ref.5) | copy-start | bytes 393220
  68.9 13.4 %copy-start.2 = (f32[256,128]{1,0:T(8,128)S(1)}, f32[256,128]{1,0:T(8,128)}, u32[]{:S(2)}) copy-start(f32[256,128]{1,0:T(8,128)} %res_ref.3) | copy-start | bytes 393220
  68.9 13.4 %all-to-all-start.1 = ((bf16[8,256,128]{2,1,0:T(8,128)(2,1)}), bf16[8,256,128]{2,1,0:T(8,128)(2,1)S(1)}, u32[]{:S(2)}, u32[]{:S(2)}) async-start(bf16[8,256,128]{2,1,0:T(8,128)(2,1)} %bitcast.3), calls=%async_computation.1 | async-start | bytes 1048576 | tf_op jit(solution)/shard_map/all_to_all | solution.py:225
  82.5 25.5 %copy-start.3 = (f32[256,128]{1,0:T(8,128)S(1)}, f32[256,128]{1,0:T(8,128)}, u32[]{:S(2)}) copy-start(f32[256,128]{1,0:T(8,128)} %sol_ref.1) | copy-start | bytes 393220

commit v5 on v4

--- a/solution.py
+++ b/solution.py
@@ -25,7 +25,13 @@
     return one, two, rest - two
 
 
-def prep_kernel(points_ref, inv_ref, dir_ref, row_ref, packed_ref):
+def prep_kernel(points_hbm, inv_hbm, dir_hbm, row_ref, packed_ref, points_ref, inv_ref, dir_ref, done):
+    pairs = ((points_hbm, points_ref), (inv_hbm, inv_ref), (dir_hbm, dir_ref))
+    copies = [pltpu.make_async_copy(a, b, done.at[i]) for i, (a, b) in enumerate(pairs)]
+    for copy in copies:
+        copy.start()
+    for copy in copies:
+        copy.wait()
     count = points_ref.shape[1]
     square = (FEATURES, FEATURES)
     diagonal = lax.broadcasted_iota(jnp.int32, square, 0) == lax.broadcasted_iota(jnp.int32, square, 1)
@@ -42,7 +48,9 @@
         stacked = jnp.concatenate([front[:, :half], tail[:, :half], front[:, half:], tail[:, half:]], axis=0)
         return stacked.T.astype(jnp.bfloat16)
 
-    row_ref[...] = operand(x, 0, 3)
+    row = operand(x, 0, 3)
+    for j in range(row_ref.shape[0]):
+        row_ref[j] = row
     packed_ref[0, :256, :] = dir_ref[...].astype(jnp.bfloat16)
     packed_ref[0, 256:, :] = operand(-2.0 * x, 3, 0)
 
@@ -66,7 +74,8 @@
     rows_ref, bundles, refs = refs[0], refs[1 : 1 + n_bundles], refs[1 + n_bundles :]
     if has_sum:
         sum_ref, refs = refs[0], refs[1:]
-    out_ref, cols_ref, dirs_ref, acc_ref, ahead_ref = refs
+    out_ref, cols_ref, dirs_ref, ahead_ref, *refs = refs
+    acc_ref = refs[0] if refs else out_ref
     pieces = bundles[0].shape[0]
     total = n_bundles * pieces
     lane = lax.broadcasted_iota(jnp.int32, (1, 128), 1)
@@ -78,7 +87,10 @@
         both = bundle[n % pieces, 256:, :]
         cols_ref[n, :128, :] = both * first
         cols_ref[n, 128:, :] = both * second
-    acc_ref[...] = sum_ref[...] if has_sum else jnp.zeros_like(acc_ref)
+    if not has_sum:
+        acc_ref[...] = jnp.zeros_like(acc_ref)
+    elif refs:
+        acc_ref[...] = sum_ref[...]
 
     per_piece = rows_ref.shape[0] // tile
 
@@ -102,7 +114,8 @@
         return 0
 
     lax.fori_loop(0, total * per_piece // 2, body, 0)
-    out_ref[...] = acc_ref[...].astype(out_ref.dtype)
+    if refs:
+        out_ref[...] = acc_ref[...].astype(out_ref.dtype)
 
 
 def tiles(rows, bundles, so_far, last=False):
@@ -120,9 +133,10 @@
         scratch_shapes=[
             pltpu.VMEM((n, 256, 128), jnp.bfloat16),
             pltpu.VMEM((n, 256, 128), jnp.bfloat16),
-            pltpu.VMEM((count, 128), jnp.float32),
             pltpu.VMEM((2, tile, 256), jnp.float32),
-        ],
+        ]
+        + [pltpu.VMEM((count, 128), jnp.float32)] * last,
+        input_output_aliases={} if so_far is None or last else {len(args) - 1: 0},
         compiler_params=VMEM,
         cost_estimate=pl.CostEstimate(flops=count * n * 256 * 256, bytes_accessed=0, transcendentals=0),
     )(*args)
@@ -170,58 +184,68 @@
     whole = pl.BlockSpec(memory_space=pltpu.VMEM)
 
     def after(x, done):
-        return lax.optimization_barrier((x, done))[0]
-
-    row, packed = pl.pallas_call(
+        return lax.optimization_barrier((x, done))
+
+    def core(x):
+        return turned(x, "c", 1)
+
+    n_rows = lax.axis_size(ROWS)
+    anywhere = pl.BlockSpec(memory_space=pl.ANY)
+    row, own = pl.pallas_call(
         prep_kernel,
         out_shape=(
-            jax.ShapeDtypeStruct((128, 128), jnp.bfloat16),
+            jax.ShapeDtypeStruct((n_rows, 128, 128), jnp.bfloat16),
             jax.ShapeDtypeStruct((1, 384, 128), jnp.bfloat16),
         ),
-        in_specs=[whole] * 3,
+        in_specs=[anywhere] * 3,
         out_specs=(whole,) * 2,
-        compiler_params=VMEM,
+        scratch_shapes=[
+            pltpu.VMEM((FEATURES, 256), jnp.bfloat16),
+            pltpu.VMEM((1, FEATURES), jnp.float32),
+            pltpu.VMEM((256, 128), jnp.float32),
+            pltpu.SemaphoreType.DMA((3,)),
+        ],
     )(points.T, inv_length.reshape(1, FEATURES), direction)
 
-    mirror = mirrored(packed, DEPTH)
-    n_rows = lax.axis_size(ROWS)
+    zm, mirror, own_core = turned(own, "zm", 1), mirrored(own, DEPTH), core(own)
     rows = pl.pallas_call(
         rows_kernel,
         out_shape=jax.ShapeDtypeStruct((n_rows, 256, 128), jnp.bfloat16),
         in_specs=[whole],
         out_specs=whole,
         compiler_params=VMEM,
-    )(from_all(row, ROWS)).reshape(n_rows * 256, 128)
-    def core(x):
-        return turned(x, "c", 1)
-
-    packed_here = after(packed, rows)
-    so_far = tiles(rows, [packed_here, core(packed)], None)
-    mirror = after(mirror, so_far)
-    pair = jnp.concatenate([packed, mirror], axis=0)
-    zl, yh, zm = (turned(pair, a, 1) for a in ("zl", "yh", "zm"))
-    so_far = tiles(rows, [mirror, core(mirror)], so_far)
-
-    zl, yh = after((zl, yh), so_far)
-    zl_core, yh_core, zl_yh = core(zl), core(yh), turned(zl, "yh", 1)
-    so_far = tiles(rows, [zl, yh], so_far)
-
-    zm = after(zm, so_far)
-    zm_core, zm_zl, zm_yh = core(zm), turned(zm, "zl", 1), turned(zm, "yh", 1)
-    so_far = tiles(rows, [zl_core, yh_core, zm], so_far)
-
-    zl_yh, zm_yh = after((zl_yh, zm_yh), so_far)
-    zl_yh_core, all_three = core(zl_yh), turned(zm_yh, "zl", 1)
-    so_far = tiles(rows, [zl_yh, zm_core], so_far)
-
-    zm_zl, zm_yh = after((zm_zl, zm_yh), so_far)
-    zm_zl_core, zm_yh_core = core(zm_zl), core(zm_yh)
-    so_far = tiles(rows, [zm_zl, zm_yh], so_far)
-
-    all_three = after(all_three, so_far)
-    all_three_core = core(all_three)
-    so_far = tiles(rows, [zl_yh_core, zm_zl_core, zm_yh_core], so_far)
-    so_far = tiles(rows, [all_three, all_three_core], so_far, True)
+    )(lax.all_to_all(row, ROWS, 0, 0, tiled=True)).reshape(n_rows * 256, 128)
+
+    zm, rows = after(zm, rows)
+    a = jnp.concatenate([own, zm], axis=0)
+    zm_core, a_zl, a_yh = core(zm), turned(a, "zl", 1), turned(a, "yh", 1)
+    so_far = tiles(rows, [own, own_core], None)
+
+    mirror, so_far = after(mirror, so_far)
+    mirror_zm = turned(mirror, "zm", 1)
+    so_far = tiles(rows, [zm, zm_core], so_far)
+
+    (a_zl, a_yh), so_far = after((a_zl, a_yh), so_far)
+    a_zl_core, a_yh_core, a_zl_yh = core(a_zl), core(a_yh), turned(a_zl, "yh", 1)
+    so_far = tiles(rows, [a_zl, a_yh], so_far)
+
+    mirror_zm, so_far = after(mirror_zm, so_far)
+    b = jnp.concatenate([mirror, mirror_zm], axis=0)
+    b_core, b_zl, b_yh = core(b), turned(b, "zl", 1), turned(b, "yh", 1)
+    so_far = tiles(rows, [a_zl_core, a_yh_core, b], so_far)
+
+    a_zl_yh, so_far = after(a_zl_yh, so_far)
+    a_zl_yh_core = core(a_zl_yh)
+    so_far = tiles(rows, [a_zl_yh, b_core], so_far)
+
+    (b_zl, b_yh), so_far = after((b_zl, b_yh), so_far)
+    b_zl_core, b_yh_core, b_zl_yh = core(b_zl), core(b_yh), turned(b_zl, "yh", 1)
+    so_far = tiles(rows, [a_zl_yh_core, b_zl, b_yh], so_far)
+
+    b_zl_yh, so_far = after(b_zl_yh, so_far)
+    b_zl_yh_core = core(b_zl_yh)
+    so_far = tiles(rows, [b_zl_core, b_yh_core, b_zl_yh], so_far)
+    so_far = tiles(rows, [b_zl_yh_core], so_far, True)
     parts = lax.all_to_all(so_far.reshape(n_rows, 256, 128), ROWS, 0, 0, tiled=True)
     f32 = jax.ShapeDtypeStruct(direction.shape, jnp.float32)
     image, sums = pl.pallas_call(

time: 109 us -> 104 us (0.954)
  waiting for transfers between devices: 16.6 us -> 10.6 us
  starting transfers between devices: 30.2 us -> 33.2 us
  local copies, waits for them, and re-layouts: 3.06 us -> 0.08 us
    ppermute x16 -> x17, starting transfers between devices: 14.5 us -> 19.3 us  [turned(): return lax.ppermute(x, axis, [(i, (i + by) % count) for i in range(count)])]
    ppermute x16 -> x17, waiting for transfers between devices: 5.25 us -> 1.92 us  [turned(): return lax.ppermute(x, axis, [(i, (i + by) % count) for i in range(count)])]
    ppermute x1, waiting for transfers between devices: 2.85 us -> 0.01 us  [mirrored(): return lax.ppermute(x, axes, [(i, count - 1 - i) for i in range(count)])]
    unnamed x13 -> x10, local copies, waits for them, and re-layouts: 2.29 us -> 0.03 us
    ppermute x1, starting transfers between devices: 5.59 us -> 3.76 us  [mirrored(): return lax.ppermute(x, axes, [(i, count - 1 - i) for i in range(count)])]
    pallas_call x1, Pallas kernels: 0.19 us -> 1.89 us  [on_device(): pl.pallas_call(prep_kernel, out_shape=(jax.ShapeDtypeStruct((n_rows, 128,...]
    pallas_call x8, Pallas kernels: 30.7 us -> 29.4 us  [tiles(): pl.pallas_call(functools.partial(tiles_kernel, len(bundles), so_far is no...]
  transfers between devices with their start and end apart: 19 -> 20, of which waited for: 4 -> 2; matrix products, arithmetic and copies ran while one was open for 0% -> 0% of each run, Pallas kernels for 24% -> 26%
where the time goes in v5:
time: 104 us
  starting transfers between devices  33.2 us (32%)
  Pallas kernels  32.4 us (31%)
  blocking collectives  25.8 us (25%)
  waiting for transfers between devices  10.6 us (10%)
  between operations  1.48 us (1%)
    pallas_call x8, Pallas kernels, tiles(): pl.pallas_call(functools.partial(tiles_kernel, len(bundles), so_far is no...  29.4 us
    all_to_all x2, blocking collectives, from_all(): lax.all_to_all(jnp.broadcast_to(x[None], (count,) + x.shape), axes, 0, 0,...  25.8 us
    ppermute x17, starting transfers between devices, turned(): return lax.ppermute(x, axis, [(i, (i + by) % count) for i in range(count)])  19.3 us
    all_to_all x1, waiting for transfers between devices, on_device(): lax.all_to_all(so_far.reshape(n_rows, 256, 128), ROWS, 0, 0, tiled=True)  8.67 us
    all_to_all x1, starting transfers between devices, on_device(): lax.all_to_all(row, ROWS, 0, 0, tiled=True)  6.01 us
    all_to_all x1, starting transfers between devices, on_device(): lax.all_to_all(so_far.reshape(n_rows, 256, 128), ROWS, 0, 0, tiled=True)  4.14 us
    ppermute x1, starting transfers between devices, mirrored(): return lax.ppermute(x, axes, [(i, count - 1 - i) for i in range(count)])  3.76 us
  transfers between devices with their start and end apart: 20, of which 2 were waited for; matrix products, arithmetic and copies ran while one was open for 0% of the time, Pallas kernels for 26%

profile of v5, /device:TPU:1, one launch (start us, length us, event | category | flops | bytes accessed | tf_op | source)
XLA Modules:
  0.0 103.6 jit_solution(8933961749409072152)
XLA Ops:
  0.6 1.9 %shard_map.85 = (bf16[8,128,128]{2,1,0:T(8,128)(2,1)}, bf16[1,384,128]{2,1,0:T(8,128)(2,1)}) custom-call(bf16[32,256]{1,0:T(8,128)(2,1)} %bitcast.14, f32[1,32]{1,0:T(1,128)} %bitcast.15, f32[256,128]{1,0:T(8,128)} %dir_ref.3), custom_call_target="tpu_custom_call" | custom-call | tf_op jit(solution)/shard_map/pallas_call | solution.py:194
  2.5 0.0 copy-start.2
  2.5 6.0 %all-to-all-start = ((bf16[8,128,128]{2,1,0:T(8,128)(2,1)}), bf16[8,128,128]{2,1,0:T(8,128)(2,1)S(1)}, u32[]{:S(2)}, u32[]{:S(2)}) async-start(bf16[8,128,128]{2,1,0:T(8,128)(2,1)} %get-tuple-element.24), calls=%async_computation | async-start | bytes 524288 | tf_op jit(solution)/shard_map/all_to_all | solution.py:217
  8.5 0.0 copy-done.2
  8.6 3.1 %collective-permute-start = (bf16[1,384,128]{2,1,0:T(8,128)(2,1)S(1)}, bf16[1,384,128]{2,1,0:T(8,128)(2,1)S(1)}, u32[]{:S(2)}, u32[]{:S(2)}) collective-permute-start(bf16[1,384,128]{2,1,0:T(8,128)(2,1)S(1)} %copy-done.2), channel_id=1, source_target_pairs={{0,2},{2,0},{1,3},{3,1},{4,6},{6,4},{5,7},{7,5},{8,10},{10,8},{9,1... | collective-permute-start | bytes 294920 | tf_op jit(solution)/shard_map/ppermute | solution.py:170
  11.6 1.2 %collective-permute-start.2 = (bf16[1,384,128]{2,1,0:T(8,128)(2,1)S(1)}, bf16[1,384,128]{2,1,0:T(8,128)(2,1)S(1)}, u32[]{:S(2)}, u32[]{:S(2)}) collective-permute-start(bf16[1,384,128]{2,1,0:T(8,128)(2,1)S(1)} %copy-done.2), channel_id=1, source_target_pairs={{0,16},{16,0},{1,17},{17,1},{2,18},{18,2},{3,19},{19,3},{4,20},{20... | collective-permute-start | bytes 294920 | tf_op jit(solution)/shard_map/ppermute | solution.py:170
  12.9 3.8 %collective-permute-start.1 = (bf16[1,384,128]{2,1,0:T(8,128)(2,1)S(1)}, bf16[1,384,128]{2,1,0:T(8,128)(2,1)S(1)}, u32[]{:S(2)}, u32[]{:S(2)}) collective-permute-start(bf16[1,384,128]{2,1,0:T(8,128)(2,1)S(1)} %copy-done.2), channel_id=1, source_target_pairs={{0,7},{1,6},{2,5},{3,4},{4,3},{5,2},{6,1},{7,0},{8,15},{9,14},{10,... | collective-permute-start | bytes 294920 | tf_op jit(solution)/shard_map/ppermute | solution.py:175
  16.6 0.0 all-to-all-done.x_ref
  16.6 0.1 shard_map.86
  16.8 0.0 collective-permute-done.refs_1_
  16.8 1.7 %collective-permute-start.4 = (bf16[2,384,128]{2,1,0:T(8,128)(2,1)S(1)}, bf16[2,384,128]{2,1,0:T(8,128)(2,1)S(1)}, u32[]{:S(2)}, u32[]{:S(2)}) collective-permute-start(bf16[2,384,128]{2,1,0:T(8,128)(2,1)S(1)} %constant_dynamic-update-slice_fusion), channel_id=1, source_target_pairs={{0,1},{1,0},{2,3},{3,2},{4,5},{5,4},{6,7},{7,6},{8,9},{9,8},{10,11... | collective-permute-start | bytes 589832 | tf_op jit(solution)/shard_map/ppermute | solution.py:170
  18.5 2.6 %collective-permute-start.5 = (bf16[2,384,128]{2,1,0:T(8,128)(2,1)S(1)}, bf16[2,384,128]{2,1,0:T(8,128)(2,1)S(1)}, u32[]{:S(2)}, u32[]{:S(2)}) collective-permute-start(bf16[2,384,128]{2,1,0:T(8,128)(2,1)S(1)} %constant_dynamic-update-slice_fusion), channel_id=1, source_target_pairs={{0,8},{8,0},{1,9},{9,1},{2,10},{10,2},{3,11},{11,3},{4,12},{12,4},... | collective-permute-start | bytes 589832 | tf_op jit(solution)/shard_map/ppermute | solution.py:170
  21.2 0.8 collective-permute-start.6
  22.0 0.0 collective-permute-done.2.refs_2_
  22.0 2.1 %shard_map.87.refs_3_ = f32[2048,128]{1,0:T(8,128)S(1)} custom-call(bf16[2048,128]{1,0:T(8,128)(2,1)S(1)} %bitcast.6, bf16[1,384,128]{2,1,0:T(8,128)(2,1)S(1)} %copy-done.2, bf16[1,384,128]{2,1,0:T(8,128)(2,1)S(1)} %collective-permute-done.2.refs_2_), custom_call_target="tpu_custom_call" | custom-call | flops 268435456 | tf_op jit(solution)/shard_map/pallas_call | solution.py:128
  24.1 0.0 collective-permute-done.1
  24.1 2.9 %collective-permute-start.3 = (bf16[1,384,128]{2,1,0:T(8,128)(2,1)S(1)}, bf16[1,384,128]{2,1,0:T(8,128)(2,1)S(1)}, u32[]{:S(2)}, u32[]{:S(2)}) collective-permute-start(bf16[1,384,128]{2,1,0:T(8,128)(2,1)S(1)} %collective-permute-done.1), channel_id=1, source_target_pairs={{0,2},{2,0},{1,3},{3,1},{4,6},{6,4},{5,7},{7,5},{8,10},{10,8},{9,1... | collective-permute-start | bytes 294920 | tf_op jit(solution)/shard_map/ppermute | solution.py:170
  27.0 0.0 collective-permute-done.6.refs_2_
  27.0 2.0 %shard_map.88.refs_3_ = f32[2048,128]{1,0:T(8,128)S(1)} custom-call(bf16[2048,128]{1,0:T(8,128)(2,1)S(1)} %bitcast.7, bf16[1,384,128]{2,1,0:T(8,128)(2,1)S(1)} %collective-permute-done.refs_1_, bf16[1,384,128]{2,1,0:T(8,128)(2,1)S(1)} %collective-permute-done.6.refs_2_, f32[2048,128]{1,0:T(8,128)S(1)} %shard_map.87.refs_3_), custom_call_target="tpu_custom_call", output_to_operand_aliasing={{}: (3, {})} | custom-call | flops 268435456 | tf_op jit(solution)/shard_map/pallas_call | solution.py:128
  29.0 0.0 collective-permute-done.4.refs_1_
  29.0 0.0 collective-permute-done.5.refs_2_
  29.0 0.4 collective-permute-start.10
  29.4 0.6 collective-permute-start.9
  30.0 0.3 collective-permute-start.11
  30.3 3.7 %shard_map.89.refs_4_ = f32[2048,128]{1,0:T(8,128)S(1)} custom-call(bf16[2048,128]{1,0:T(8,128)(2,1)S(1)} %bitcast.8, bf16[2,384,128]{2,1,0:T(8,128)(2,1)S(1)} %collective-permute-done.4.refs_1_, bf16[2,384,128]{2,1,0:T(8,128)(2,1)S(1)} %collective-permute-done.5.refs_2_, f32[2048,128]{1,0:T(8,128)S(1)} %shard_map.88.refs_3_), custom_call_target="tpu_custom_call", output_to_operand_aliasing={{}: (3, {})} | custom-call | flops 536870912 | tf_op jit(solution)/shard_map/pallas_call | solution.py:128
  34.0 0.0 collective-permute-done.3
  34.0 0.3 collective-permute-start.12
  34.3 0.1 collective-permute-start.7
  34.4 0.0 collective-permute-done.10.refs_1_
  34.4 2.6 %collective-permute-start.8 = (bf16[2,384,128]{2,1,0:T(8,128)(2,1)S(1)}, bf16[2,384,128]{2,1,0:T(8,128)(2,1)S(1)}, u32[]{:S(2)}, u32[]{:S(2)}) collective-permute-start(bf16[2,384,128]{2,1,0:T(8,128)(2,1)S(1)} %constant_dynamic-update-slice_fusion.2.refs_3_), channel_id=1, source_target_pairs={{0,8},{8,0},{1,9},{9,1},{2,10},{10,2},{3,11},{11,3},{4,12},{12,4},... | collective-permute-start | bytes 589832 | tf_op jit(solution)/shard_map/ppermute | solution.py:170
  37.0 0.0 collective-permute-done.11.refs_2_
  37.1 5.0 %shard_map.90.refs_3_ = f32[2048,128]{1,0:T(8,128)S(1)} custom-call(bf16[2048,128]{1,0:T(8,128)(2,1)S(1)} %bitcast.9, bf16[2,384,128]{2,1,0:T(8,128)(2,1)S(1)} %collective-permute-done.10.refs_1_, bf16[2,384,128]{2,1,0:T(8,128)(2,1)S(1)} %collective-permute-done.11.refs_2_, ...), custom_call_target="tpu_custom_call", output_to_operand_aliasing={{}: (4, {})} | custom-call | flops 805306368 | tf_op jit(solution)/shard_map/pallas_call | solution.py:128
  42.1 0.0 collective-permute-done.9.refs_1_
  42.1 0.6 collective-permute-start.14
  42.7 0.0 collective-permute-done.12.refs_2_
  42.7 3.7 %shard_map.91.refs_4_ = f32[2048,128]{1,0:T(8,128)S(1)} custom-call(bf16[2048,128]{1,0:T(8,128)(2,1)S(1)} %bitcast.10, bf16[2,384,128]{2,1,0:T(8,128)(2,1)S(1)} %collective-permute-done.9.refs_1_, bf16[2,384,128]{2,1,0:T(8,128)(2,1)S(1)} %collective-permute-done.12.refs_2_, f32[2048,128]{1,0:T(8,128)S(1)} %shard_map.90.refs_3_), custom_call_target="tpu_custom_call", output_to_operand_aliasing={{}: (3, {})} | custom-call | flops 536870912 | tf_op jit(solution)/shard_map/pallas_call | solution.py:128
  46.4 0.0 collective-permute-done.7.refs_2_
  46.5 0.0 collective-permute-done.8.refs_3_
  46.5 0.7 collective-permute-start.13
  47.2 0.3 collective-permute-start.16
  47.5 0.2 collective-permute-start.17
  47.7 0.0 collective-permute-done.14.refs_1_
  47.7 5.0 %shard_map.92.refs_4_ = f32[2048,128]{1,0:T(8,128)S(1)} custom-call(bf16[2048,128]{1,0:T(8,128)(2,1)S(1)} %bitcast.11, bf16[2,384,128]{2,1,0:T(8,128)(2,1)S(1)} %collective-permute-done.14.refs_1_, bf16[2,384,128]{2,1,0:T(8,128)(2,1)S(1)} %collective-permute-done.7.refs_2_, ...), custom_call_target="tpu_custom_call", output_to_operand_aliasing={{}: (4, {})} | custom-call | flops 805306368 | tf_op jit(solution)/shard_map/pallas_call | solution.py:128
  52.7 1.9 %collective-permute-done.13.refs_3_ = bf16[2,384,128]{2,1,0:T(8,128)(2,1)S(1)} collective-permute-done((bf16[2,384,128]{2,1,0:T(8,128)(2,1)S(1)}, bf16[2,384,128]{2,1,0:T(8,128)(2,1)S(1)}, u32[]{:S(2)}, u32[]{:S(2)}) %collective-permute-start.13) | collective-permute-done | bytes 196640 | tf_op jit(solution)/shard_map/ppermute | solution.py:170
  54.6 0.8 collective-permute-start.15
  55.4 0.0 collective-permute-done.16.refs_1_
  55.4 0.0 collective-permute-done.17.refs_2_
  55.4 5.0 %shard_map.93.refs_2_ = f32[2048,128]{1,0:T(8,128)S(1)} custom-call(bf16[2048,128]{1,0:T(8,128)(2,1)S(1)} %bitcast.12, bf16[2,384,128]{2,1,0:T(8,128)(2,1)S(1)} %collective-permute-done.16.refs_1_, bf16[2,384,128]{2,1,0:T(8,128)(2,1)S(1)} %collective-permute-done.17.refs_2_, ...), custom_call_target="tpu_custom_call", output_to_operand_aliasing={{}: (4, {})} | custom-call | flops 805306368 | tf_op jit(solution)/shard_map/pallas_call | solution.py:128
  60.4 0.0 collective-permute-done.15.refs_1_
  60.4 2.9 %shard_map.94 = bf16[2048,128]{1,0:T(8,128)(2,1)} custom-call(bf16[2048,128]{1,0:T(8,128)(2,1)S(1)} %bitcast.13, bf16[2,384,128]{2,1,0:T(8,128)(2,1)S(1)} %collective-permute-done.15.refs_1_, f32[2048,128]{1,0:T(8,128)S(1)} %shard_map.93.refs_2_), custom_call_target="tpu_custom_call" | custom-call | flops 268435456 | tf_op jit(solution)/shard_map/pallas_call | solution.py:128
  63.3 0.0 copy-start
  63.3 0.0 copy-start.1
  63.3 4.1 %all-to-all-start.1 = ((bf16[8,256,128]{2,1,0:T(8,128)(2,1)}), bf16[8,256,128]{2,1,0:T(8,128)(2,1)S(1)}, u32[]{:S(2)}, u32[]{:S(2)}) async-start(bf16[8,256,128]{2,1,0:T(8,128)(2,1)} %bitcast.3), calls=%async_computation.1 | async-start | bytes 1048576 | tf_op jit(solution)/shard_map/all_to_all | solution.py:249
  68.1 8.7 %all-to-all-done.1.parts_ref = bf16[8,256,128]{2,1,0:T(8,128)(2,1)S(1)} async-done(((bf16[8,256,128]{2,1,0:T(8,128)(2,1)}), bf16[8,256,128]{2,1,0:T(8,128)(2,1)S(1)}, u32[]{:S(2)}, u32[]{:S(2)}) %all-to-all-start.1) | async-done | bytes 524320 | tf_op jit(solution)/shard_map/all_to_all | solution.py:249
  76.8 0.0 copy-done
  76.8 0.0 copy-done.1
  76.8 0.1 shard_map.95
  77.0 0.0 copy-start.3
  77.0 12.9 %all_to_all.20 = f32[32,4,128]{2,1,0:T(4,128)S(1)} all-to-all(f32[32,4,128]{2,1,0:T(4,128)S(1)} %broadcast_in_dim.4), channel_id=1, replica_groups=mesh['xh'=2,'xl'=2,'yl'=2,'c'=2,'yh'=2,'zh'=2,'zm'=2,'zl'=2] {'xh','xl',..., dimensions={0} | all-to-all | bytes 131072 | tf_op jit(solution)/shard_map/all_to_all | solution.py:180
  89.9 12.9 %all_to_all.21.sums_ref = f32[8,4,128]{2,1,0:T(4,128)S(1)} all-to-all(f32[8,4,128]{2,1,0:T(4,128)S(1)} %broadcast_in_dim.5), channel_id=1, replica_groups=mesh['xh'=2,'xl'=2,'yl'=2,'c'=2,'yh'=2,'zh'=2,'zm'=2,'zl'=2] {'zh','zm',..., dimensions={0} | all-to-all | bytes 32768 | tf_op jit(solution)/shard_map/all_to_all | solution.py:180
  102.8 0.0 copy-done.3
  102.8 0.8 shard_map.96
  (7 shorter events, 0.1 us)
Async XLA Ops:
  2.5 6.0 %copy-start.2 = (bf16[1,384,128]{2,1,0:T(8,128)(2,1)S(1)}, bf16[1,384,128]{2,1,0:T(8,128)(2,1)}, u32[]{:S(2)}) copy-start(bf16[1,384,128]{2,1,0:T(8,128)(2,1)} %get-tuple-element.23.refs_1_) | copy-start | bytes 294916
  2.5 14.1 %all-to-all-start = ((bf16[8,128,128]{2,1,0:T(8,128)(2,1)}), bf16[8,128,128]{2,1,0:T(8,128)(2,1)S(1)}, u32[]{:S(2)}, u32[]{:S(2)}) async-start(bf16[8,128,128]{2,1,0:T(8,128)(2,1)} %get-tuple-element.24), calls=%async_computation | async-start | bytes 524288 | tf_op jit(solution)/shard_map/all_to_all | solution.py:217
  8.6 8.2 %collective-permute-start = (bf16[1,384,128]{2,1,0:T(8,128)(2,1)S(1)}, bf16[1,384,128]{2,1,0:T(8,128)(2,1)S(1)}, u32[]{:S(2)}, u32[]{:S(2)}) collective-permute-start(bf16[1,384,128]{2,1,0:T(8,128)(2,1)S(1)} %copy-done.2), channel_id=1, source_target_pairs={{0,2},{2,0},{1,3},{3,1},{4,6},{6,4},{5,7},{7,5},{8,10},{10,8},{9,1... | collective-permute-start | bytes 294920 | tf_op jit(solution)/shard_map/ppermute | solution.py:170
  11.6 10.4 %collective-permute-start.2 = (bf16[1,384,128]{2,1,0:T(8,128)(2,1)S(1)}, bf16[1,384,128]{2,1,0:T(8,128)(2,1)S(1)}, u32[]{:S(2)}, u32[]{:S(2)}) collective-permute-start(bf16[1,384,128]{2,1,0:T(8,128)(2,1)S(1)} %copy-done.2), channel_id=1, source_target_pairs={{0,16},{16,0},{1,17},{17,1},{2,18},{18,2},{3,19},{19,3},{4,20},{20... | collective-permute-start | bytes 294920 | tf_op jit(solution)/shard_map/ppermute | solution.py:170
  12.9 11.2 %collective-permute-start.1 = (bf16[1,384,128]{2,1,0:T(8,128)(2,1)S(1)}, bf16[1,384,128]{2,1,0:T(8,128)(2,1)S(1)}, u32[]{:S(2)}, u32[]{:S(2)}) collective-permute-start(bf16[1,384,128]{2,1,0:T(8,128)(2,1)S(1)} %copy-done.2), channel_id=1, source_target_pairs={{0,7},{1,6},{2,5},{3,4},{4,3},{5,2},{6,1},{7,0},{8,15},{9,14},{10,... | collective-permute-start | bytes 294920 | tf_op jit(solution)/shard_map/ppermute | solution.py:175
  16.8 12.2 %collective-permute-start.4 = (bf16[2,384,128]{2,1,0:T(8,128)(2,1)S(1)}, bf16[2,384,128]{2,1,0:T(8,128)(2,1)S(1)}, u32[]{:S(2)}, u32[]{:S(2)}) collective-permute-start(bf16[2,384,128]{2,1,0:T(8,128)(2,1)S(1)} %constant_dynamic-update-slice_fusion), channel_id=1, source_target_pairs={{0,1},{1,0},{2,3},{3,2},{4,5},{5,4},{6,7},{7,6},{8,9},{9,8},{10,11... | collective-permute-start | bytes 589832 | tf_op jit(solution)/shard_map/ppermute | solution.py:170
  18.5 10.5 %collective-permute-start.5 = (bf16[2,384,128]{2,1,0:T(8,128)(2,1)S(1)}, bf16[2,384,128]{2,1,0:T(8,128)(2,1)S(1)}, u32[]{:S(2)}, u32[]{:S(2)}) collective-permute-start(bf16[2,384,128]{2,1,0:T(8,128)(2,1)S(1)} %constant_dynamic-update-slice_fusion), channel_id=1, source_target_pairs={{0,8},{8,0},{1,9},{9,1},{2,10},{10,2},{3,11},{11,3},{4,12},{12,4},... | collective-permute-start | bytes 589832 | tf_op jit(solution)/shard_map/ppermute | solution.py:170
  21.2 5.8 %collective-permute-start.6 = (bf16[1,384,128]{2,1,0:T(8,128)(2,1)S(1)}, bf16[1,384,128]{2,1,0:T(8,128)(2,1)S(1)}, u32[]{:S(2)}, u32[]{:S(2)}) collective-permute-start(bf16[1,384,128]{2,1,0:T(8,128)(2,1)S(1)} %collective-permute-done.refs_1_), channel_id=1, source_target_pairs={{0,16},{16,0},{1,17},{17,1},{2,18},{18,2},{3,19},{19,3},{4,20},{20... | collective-permute-start | bytes 294920 | tf_op jit(solution)/shard_map/ppermute | solution.py:170
  24.1 9.9 %collective-permute-start.3 = (bf16[1,384,128]{2,1,0:T(8,128)(2,1)S(1)}, bf16[1,384,128]{2,1,0:T(8,128)(2,1)S(1)}, u32[]{:S(2)}, u32[]{:S(2)}) collective-permute-start(bf16[1,384,128]{2,1,0:T(8,128)(2,1)S(1)} %collective-permute-done.1), channel_id=1, source_target_pairs={{0,2},{2,0},{1,3},{3,1},{4,6},{6,4},{5,7},{7,5},{8,10},{10,8},{9,1... | collective-permute-start | bytes 294920 | tf_op jit(solution)/shard_map/ppermute | solution.py:170
  29.0 5.4 %collective-permute-start.10 = (bf16[2,384,128]{2,1,0:T(8,128)(2,1)S(1)}, bf16[2,384,128]{2,1,0:T(8,128)(2,1)S(1)}, u32[]{:S(2)}, u32[]{:S(2)}) collective-permute-start(bf16[2,384,128]{2,1,0:T(8,128)(2,1)S(1)} %collective-permute-done.4.refs_1_), channel_id=1, source_target_pairs={{0,16},{16,0},{1,17},{17,1},{2,18},{18,2},{3,19},{19,3},{4,20},{20... | collective-permute-start | bytes 589832 | tf_op jit(solution)/shard_map/ppermute | solution.py:170
  29.4 12.7 %collective-permute-start.9 = (bf16[2,384,128]{2,1,0:T(8,128)(2,1)S(1)}, bf16[2,384,128]{2,1,0:T(8,128)(2,1)S(1)}, u32[]{:S(2)}, u32[]{:S(2)}) collective-permute-start(bf16[2,384,128]{2,1,0:T(8,128)(2,1)S(1)} %collective-permute-done.4.refs_1_), channel_id=1, source_target_pairs={{0,8},{8,0},{1,9},{9,1},{2,10},{10,2},{3,11},{11,3},{4,12},{12,4},... | collective-permute-start | bytes 589832 | tf_op jit(solution)/shard_map/ppermute | solution.py:170
  30.0 7.1 %collective-permute-start.11 = (bf16[2,384,128]{2,1,0:T(8,128)(2,1)S(1)}, bf16[2,384,128]{2,1,0:T(8,128)(2,1)S(1)}, u32[]{:S(2)}, u32[]{:S(2)}) collective-permute-start(bf16[2,384,128]{2,1,0:T(8,128)(2,1)S(1)} %collective-permute-done.5.refs_2_), channel_id=1, source_target_pairs={{0,16},{16,0},{1,17},{17,1},{2,18},{18,2},{3,19},{19,3},{4,20},{20... | collective-permute-start | bytes 589832 | tf_op jit(solution)/shard_map/ppermute | solution.py:170
  34.0 8.7 %collective-permute-start.12 = (bf16[2,384,128]{2,1,0:T(8,128)(2,1)S(1)}, bf16[2,384,128]{2,1,0:T(8,128)(2,1)S(1)}, u32[]{:S(2)}, u32[]{:S(2)}) collective-permute-start(bf16[2,384,128]{2,1,0:T(8,128)(2,1)S(1)} %constant_dynamic-update-slice_fusion.2.refs_3_), channel_id=1, source_target_pairs={{0,16},{16,0},{1,17},{17,1},{2,18},{18,2},{3,19},{19,3},{4,20},{20... | collective-permute-start | bytes 589832 | tf_op jit(solution)/shard_map/ppermute | solution.py:170
  34.3 12.1 %collective-permute-start.7 = (bf16[2,384,128]{2,1,0:T(8,128)(2,1)S(1)}, bf16[2,384,128]{2,1,0:T(8,128)(2,1)S(1)}, u32[]{:S(2)}, u32[]{:S(2)}) collective-permute-start(bf16[2,384,128]{2,1,0:T(8,128)(2,1)S(1)} %constant_dynamic-update-slice_fusion.2.refs_3_), channel_id=1, source_target_pairs={{0,1},{1,0},{2,3},{3,2},{4,5},{5,4},{6,7},{7,6},{8,9},{9,8},{10,11... | collective-permute-start | bytes 589832 | tf_op jit(solution)/shard_map/ppermute | solution.py:170
  34.4 12.0 %collective-permute-start.8 = (bf16[2,384,128]{2,1,0:T(8,128)(2,1)S(1)}, bf16[2,384,128]{2,1,0:T(8,128)(2,1)S(1)}, u32[]{:S(2)}, u32[]{:S(2)}) collective-permute-start(bf16[2,384,128]{2,1,0:T(8,128)(2,1)S(1)} %constant_dynamic-update-slice_fusion.2.refs_3_), channel_id=1, source_target_pairs={{0,8},{8,0},{1,9},{9,1},{2,10},{10,2},{3,11},{11,3},{4,12},{12,4},... | collective-permute-start | bytes 589832 | tf_op jit(solution)/shard_map/ppermute | solution.py:170
  42.1 5.6 %collective-permute-start.14 = (bf16[2,384,128]{2,1,0:T(8,128)(2,1)S(1)}, bf16[2,384,128]{2,1,0:T(8,128)(2,1)S(1)}, u32[]{:S(2)}, u32[]{:S(2)}) collective-permute-start(bf16[2,384,128]{2,1,0:T(8,128)(2,1)S(1)} %collective-permute-done.9.refs_1_), channel_id=1, source_target_pairs={{0,16},{16,0},{1,17},{17,1},{2,18},{18,2},{3,19},{19,3},{4,20},{20... | collective-permute-start | bytes 589832 | tf_op jit(solution)/shard_map/ppermute | solution.py:170
  46.5 8.1 %collective-permute-start.13 = (bf16[2,384,128]{2,1,0:T(8,128)(2,1)S(1)}, bf16[2,384,128]{2,1,0:T(8,128)(2,1)S(1)}, u32[]{:S(2)}, u32[]{:S(2)}) collective-permute-start(bf16[2,384,128]{2,1,0:T(8,128)(2,1)S(1)} %collective-permute-done.7.refs_2_), channel_id=1, source_target_pairs={{0,8},{8,0},{1,9},{9,1},{2,10},{10,2},{3,11},{11,3},{4,12},{12,4},... | collective-permute-start | bytes 589832 | tf_op jit(solution)/shard_map/ppermute | solution.py:170
  47.2 8.2 %collective-permute-start.16 = (bf16[2,384,128]{2,1,0:T(8,128)(2,1)S(1)}, bf16[2,384,128]{2,1,0:T(8,128)(2,1)S(1)}, u32[]{:S(2)}, u32[]{:S(2)}) collective-permute-start(bf16[2,384,128]{2,1,0:T(8,128)(2,1)S(1)} %collective-permute-done.7.refs_2_), channel_id=1, source_target_pairs={{0,16},{16,0},{1,17},{17,1},{2,18},{18,2},{3,19},{19,3},{4,20},{20... | collective-permute-start | bytes 589832 | tf_op jit(solution)/shard_map/ppermute | solution.py:170
  47.5 7.9 %collective-permute-start.17 = (bf16[2,384,128]{2,1,0:T(8,128)(2,1)S(1)}, bf16[2,384,128]{2,1,0:T(8,128)(2,1)S(1)}, u32[]{:S(2)}, u32[]{:S(2)}) collective-permute-start(bf16[2,384,128]{2,1,0:T(8,128)(2,1)S(1)} %collective-permute-done.8.refs_3_), channel_id=1, source_target_pairs={{0,16},{16,0},{1,17},{17,1},{2,18},{18,2},{3,19},{19,3},{4,20},{20... | collective-permute-start | bytes 589832 | tf_op jit(solution)/shard_map/ppermute | solution.py:170
  54.6 5.8 %collective-permute-start.15 = (bf16[2,384,128]{2,1,0:T(8,128)(2,1)S(1)}, bf16[2,384,128]{2,1,0:T(8,128)(2,1)S(1)}, u32[]{:S(2)}, u32[]{:S(2)}) collective-permute-start(bf16[2,384,128]{2,1,0:T(8,128)(2,1)S(1)} %collective-permute-done.13.refs_3_), channel_id=1, source_target_pairs={{0,16},{16,0},{1,17},{17,1},{2,18},{18,2},{3,19},{19,3},{4,20},{20... | collective-permute-start | bytes 589832 | tf_op jit(solution)/shard_map/ppermute | solution.py:170
  63.3 13.5 %copy-start = (f32[256,128]{1,0:T(8,128)S(1)}, f32[256,128]{1,0:T(8,128)}, u32[]{:S(2)}) copy-start(f32[256,128]{1,0:T(8,128)} %dir_ref.3) | copy-start | bytes 393220
  63.3 13.5 %copy-start.1 = (f32[256,128]{1,0:T(8,128)S(1)}, f32[256,128]{1,0:T(8,128)}, u32[]{:S(2)}) copy-start(f32[256,128]{1,0:T(8,128)} %res_ref.3) | copy-start | bytes 393220
  63.3 13.5 %all-to-all-start.1 = ((bf16[8,256,128]{2,1,0:T(8,128)(2,1)}), bf16[8,256,128]{2,1,0:T(8,128)(2,1)S(1)}, u32[]{:S(2)}, u32[]{:S(2)}) async-start(bf16[8,256,128]{2,1,0:T(8,128)(2,1)} %bitcast.3), calls=%async_computation.1 | async-start | bytes 1048576 | tf_op jit(solution)/shard_map/all_to_all | solution.py:249
  77.0 25.9 %copy-start.3 = (f32[256,128]{1,0:T(8,128)S(1)}, f32[256,128]{1,0:T(8,128)}, u32[]{:S(2)}) copy-start(f32[256,128]{1,0:T(8,128)} %sol_ref.1) | copy-start | bytes 393220

commit v6 on v5

--- a/solution.py
+++ b/solution.py
@@ -219,10 +219,10 @@
     zm, rows = after(zm, rows)
     a = jnp.concatenate([own, zm], axis=0)
     zm_core, a_zl, a_yh = core(zm), turned(a, "zl", 1), turned(a, "yh", 1)
+    mirror, rows = after(mirror, rows)
+    mirror_zm = turned(mirror, "zm", 1)
     so_far = tiles(rows, [own, own_core], None)
 
-    mirror, so_far = after(mirror, so_far)
-    mirror_zm = turned(mirror, "zm", 1)
     so_far = tiles(rows, [zm, zm_core], so_far)
 
     (a_zl, a_yh), so_far = after((a_zl, a_yh), so_far)
@@ -233,18 +233,16 @@
     b = jnp.concatenate([mirror, mirror_zm], axis=0)
     b_core, b_zl, b_yh = core(b), turned(b, "zl", 1), turned(b, "yh", 1)
     so_far = tiles(rows, [a_zl_core, a_yh_core, b], so_far)
-
-    a_zl_yh, so_far = after(a_zl_yh, so_far)
-    a_zl_yh_core = core(a_zl_yh)
     so_far = tiles(rows, [a_zl_yh, b_core], so_far)
 
-    (b_zl, b_yh), so_far = after((b_zl, b_yh), so_far)
-    b_zl_core, b_yh_core, b_zl_yh = core(b_zl), core(b_yh), turned(b_zl, "yh", 1)
-    so_far = tiles(rows, [a_zl_yh_core, b_zl, b_yh], so_far)
+    (a_zl_yh, b_zl, b_yh), so_far = after((a_zl_yh, b_zl, b_yh), so_far)
+    a_zl_yh_core, b_zl_core, b_yh_core, b_zl_yh = core(a_zl_yh), core(b_zl), core(b_yh), turned(b_zl, "yh", 1)
+    so_far = tiles(rows, [b_zl, b_yh], so_far)
+    so_far = tiles(rows, [a_zl_yh_core, b_zl_core], so_far)
 
     b_zl_yh, so_far = after(b_zl_yh, so_far)
     b_zl_yh_core = core(b_zl_yh)
-    so_far = tiles(rows, [b_zl_core, b_yh_core, b_zl_yh], so_far)
+    so_far = tiles(rows, [b_yh_core, b_zl_yh], so_far)
     so_far = tiles(rows, [b_zl_yh_core], so_far, True)
     parts = lax.all_to_all(so_far.reshape(n_rows, 256, 128), ROWS, 0, 0, tiled=True)
     f32 = jax.ShapeDtypeStruct(direction.shape, jnp.float32)

time: 104 us -> 104 us (level)
  waiting for transfers between devices: 10.6 us -> 8.91 us
    ppermute x17, waiting for transfers between devices: 1.92 us -> 0.47 us  [turned(): return lax.ppermute(x, axis, [(i, (i + by) % count) for i in range(count)])]
    pallas_call x8 -> x9, Pallas kernels: 29.4 us -> 30.5 us  [tiles(): pl.pallas_call(functools.partial(tiles_kernel, len(bundles), so_far is no...]
  transfers between devices with their start and end apart: 20 -> 20, of which waited for: 2 -> 2; matrix products, arithmetic and copies ran while one was open for 0% -> 0% of each run, Pallas kernels for 26% -> 27%
where the time goes in v6:
time: 104 us; the launch traced here: 103 us
  Pallas kernels  33.4 us (32%)
  starting transfers between devices  33.4 us (32%)
  blocking collectives  26.1 us (25%)
  waiting for transfers between devices  8.91 us (9%)
  between operations  1.52 us (1%)
    pallas_call x9, Pallas kernels, tiles(): pl.pallas_call(functools.partial(tiles_kernel, len(bundles), so_far is no...  30.5 us
    all_to_all x2, blocking collectives, from_all(): lax.all_to_all(jnp.broadcast_to(x[None], (count,) + x.shape), axes, 0, 0,...  26.1 us
    ppermute x17, starting transfers between devices, turned(): return lax.ppermute(x, axis, [(i, (i + by) % count) for i in range(count)])  19.2 us
    all_to_all x1, waiting for transfers between devices, on_device(): lax.all_to_all(so_far.reshape(n_rows, 256, 128), ROWS, 0, 0, tiled=True)  8.43 us
    all_to_all x1, starting transfers between devices, on_device(): lax.all_to_all(row, ROWS, 0, 0, tiled=True)  6.01 us
    all_to_all x1, starting transfers between devices, on_device(): lax.all_to_all(so_far.reshape(n_rows, 256, 128), ROWS, 0, 0, tiled=True)  4.53 us
    ppermute x1, starting transfers between devices, mirrored(): return lax.ppermute(x, axes, [(i, count - 1 - i) for i in range(count)])  3.76 us
  transfers between devices with their start and end apart: 20, of which 2 were waited for; matrix products, arithmetic and copies ran while one was open for 0% of the time, Pallas kernels for 27%

profile of v6, /device:TPU:1, one launch (start us, length us, event | category | flops | bytes accessed | tf_op | source)
XLA Modules:
  0.0 103.5 jit_solution(15225105735912001048)
XLA Ops:
  0.6 1.9 %shard_map.85 = (bf16[8,128,128]{2,1,0:T(8,128)(2,1)}, bf16[1,384,128]{2,1,0:T(8,128)(2,1)}) custom-call(bf16[32,256]{1,0:T(8,128)(2,1)} %bitcast.15, f32[1,32]{1,0:T(1,128)} %bitcast.16, f32[256,128]{1,0:T(8,128)} %dir_ref.3), custom_call_target="tpu_custom_call" | custom-call | tf_op jit(solution)/shard_map/pallas_call | solution.py:194
  2.5 0.0 copy-start.2
  2.5 6.0 %all-to-all-start = ((bf16[8,128,128]{2,1,0:T(8,128)(2,1)}), bf16[8,128,128]{2,1,0:T(8,128)(2,1)S(1)}, u32[]{:S(2)}, u32[]{:S(2)}) async-start(bf16[8,128,128]{2,1,0:T(8,128)(2,1)} %get-tuple-element.23), calls=%async_computation | async-start | bytes 524288 | tf_op jit(solution)/shard_map/all_to_all | solution.py:217
  8.5 0.0 copy-done.2
  8.6 3.1 %collective-permute-start.1 = (bf16[1,384,128]{2,1,0:T(8,128)(2,1)S(1)}, bf16[1,384,128]{2,1,0:T(8,128)(2,1)S(1)}, u32[]{:S(2)}, u32[]{:S(2)}) collective-permute-start(bf16[1,384,128]{2,1,0:T(8,128)(2,1)S(1)} %copy-done.2), channel_id=1, source_target_pairs={{0,2},{2,0},{1,3},{3,1},{4,6},{6,4},{5,7},{7,5},{8,10},{10,8},{9,1... | collective-permute-start | bytes 294920 | tf_op jit(solution)/shard_map/ppermute | solution.py:170
  11.6 3.8 %collective-permute-start = (bf16[1,384,128]{2,1,0:T(8,128)(2,1)S(1)}, bf16[1,384,128]{2,1,0:T(8,128)(2,1)S(1)}, u32[]{:S(2)}, u32[]{:S(2)}) collective-permute-start(bf16[1,384,128]{2,1,0:T(8,128)(2,1)S(1)} %copy-done.2), channel_id=1, source_target_pairs={{0,7},{1,6},{2,5},{3,4},{4,3},{5,2},{6,1},{7,0},{8,15},{9,14},{10,... | collective-permute-start | bytes 294920 | tf_op jit(solution)/shard_map/ppermute | solution.py:175
  15.4 0.0 all-to-all-done.x_ref
  15.4 0.1 shard_map.86
  15.5 0.0 collective-permute-done.1.refs_1_
  15.6 1.7 %collective-permute-start.2 = (bf16[2,384,128]{2,1,0:T(8,128)(2,1)S(1)}, bf16[2,384,128]{2,1,0:T(8,128)(2,1)S(1)}, u32[]{:S(2)}, u32[]{:S(2)}) collective-permute-start(bf16[2,384,128]{2,1,0:T(8,128)(2,1)S(1)} %constant_dynamic-update-slice_fusion), channel_id=1, source_target_pairs={{0,1},{1,0},{2,3},{3,2},{4,5},{5,4},{6,7},{7,6},{8,9},{9,8},{10,11... | collective-permute-start | bytes 589832 | tf_op jit(solution)/shard_map/ppermute | solution.py:170
  17.3 2.6 %collective-permute-start.3 = (bf16[2,384,128]{2,1,0:T(8,128)(2,1)S(1)}, bf16[2,384,128]{2,1,0:T(8,128)(2,1)S(1)}, u32[]{:S(2)}, u32[]{:S(2)}) collective-permute-start(bf16[2,384,128]{2,1,0:T(8,128)(2,1)S(1)} %constant_dynamic-update-slice_fusion), channel_id=1, source_target_pairs={{0,8},{8,0},{1,9},{9,1},{2,10},{10,2},{3,11},{11,3},{4,12},{12,4},... | collective-permute-start | bytes 589832 | tf_op jit(solution)/shard_map/ppermute | solution.py:170
  19.9 2.1 %collective-permute-start.5 = (bf16[1,384,128]{2,1,0:T(8,128)(2,1)S(1)}, bf16[1,384,128]{2,1,0:T(8,128)(2,1)S(1)}, u32[]{:S(2)}, u32[]{:S(2)}) collective-permute-start(bf16[1,384,128]{2,1,0:T(8,128)(2,1)S(1)} %copy-done.2), channel_id=1, source_target_pairs={{0,16},{16,0},{1,17},{17,1},{2,18},{18,2},{3,19},{19,3},{4,20},{20... | collective-permute-start | bytes 294920 | tf_op jit(solution)/shard_map/ppermute | solution.py:170
  22.0 0.0 collective-permute-start.4
  22.0 0.0 collective-permute-done
  22.0 2.8 %collective-permute-start.7 = (bf16[1,384,128]{2,1,0:T(8,128)(2,1)S(1)}, bf16[1,384,128]{2,1,0:T(8,128)(2,1)S(1)}, u32[]{:S(2)}, u32[]{:S(2)}) collective-permute-start(bf16[1,384,128]{2,1,0:T(8,128)(2,1)S(1)} %collective-permute-done), channel_id=1, source_target_pairs={{0,2},{2,0},{1,3},{3,1},{4,6},{6,4},{5,7},{7,5},{8,10},{10,8},{9,1... | collective-permute-start | bytes 294920 | tf_op jit(solution)/shard_map/ppermute | solution.py:170
  24.8 0.0 collective-permute-done.5.refs_2_
  24.8 2.1 %shard_map.87.refs_3_ = f32[2048,128]{1,0:T(8,128)S(1)} custom-call(bf16[2048,128]{1,0:T(8,128)(2,1)S(1)} %bitcast.6, bf16[1,384,128]{2,1,0:T(8,128)(2,1)S(1)} %copy-done.2, bf16[1,384,128]{2,1,0:T(8,128)(2,1)S(1)} %collective-permute-done.5.refs_2_), custom_call_target="tpu_custom_call" | custom-call | flops 268435456 | tf_op jit(solution)/shard_map/pallas_call | solution.py:128
  26.9 0.0 collective-permute-done.4.refs_2_
  26.9 2.0 %shard_map.88.refs_3_ = f32[2048,128]{1,0:T(8,128)S(1)} custom-call(bf16[2048,128]{1,0:T(8,128)(2,1)S(1)} %bitcast.7, bf16[1,384,128]{2,1,0:T(8,128)(2,1)S(1)} %collective-permute-done.1.refs_1_, bf16[1,384,128]{2,1,0:T(8,128)(2,1)S(1)} %collective-permute-done.4.refs_2_, f32[2048,128]{1,0:T(8,128)S(1)} %shard_map.87.refs_3_), custom_call_target="tpu_custom_call", output_to_operand_aliasing={{}: (3, {})} | custom-call | flops 268435456 | tf_op jit(solution)/shard_map/pallas_call | solution.py:128
  28.9 0.0 collective-permute-done.2.refs_1_
  28.9 0.0 collective-permute-done.3.refs_2_
  28.9 0.9 collective-permute-start.11
  29.8 0.1 collective-permute-start.12
  29.9 3.7 %shard_map.89.refs_4_ = f32[2048,128]{1,0:T(8,128)S(1)} custom-call(bf16[2048,128]{1,0:T(8,128)(2,1)S(1)} %bitcast.8, bf16[2,384,128]{2,1,0:T(8,128)(2,1)S(1)} %collective-permute-done.2.refs_1_, bf16[2,384,128]{2,1,0:T(8,128)(2,1)S(1)} %collective-permute-done.3.refs_2_, f32[2048,128]{1,0:T(8,128)S(1)} %shard_map.88.refs_3_), custom_call_target="tpu_custom_call", output_to_operand_aliasing={{}: (3, {})} | custom-call | flops 536870912 | tf_op jit(solution)/shard_map/pallas_call | solution.py:128
  33.6 0.0 collective-permute-done.7
  33.6 0.5 collective-permute-start.10
  34.1 0.4 collective-permute-start.6
  34.5 0.1 collective-permute-start.8
  34.6 0.0 collective-permute-done.11.refs_1_
  34.6 2.5 %collective-permute-start.9 = (bf16[2,384,128]{2,1,0:T(8,128)(2,1)S(1)}, bf16[2,384,128]{2,1,0:T(8,128)(2,1)S(1)}, u32[]{:S(2)}, u32[]{:S(2)}) collective-permute-start(bf16[2,384,128]{2,1,0:T(8,128)(2,1)S(1)} %constant_dynamic-update-slice_fusion.2.refs_3_), channel_id=1, source_target_pairs={{0,8},{8,0},{1,9},{9,1},{2,10},{10,2},{3,11},{11,3},{4,12},{12,4},... | collective-permute-start | bytes 589832 | tf_op jit(solution)/shard_map/ppermute | solution.py:170
  37.1 0.0 collective-permute-done.12.refs_2_
  37.1 5.0 %shard_map.90.refs_3_ = f32[2048,128]{1,0:T(8,128)S(1)} custom-call(bf16[2048,128]{1,0:T(8,128)(2,1)S(1)} %bitcast.9, bf16[2,384,128]{2,1,0:T(8,128)(2,1)S(1)} %collective-permute-done.11.refs_1_, bf16[2,384,128]{2,1,0:T(8,128)(2,1)S(1)} %collective-permute-done.12.refs_2_, ...), custom_call_target="tpu_custom_call", output_to_operand_aliasing={{}: (4, {})} | custom-call | flops 805306368 | tf_op jit(solution)/shard_map/pallas_call | solution.py:128
  42.1 0.0 collective-permute-done.10.refs_2_
  42.1 0.0 collective-permute-done.6.refs_1_
  42.1 3.7 %shard_map.91.refs_3_ = f32[2048,128]{1,0:T(8,128)S(1)} custom-call(bf16[2048,128]{1,0:T(8,128)(2,1)S(1)} %bitcast.10, bf16[2,384,128]{2,1,0:T(8,128)(2,1)S(1)} %collective-permute-done.6.refs_1_, bf16[2,384,128]{2,1,0:T(8,128)(2,1)S(1)} %collective-permute-done.10.refs_2_, f32[2048,128]{1,0:T(8,128)S(1)} %shard_map.90.refs_3_), custom_call_target="tpu_custom_call", output_to_operand_aliasing={{}: (3, {})} | custom-call | flops 536870912 | tf_op jit(solution)/shard_map/pallas_call | solution.py:128
  45.8 0.0 collective-permute-done.8.refs_1_
  45.9 0.4 collective-permute-done.9.refs_2_
  46.3 0.9 collective-permute-start.14
  47.2 0.1 collective-permute-start.15
  47.3 0.4 collective-permute-start.13
  47.7 0.7 collective-permute-start.17
  48.4 3.7 %shard_map.92.refs_3_ = f32[2048,128]{1,0:T(8,128)S(1)} custom-call(bf16[2048,128]{1,0:T(8,128)(2,1)S(1)} %bitcast.11, bf16[2,384,128]{2,1,0:T(8,128)(2,1)S(1)} %collective-permute-done.8.refs_1_, bf16[2,384,128]{2,1,0:T(8,128)(2,1)S(1)} %collective-permute-done.9.refs_2_, f32[2048,128]{1,0:T(8,128)S(1)} %shard_map.91.refs_3_), custom_call_target="tpu_custom_call", output_to_operand_aliasing={{}: (3, {})} | custom-call | flops 536870912 | tf_op jit(solution)/shard_map/pallas_call | solution.py:128
  52.1 0.0 collective-permute-done.14.refs_1_
  52.1 0.0 collective-permute-done.15.refs_2_
  52.1 3.7 %shard_map.93.refs_3_ = f32[2048,128]{1,0:T(8,128)S(1)} custom-call(bf16[2048,128]{1,0:T(8,128)(2,1)S(1)} %bitcast.12, bf16[2,384,128]{2,1,0:T(8,128)(2,1)S(1)} %collective-permute-done.14.refs_1_, bf16[2,384,128]{2,1,0:T(8,128)(2,1)S(1)} %collective-permute-done.15.refs_2_, f32[2048,128]{1,0:T(8,128)S(1)} %shard_map.92.refs_3_), custom_call_target="tpu_custom_call", output_to_operand_aliasing={{}: (3, {})} | custom-call | flops 536870912 | tf_op jit(solution)/shard_map/pallas_call | solution.py:128
  55.8 0.0 collective-permute-done.13.refs_2_
  55.8 0.3 collective-permute-start.16
  56.2 0.0 collective-permute-done.17.refs_1_
  56.2 3.7 %shard_map.94.refs_2_ = f32[2048,128]{1,0:T(8,128)S(1)} custom-call(bf16[2048,128]{1,0:T(8,128)(2,1)S(1)} %bitcast.13, bf16[2,384,128]{2,1,0:T(8,128)(2,1)S(1)} %collective-permute-done.17.refs_1_, bf16[2,384,128]{2,1,0:T(8,128)(2,1)S(1)} %collective-permute-done.13.refs_2_, f32[2048,128]{1,0:T(8,128)S(1)} %shard_map.93.refs_3_), custom_call_target="tpu_custom_call", output_to_operand_aliasing={{}: (3, {})} | custom-call | flops 536870912 | tf_op jit(solution)/shard_map/pallas_call | solution.py:128
  59.9 0.0 collective-permute-done.16.refs_1_
  59.9 2.9 %shard_map.95 = bf16[2048,128]{1,0:T(8,128)(2,1)} custom-call(bf16[2048,128]{1,0:T(8,128)(2,1)S(1)} %bitcast.14, bf16[2,384,128]{2,1,0:T(8,128)(2,1)S(1)} %collective-permute-done.16.refs_1_, f32[2048,128]{1,0:T(8,128)S(1)} %shard_map.94.refs_2_), custom_call_target="tpu_custom_call" | custom-call | flops 268435456 | tf_op jit(solution)/shard_map/pallas_call | solution.py:128
  62.8 0.0 copy-start
  62.8 0.0 copy-start.1
  62.8 4.5 %all-to-all-start.1 = ((bf16[8,256,128]{2,1,0:T(8,128)(2,1)}), bf16[8,256,128]{2,1,0:T(8,128)(2,1)S(1)}, u32[]{:S(2)}, u32[]{:S(2)}) async-start(bf16[8,256,128]{2,1,0:T(8,128)(2,1)} %bitcast.3), calls=%async_computation.1 | async-start | bytes 1048576 | tf_op jit(solution)/shard_map/all_to_all | solution.py:247
  68.0 8.4 %all-to-all-done.1.parts_ref = bf16[8,256,128]{2,1,0:T(8,128)(2,1)S(1)} async-done(((bf16[8,256,128]{2,1,0:T(8,128)(2,1)}), bf16[8,256,128]{2,1,0:T(8,128)(2,1)S(1)}, u32[]{:S(2)}, u32[]{:S(2)}) %all-to-all-start.1) | async-done | bytes 524320 | tf_op jit(solution)/shard_map/all_to_all | solution.py:247
  76.4 0.0 copy-done
  76.4 0.0 copy-done.1
  76.4 0.1 shard_map.96
  76.6 0.0 copy-start.3
  76.6 13.7 %all_to_all.20 = f32[32,4,128]{2,1,0:T(4,128)S(1)} all-to-all(f32[32,4,128]{2,1,0:T(4,128)S(1)} %broadcast_in_dim.4), channel_id=1, replica_groups=mesh['xh'=2,'xl'=2,'yl'=2,'c'=2,'yh'=2,'zh'=2,'zm'=2,'zl'=2] {'xh','xl',..., dimensions={0} | all-to-all | bytes 131072 | tf_op jit(solution)/shard_map/all_to_all | solution.py:180
  90.4 12.3 %all_to_all.21.sums_ref = f32[8,4,128]{2,1,0:T(4,128)S(1)} all-to-all(f32[8,4,128]{2,1,0:T(4,128)S(1)} %broadcast_in_dim.5), channel_id=1, replica_groups=mesh['xh'=2,'xl'=2,'yl'=2,'c'=2,'yh'=2,'zh'=2,'zm'=2,'zl'=2] {'zh','zm',..., dimensions={0} | all-to-all | bytes 32768 | tf_op jit(solution)/shard_map/all_to_all | solution.py:180
  102.7 0.0 copy-done.3
  102.7 0.8 shard_map.97
  (7 shorter events, 0.1 us)
Async XLA Ops:
  2.5 6.0 %copy-start.2 = (bf16[1,384,128]{2,1,0:T(8,128)(2,1)S(1)}, bf16[1,384,128]{2,1,0:T(8,128)(2,1)}, u32[]{:S(2)}) copy-start(bf16[1,384,128]{2,1,0:T(8,128)(2,1)} %get-tuple-element.22.refs_1_) | copy-start | bytes 294916
  2.5 12.9 %all-to-all-start = ((bf16[8,128,128]{2,1,0:T(8,128)(2,1)}), bf16[8,128,128]{2,1,0:T(8,128)(2,1)S(1)}, u32[]{:S(2)}, u32[]{:S(2)}) async-start(bf16[8,128,128]{2,1,0:T(8,128)(2,1)} %get-tuple-element.23), calls=%async_computation | async-start | bytes 524288 | tf_op jit(solution)/shard_map/all_to_all | solution.py:217
  8.6 7.0 %collective-permute-start.1 = (bf16[1,384,128]{2,1,0:T(8,128)(2,1)S(1)}, bf16[1,384,128]{2,1,0:T(8,128)(2,1)S(1)}, u32[]{:S(2)}, u32[]{:S(2)}) collective-permute-start(bf16[1,384,128]{2,1,0:T(8,128)(2,1)S(1)} %copy-done.2), channel_id=1, source_target_pairs={{0,2},{2,0},{1,3},{3,1},{4,6},{6,4},{5,7},{7,5},{8,10},{10,8},{9,1... | collective-permute-start | bytes 294920 | tf_op jit(solution)/shard_map/ppermute | solution.py:170
  11.6 10.4 %collective-permute-start = (bf16[1,384,128]{2,1,0:T(8,128)(2,1)S(1)}, bf16[1,384,128]{2,1,0:T(8,128)(2,1)S(1)}, u32[]{:S(2)}, u32[]{:S(2)}) collective-permute-start(bf16[1,384,128]{2,1,0:T(8,128)(2,1)S(1)} %copy-done.2), channel_id=1, source_target_pairs={{0,7},{1,6},{2,5},{3,4},{4,3},{5,2},{6,1},{7,0},{8,15},{9,14},{10,... | collective-permute-start | bytes 294920 | tf_op jit(solution)/shard_map/ppermute | solution.py:175
  15.6 13.3 %collective-permute-start.2 = (bf16[2,384,128]{2,1,0:T(8,128)(2,1)S(1)}, bf16[2,384,128]{2,1,0:T(8,128)(2,1)S(1)}, u32[]{:S(2)}, u32[]{:S(2)}) collective-permute-start(bf16[2,384,128]{2,1,0:T(8,128)(2,1)S(1)} %constant_dynamic-update-slice_fusion), channel_id=1, source_target_pairs={{0,1},{1,0},{2,3},{3,2},{4,5},{5,4},{6,7},{7,6},{8,9},{9,8},{10,11... | collective-permute-start | bytes 589832 | tf_op jit(solution)/shard_map/ppermute | solution.py:170
  17.3 11.6 %collective-permute-start.3 = (bf16[2,384,128]{2,1,0:T(8,128)(2,1)S(1)}, bf16[2,384,128]{2,1,0:T(8,128)(2,1)S(1)}, u32[]{:S(2)}, u32[]{:S(2)}) collective-permute-start(bf16[2,384,128]{2,1,0:T(8,128)(2,1)S(1)} %constant_dynamic-update-slice_fusion), channel_id=1, source_target_pairs={{0,8},{8,0},{1,9},{9,1},{2,10},{10,2},{3,11},{11,3},{4,12},{12,4},... | collective-permute-start | bytes 589832 | tf_op jit(solution)/shard_map/ppermute | solution.py:170
  19.9 4.9 %collective-permute-start.5 = (bf16[1,384,128]{2,1,0:T(8,128)(2,1)S(1)}, bf16[1,384,128]{2,1,0:T(8,128)(2,1)S(1)}, u32[]{:S(2)}, u32[]{:S(2)}) collective-permute-start(bf16[1,384,128]{2,1,0:T(8,128)(2,1)S(1)} %copy-done.2), channel_id=1, source_target_pairs={{0,16},{16,0},{1,17},{17,1},{2,18},{18,2},{3,19},{19,3},{4,20},{20... | collective-permute-start | bytes 294920 | tf_op jit(solution)/shard_map/ppermute | solution.py:170
  22.0 4.9 %collective-permute-start.4 = (bf16[1,384,128]{2,1,0:T(8,128)(2,1)S(1)}, bf16[1,384,128]{2,1,0:T(8,128)(2,1)S(1)}, u32[]{:S(2)}, u32[]{:S(2)}) collective-permute-start(bf16[1,384,128]{2,1,0:T(8,128)(2,1)S(1)} %collective-permute-done.1.refs_1_), channel_id=1, source_target_pairs={{0,16},{16,0},{1,17},{17,1},{2,18},{18,2},{3,19},{19,3},{4,20},{20... | collective-permute-start | bytes 294920 | tf_op jit(solution)/shard_map/ppermute | solution.py:170
  22.0 11.6 %collective-permute-start.7 = (bf16[1,384,128]{2,1,0:T(8,128)(2,1)S(1)}, bf16[1,384,128]{2,1,0:T(8,128)(2,1)S(1)}, u32[]{:S(2)}, u32[]{:S(2)}) collective-permute-start(bf16[1,384,128]{2,1,0:T(8,128)(2,1)S(1)} %collective-permute-done), channel_id=1, source_target_pairs={{0,2},{2,0},{1,3},{3,1},{4,6},{6,4},{5,7},{7,5},{8,10},{10,8},{9,1... | collective-permute-start | bytes 294920 | tf_op jit(solution)/shard_map/ppermute | solution.py:170
  28.9 5.7 %collective-permute-start.11 = (bf16[2,384,128]{2,1,0:T(8,128)(2,1)S(1)}, bf16[2,384,128]{2,1,0:T(8,128)(2,1)S(1)}, u32[]{:S(2)}, u32[]{:S(2)}) collective-permute-start(bf16[2,384,128]{2,1,0:T(8,128)(2,1)S(1)} %collective-permute-done.2.refs_1_), channel_id=1, source_target_pairs={{0,16},{16,0},{1,17},{17,1},{2,18},{18,2},{3,19},{19,3},{4,20},{20... | collective-permute-start | bytes 589832 | tf_op jit(solution)/shard_map/ppermute | solution.py:170
  29.8 7.3 %collective-permute-start.12 = (bf16[2,384,128]{2,1,0:T(8,128)(2,1)S(1)}, bf16[2,384,128]{2,1,0:T(8,128)(2,1)S(1)}, u32[]{:S(2)}, u32[]{:S(2)}) collective-permute-start(bf16[2,384,128]{2,1,0:T(8,128)(2,1)S(1)} %collective-permute-done.3.refs_2_), channel_id=1, source_target_pairs={{0,16},{16,0},{1,17},{17,1},{2,18},{18,2},{3,19},{19,3},{4,20},{20... | collective-permute-start | bytes 589832 | tf_op jit(solution)/shard_map/ppermute | solution.py:170
  33.6 8.5 %collective-permute-start.10 = (bf16[2,384,128]{2,1,0:T(8,128)(2,1)S(1)}, bf16[2,384,128]{2,1,0:T(8,128)(2,1)S(1)}, u32[]{:S(2)}, u32[]{:S(2)}) collective-permute-start(bf16[2,384,128]{2,1,0:T(8,128)(2,1)S(1)} %constant_dynamic-update-slice_fusion.2.refs_3_), channel_id=1, source_target_pairs={{0,16},{16,0},{1,17},{17,1},{2,18},{18,2},{3,19},{19,3},{4,20},{20... | collective-permute-start | bytes 589832 | tf_op jit(solution)/shard_map/ppermute | solution.py:170
  34.1 8.0 %collective-permute-start.6 = (bf16[2,384,128]{2,1,0:T(8,128)(2,1)S(1)}, bf16[2,384,128]{2,1,0:T(8,128)(2,1)S(1)}, u32[]{:S(2)}, u32[]{:S(2)}) collective-permute-start(bf16[2,384,128]{2,1,0:T(8,128)(2,1)S(1)} %collective-permute-done.2.refs_1_), channel_id=1, source_target_pairs={{0,8},{8,0},{1,9},{9,1},{2,10},{10,2},{3,11},{11,3},{4,12},{12,4},... | collective-permute-start | bytes 589832 | tf_op jit(solution)/shard_map/ppermute | solution.py:170
  34.5 11.4 %collective-permute-start.8 = (bf16[2,384,128]{2,1,0:T(8,128)(2,1)S(1)}, bf16[2,384,128]{2,1,0:T(8,128)(2,1)S(1)}, u32[]{:S(2)}, u32[]{:S(2)}) collective-permute-start(bf16[2,384,128]{2,1,0:T(8,128)(2,1)S(1)} %constant_dynamic-update-slice_fusion.2.refs_3_), channel_id=1, source_target_pairs={{0,1},{1,0},{2,3},{3,2},{4,5},{5,4},{6,7},{7,6},{8,9},{9,8},{10,11... | collective-permute-start | bytes 589832 | tf_op jit(solution)/shard_map/ppermute | solution.py:170
  34.6 11.7 %collective-permute-start.9 = (bf16[2,384,128]{2,1,0:T(8,128)(2,1)S(1)}, bf16[2,384,128]{2,1,0:T(8,128)(2,1)S(1)}, u32[]{:S(2)}, u32[]{:S(2)}) collective-permute-start(bf16[2,384,128]{2,1,0:T(8,128)(2,1)S(1)} %constant_dynamic-update-slice_fusion.2.refs_3_), channel_id=1, source_target_pairs={{0,8},{8,0},{1,9},{9,1},{2,10},{10,2},{3,11},{11,3},{4,12},{12,4},... | collective-permute-start | bytes 589832 | tf_op jit(solution)/shard_map/ppermute | solution.py:170
  46.3 5.8 %collective-permute-start.14 = (bf16[2,384,128]{2,1,0:T(8,128)(2,1)S(1)}, bf16[2,384,128]{2,1,0:T(8,128)(2,1)S(1)}, u32[]{:S(2)}, u32[]{:S(2)}) collective-permute-start(bf16[2,384,128]{2,1,0:T(8,128)(2,1)S(1)} %collective-permute-done.6.refs_1_), channel_id=1, source_target_pairs={{0,16},{16,0},{1,17},{17,1},{2,18},{18,2},{3,19},{19,3},{4,20},{20... | collective-permute-start | bytes 589832 | tf_op jit(solution)/shard_map/ppermute | solution.py:170
  47.2 4.9 %collective-permute-start.15 = (bf16[2,384,128]{2,1,0:T(8,128)(2,1)S(1)}, bf16[2,384,128]{2,1,0:T(8,128)(2,1)S(1)}, u32[]{:S(2)}, u32[]{:S(2)}) collective-permute-start(bf16[2,384,128]{2,1,0:T(8,128)(2,1)S(1)} %collective-permute-done.8.refs_1_), channel_id=1, source_target_pairs={{0,16},{16,0},{1,17},{17,1},{2,18},{18,2},{3,19},{19,3},{4,20},{20... | collective-permute-start | bytes 589832 | tf_op jit(solution)/shard_map/ppermute | solution.py:170
  47.3 8.5 %collective-permute-start.13 = (bf16[2,384,128]{2,1,0:T(8,128)(2,1)S(1)}, bf16[2,384,128]{2,1,0:T(8,128)(2,1)S(1)}, u32[]{:S(2)}, u32[]{:S(2)}) collective-permute-start(bf16[2,384,128]{2,1,0:T(8,128)(2,1)S(1)} %collective-permute-done.8.refs_1_), channel_id=1, source_target_pairs={{0,8},{8,0},{1,9},{9,1},{2,10},{10,2},{3,11},{11,3},{4,12},{12,4},... | collective-permute-start | bytes 589832 | tf_op jit(solution)/shard_map/ppermute | solution.py:170
  47.7 8.5 %collective-permute-start.17 = (bf16[2,384,128]{2,1,0:T(8,128)(2,1)S(1)}, bf16[2,384,128]{2,1,0:T(8,128)(2,1)S(1)}, u32[]{:S(2)}, u32[]{:S(2)}) collective-permute-start(bf16[2,384,128]{2,1,0:T(8,128)(2,1)S(1)} %collective-permute-done.9.refs_2_), channel_id=1, source_target_pairs={{0,16},{16,0},{1,17},{17,1},{2,18},{18,2},{3,19},{19,3},{4,20},{20... | collective-permute-start | bytes 589832 | tf_op jit(solution)/shard_map/ppermute | solution.py:170
  55.8 4.0 %collective-permute-start.16 = (bf16[2,384,128]{2,1,0:T(8,128)(2,1)S(1)}, bf16[2,384,128]{2,1,0:T(8,128)(2,1)S(1)}, u32[]{:S(2)}, u32[]{:S(2)}) collective-permute-start(bf16[2,384,128]{2,1,0:T(8,128)(2,1)S(1)} %collective-permute-done.13.refs_2_), channel_id=1, source_target_pairs={{0,16},{16,0},{1,17},{17,1},{2,18},{18,2},{3,19},{19,3},{4,20},{20... | collective-permute-start | bytes 589832 | tf_op jit(solution)/shard_map/ppermute | solution.py:170
  62.8 13.6 %copy-start = (f32[256,128]{1,0:T(8,128)S(1)}, f32[256,128]{1,0:T(8,128)}, u32[]{:S(2)}) copy-start(f32[256,128]{1,0:T(8,128)} %dir_ref.3) | copy-start | bytes 393220
  62.8 13.6 %copy-start.1 = (f32[256,128]{1,0:T(8,128)S(1)}, f32[256,128]{1,0:T(8,128)}, u32[]{:S(2)}) copy-start(f32[256,128]{1,0:T(8,128)} %res_ref.3) | copy-start | bytes 393220
  62.8 13.6 %all-to-all-start.1 = ((bf16[8,256,128]{2,1,0:T(8,128)(2,1)}), bf16[8,256,128]{2,1,0:T(8,128)(2,1)S(1)}, u32[]{:S(2)}, u32[]{:S(2)}) async-start(bf16[8,256,128]{2,1,0:T(8,128)(2,1)} %bitcast.3), calls=%async_computation.1 | async-start | bytes 1048576 | tf_op jit(solution)/shard_map/all_to_all | solution.py:247
  76.6 26.1 %copy-start.3 = (f32[256,128]{1,0:T(8,128)S(1)}, f32[256,128]{1,0:T(8,128)}, u32[]{:S(2)}) copy-start(f32[256,128]{1,0:T(8,128)} %sol_ref.1) | copy-start | bytes 393220

commit v7 on v6

--- a/solution.py
+++ b/solution.py
@@ -76,15 +76,14 @@
         sum_ref, refs = refs[0], refs[1:]
     out_ref, cols_ref, dirs_ref, ahead_ref, *refs = refs
     acc_ref = refs[0] if refs else out_ref
-    pieces = bundles[0].shape[0]
-    total = n_bundles * pieces
+    pieces = [(bundle, j) for bundle in bundles for j in range(bundle.shape[0])]
+    total = len(pieces)
     lane = lax.broadcasted_iota(jnp.int32, (1, 128), 1)
     first = jnp.where(lane < 64, 1.0, 0.0).astype(jnp.bfloat16)
     second = jnp.where(lane < 64, 0.0, 1.0).astype(jnp.bfloat16)
-    for n in range(total):
-        bundle = bundles[n // pieces]
-        dirs_ref[n] = bundle[n % pieces, :256, :]
-        both = bundle[n % pieces, 256:, :]
+    for n, (bundle, j) in enumerate(pieces):
+        dirs_ref[n] = bundle[j, :256, :]
+        both = bundle[j, 256:, :]
         cols_ref[n, :128, :] = both * first
         cols_ref[n, 128:, :] = both * second
     if not has_sum:
@@ -119,10 +118,9 @@
 
 
 def tiles(rows, bundles, so_far, last=False):
-    pieces = bundles[0].shape[0]
-    n = len(bundles) * pieces
+    n = sum(bundle.shape[0] for bundle in bundles)
     count = rows.shape[0]
-    tile = count if n > 4 else count // 2
+    tile = count if n > 4 and n % 2 == 0 else count // 2
     args = (rows, *bundles) + (() if so_far is None else (so_far,))
     whole = pl.BlockSpec(memory_space=pltpu.VMEM)
     return pl.pallas_call(
@@ -216,14 +214,14 @@
         compiler_params=VMEM,
     )(lax.all_to_all(row, ROWS, 0, 0, tiled=True)).reshape(n_rows * 256, 128)
 
-    zm, rows = after(zm, rows)
+    so_far = tiles(rows, [own, own_core], None)
+
+    zm, so_far = after(zm, so_far)
     a = jnp.concatenate([own, zm], axis=0)
     zm_core, a_zl, a_yh = core(zm), turned(a, "zl", 1), turned(a, "yh", 1)
-    mirror, rows = after(mirror, rows)
+    mirror, so_far = after(mirror, so_far)
     mirror_zm = turned(mirror, "zm", 1)
-    so_far = tiles(rows, [own, own_core], None)
-
-    so_far = tiles(rows, [zm, zm_core], so_far)
+    so_far = tiles(rows, [zm, zm_core, mirror], so_far)
 
     (a_zl, a_yh), so_far = after((a_zl, a_yh), so_far)
     a_zl_core, a_yh_core, a_zl_yh = core(a_zl), core(a_yh), turned(a_zl, "yh", 1)
@@ -232,7 +230,7 @@
     mirror_zm, so_far = after(mirror_zm, so_far)
     b = jnp.concatenate([mirror, mirror_zm], axis=0)
     b_core, b_zl, b_yh = core(b), turned(b, "zl", 1), turned(b, "yh", 1)
-    so_far = tiles(rows, [a_zl_core, a_yh_core, b], so_far)
+    so_far = tiles(rows, [a_zl_core, a_yh_core, mirror_zm], so_far)
     so_far = tiles(rows, [a_zl_yh, b_core], so_far)
 
     (a_zl_yh, b_zl, b_yh), so_far = after((a_zl_yh, b_zl, b_yh), so_far)

time: 104 us -> 104 us (level)
  blocking collectives: 26.1 us -> 24.6 us
  starting transfers between devices: 33.4 us -> 34.5 us
    all_to_all x2, blocking collectives: 26.1 us -> 24.6 us  [from_all(): lax.all_to_all(jnp.broadcast_to(x[None], (count,) + x.shape), axes, 0, 0,...]
  transfers between devices with their start and end apart: 20 -> 20, of which waited for: 2 -> 3; matrix products, arithmetic and copies ran while one was open for 0% -> 0% of each run, Pallas kernels for 27% -> 27%
where the time goes in v7:
time: 104 us
  starting transfers between devices  34.5 us (33%)
  Pallas kernels  33.8 us (32%)
  blocking collectives  24.6 us (24%)
  waiting for transfers between devices  9.18 us (9%)
  between operations  1.53 us (1%)
    pallas_call x9, Pallas kernels, tiles(): pl.pallas_call(functools.partial(tiles_kernel, len(bundles), so_far is no...  30.9 us
    all_to_all x2, blocking collectives, from_all(): lax.all_to_all(jnp.broadcast_to(x[None], (count,) + x.shape), axes, 0, 0,...  24.6 us
    ppermute x17, starting transfers between devices, turned(): return lax.ppermute(x, axis, [(i, (i + by) % count) for i in range(count)])  19.9 us
    all_to_all x1, waiting for transfers between devices, on_device(): lax.all_to_all(so_far.reshape(n_rows, 256, 128), ROWS, 0, 0, tiled=True)  8.43 us
    all_to_all x1, starting transfers between devices, on_device(): lax.all_to_all(row, ROWS, 0, 0, tiled=True)  6.01 us
    all_to_all x1, starting transfers between devices, on_device(): lax.all_to_all(so_far.reshape(n_rows, 256, 128), ROWS, 0, 0, tiled=True)  4.87 us
    ppermute x1, starting transfers between devices, mirrored(): return lax.ppermute(x, axes, [(i, count - 1 - i) for i in range(count)])  3.76 us
  transfers between devices with their start and end apart: 20, of which 3 were waited for; matrix products, arithmetic and copies ran while one was open for 0% of the time, Pallas kernels for 27%

profile of v7, /device:TPU:1, one launch (start us, length us, event | category | flops | bytes accessed | tf_op | source)
XLA Modules:
  0.0 103.8 jit_solution(8851485366155014981)
XLA Ops:
  0.6 1.9 %shard_map.85 = (bf16[8,128,128]{2,1,0:T(8,128)(2,1)}, bf16[1,384,128]{2,1,0:T(8,128)(2,1)}) custom-call(bf16[32,256]{1,0:T(8,128)(2,1)} %bitcast.15, f32[1,32]{1,0:T(1,128)} %bitcast.16, f32[256,128]{1,0:T(8,128)} %dir_ref.3), custom_call_target="tpu_custom_call" | custom-call | tf_op jit(solution)/shard_map/pallas_call | solution.py:192
  2.5 0.0 copy-start.2
  2.5 6.0 %all-to-all-start = ((bf16[8,128,128]{2,1,0:T(8,128)(2,1)}), bf16[8,128,128]{2,1,0:T(8,128)(2,1)S(1)}, u32[]{:S(2)}, u32[]{:S(2)}) async-start(bf16[8,128,128]{2,1,0:T(8,128)(2,1)} %get-tuple-element.22), calls=%async_computation | async-start | bytes 524288 | tf_op jit(solution)/shard_map/all_to_all | solution.py:215
  8.5 0.0 copy-done.2
  8.6 1.0 %collective-permute-start.1 = (bf16[1,384,128]{2,1,0:T(8,128)(2,1)S(1)}, bf16[1,384,128]{2,1,0:T(8,128)(2,1)S(1)}, u32[]{:S(2)}, u32[]{:S(2)}) collective-permute-start(bf16[1,384,128]{2,1,0:T(8,128)(2,1)S(1)} %copy-done.2), channel_id=1, source_target_pairs={{0,16},{16,0},{1,17},{17,1},{2,18},{18,2},{3,19},{19,3},{4,20},{20... | collective-permute-start | bytes 294920 | tf_op jit(solution)/shard_map/ppermute | solution.py:168
  9.6 3.0 %collective-permute-start = (bf16[1,384,128]{2,1,0:T(8,128)(2,1)S(1)}, bf16[1,384,128]{2,1,0:T(8,128)(2,1)S(1)}, u32[]{:S(2)}, u32[]{:S(2)}) collective-permute-start(bf16[1,384,128]{2,1,0:T(8,128)(2,1)S(1)} %copy-done.2), channel_id=1, source_target_pairs={{0,2},{2,0},{1,3},{3,1},{4,6},{6,4},{5,7},{7,5},{8,10},{10,8},{9,1... | collective-permute-start | bytes 294920 | tf_op jit(solution)/shard_map/ppermute | solution.py:168
  12.6 3.8 %collective-permute-start.5 = (bf16[1,384,128]{2,1,0:T(8,128)(2,1)S(1)}, bf16[1,384,128]{2,1,0:T(8,128)(2,1)S(1)}, u32[]{:S(2)}, u32[]{:S(2)}) collective-permute-start(bf16[1,384,128]{2,1,0:T(8,128)(2,1)S(1)} %copy-done.2), channel_id=1, source_target_pairs={{0,7},{1,6},{2,5},{3,4},{4,3},{5,2},{6,1},{7,0},{8,15},{9,14},{10,... | collective-permute-start | bytes 294920 | tf_op jit(solution)/shard_map/ppermute | solution.py:173
  16.4 0.0 all-to-all-done.x_ref
  16.4 0.1 shard_map.86
  16.5 0.0 collective-permute-done.1.refs_2_
  16.5 2.1 %shard_map.87.refs_4_ = f32[2048,128]{1,0:T(8,128)S(1)} custom-call(bf16[2048,128]{1,0:T(8,128)(2,1)S(1)} %bitcast.6, bf16[1,384,128]{2,1,0:T(8,128)(2,1)S(1)} %copy-done.2, bf16[1,384,128]{2,1,0:T(8,128)(2,1)S(1)} %collective-permute-done.1.refs_2_), custom_call_target="tpu_custom_call" | custom-call | flops 268435456 | tf_op jit(solution)/shard_map/pallas_call | solution.py:126
  18.6 0.0 collective-permute-done.refs_1_
  18.6 1.7 %collective-permute-start.2 = (bf16[2,384,128]{2,1,0:T(8,128)(2,1)S(1)}, bf16[2,384,128]{2,1,0:T(8,128)(2,1)S(1)}, u32[]{:S(2)}, u32[]{:S(2)}) collective-permute-start(bf16[2,384,128]{2,1,0:T(8,128)(2,1)S(1)} %constant_dynamic-update-slice_fusion), channel_id=1, source_target_pairs={{0,1},{1,0},{2,3},{3,2},{4,5},{5,4},{6,7},{7,6},{8,9},{9,8},{10,11... | collective-permute-start | bytes 589832 | tf_op jit(solution)/shard_map/ppermute | solution.py:168
  20.4 2.6 %collective-permute-start.3 = (bf16[2,384,128]{2,1,0:T(8,128)(2,1)S(1)}, bf16[2,384,128]{2,1,0:T(8,128)(2,1)S(1)}, u32[]{:S(2)}, u32[]{:S(2)}) collective-permute-start(bf16[2,384,128]{2,1,0:T(8,128)(2,1)S(1)} %constant_dynamic-update-slice_fusion), channel_id=1, source_target_pairs={{0,8},{8,0},{1,9},{9,1},{2,10},{10,2},{3,11},{11,3},{4,12},{12,4},... | collective-permute-start | bytes 589832 | tf_op jit(solution)/shard_map/ppermute | solution.py:168
  23.0 1.2 %collective-permute-start.4 = (bf16[1,384,128]{2,1,0:T(8,128)(2,1)S(1)}, bf16[1,384,128]{2,1,0:T(8,128)(2,1)S(1)}, u32[]{:S(2)}, u32[]{:S(2)}) collective-permute-start(bf16[1,384,128]{2,1,0:T(8,128)(2,1)S(1)} %collective-permute-done.refs_1_), channel_id=1, source_target_pairs={{0,16},{16,0},{1,17},{17,1},{2,18},{18,2},{3,19},{19,3},{4,20},{20... | collective-permute-start | bytes 294920 | tf_op jit(solution)/shard_map/ppermute | solution.py:168
  24.2 0.0 collective-permute-done.5.refs_3_
  24.2 2.7 %collective-permute-start.7 = (bf16[1,384,128]{2,1,0:T(8,128)(2,1)S(1)}, bf16[1,384,128]{2,1,0:T(8,128)(2,1)S(1)}, u32[]{:S(2)}, u32[]{:S(2)}) collective-permute-start(bf16[1,384,128]{2,1,0:T(8,128)(2,1)S(1)} %collective-permute-done.5.refs_3_), channel_id=1, source_target_pairs={{0,2},{2,0},{1,3},{3,1},{4,6},{6,4},{5,7},{7,5},{8,10},{10,8},{9,1... | collective-permute-start | bytes 294920 | tf_op jit(solution)/shard_map/ppermute | solution.py:168
  26.9 0.0 collective-permute-done.4.refs_2_
  26.9 2.9 %shard_map.88.refs_3_ = f32[2048,128]{1,0:T(8,128)S(1)} custom-call(bf16[2048,128]{1,0:T(8,128)(2,1)S(1)} %bitcast.7, bf16[1,384,128]{2,1,0:T(8,128)(2,1)S(1)} %collective-permute-done.refs_1_, bf16[1,384,128]{2,1,0:T(8,128)(2,1)S(1)} %collective-permute-done.4.refs_2_, ...), custom_call_target="tpu_custom_call", output_to_operand_aliasing={{}: (4, {})} | custom-call | flops 402653184 | tf_op jit(solution)/shard_map/pallas_call | solution.py:126
  29.8 0.0 collective-permute-done.2.refs_1_
  29.8 0.0 collective-permute-done.3.refs_2_
  29.8 0.4 collective-permute-start.11
  30.1 0.2 collective-permute-start.12
  30.4 3.7 %shard_map.89.refs_4_ = f32[2048,128]{1,0:T(8,128)S(1)} custom-call(bf16[2048,128]{1,0:T(8,128)(2,1)S(1)} %bitcast.8, bf16[2,384,128]{2,1,0:T(8,128)(2,1)S(1)} %collective-permute-done.2.refs_1_, bf16[2,384,128]{2,1,0:T(8,128)(2,1)S(1)} %collective-permute-done.3.refs_2_, f32[2048,128]{1,0:T(8,128)S(1)} %shard_map.88.refs_3_), custom_call_target="tpu_custom_call", output_to_operand_aliasing={{}: (3, {})} | custom-call | flops 536870912 | tf_op jit(solution)/shard_map/pallas_call | solution.py:126
  34.1 0.0 collective-permute-done.7.refs_3_
  34.1 0.4 collective-permute-start.10
  34.5 1.7 %collective-permute-start.6 = (bf16[2,384,128]{2,1,0:T(8,128)(2,1)S(1)}, bf16[2,384,128]{2,1,0:T(8,128)(2,1)S(1)}, u32[]{:S(2)}, u32[]{:S(2)}) collective-permute-start(bf16[2,384,128]{2,1,0:T(8,128)(2,1)S(1)} %collective-permute-done.2.refs_1_), channel_id=1, source_target_pairs={{0,8},{8,0},{1,9},{9,1},{2,10},{10,2},{3,11},{11,3},{4,12},{12,4},... | collective-permute-start | bytes 589832 | tf_op jit(solution)/shard_map/ppermute | solution.py:168
  36.1 0.1 collective-permute-start.8
  36.2 0.0 collective-permute-done.11.refs_1_
  36.2 1.2 %collective-permute-start.9 = (bf16[2,384,128]{2,1,0:T(8,128)(2,1)S(1)}, bf16[2,384,128]{2,1,0:T(8,128)(2,1)S(1)}, u32[]{:S(2)}, u32[]{:S(2)}) collective-permute-start(bf16[2,384,128]{2,1,0:T(8,128)(2,1)S(1)} %constant_dynamic-update-slice_fusion.2), channel_id=1, source_target_pairs={{0,8},{8,0},{1,9},{9,1},{2,10},{10,2},{3,11},{11,3},{4,12},{12,4},... | collective-permute-start | bytes 589832 | tf_op jit(solution)/shard_map/ppermute | solution.py:168
  37.4 0.0 collective-permute-done.12.refs_2_
  37.4 4.6 %shard_map.90.refs_3_ = f32[2048,128]{1,0:T(8,128)S(1)} custom-call(bf16[2048,128]{1,0:T(8,128)(2,1)S(1)} %bitcast.9, bf16[2,384,128]{2,1,0:T(8,128)(2,1)S(1)} %collective-permute-done.11.refs_1_, bf16[2,384,128]{2,1,0:T(8,128)(2,1)S(1)} %collective-permute-done.12.refs_2_, ...), custom_call_target="tpu_custom_call", output_to_operand_aliasing={{}: (4, {})} | custom-call | flops 671088640 | tf_op jit(solution)/shard_map/pallas_call | solution.py:126
  42.0 0.0 collective-permute-done.10.refs_2_
  42.0 0.2 collective-permute-done.6.refs_1_
  42.2 3.7 %shard_map.91.refs_3_ = f32[2048,128]{1,0:T(8,128)S(1)} custom-call(bf16[2048,128]{1,0:T(8,128)(2,1)S(1)} %bitcast.10, bf16[2,384,128]{2,1,0:T(8,128)(2,1)S(1)} %collective-permute-done.6.refs_1_, bf16[2,384,128]{2,1,0:T(8,128)(2,1)S(1)} %collective-permute-done.10.refs_2_, f32[2048,128]{1,0:T(8,128)S(1)} %shard_map.90.refs_3_), custom_call_target="tpu_custom_call", output_to_operand_aliasing={{}: (3, {})} | custom-call | flops 536870912 | tf_op jit(solution)/shard_map/pallas_call | solution.py:126
  45.9 0.0 collective-permute-done.8.refs_1_
  45.9 0.5 collective-permute-done.9.refs_2_
  46.4 1.3 %collective-permute-start.14 = (bf16[2,384,128]{2,1,0:T(8,128)(2,1)S(1)}, bf16[2,384,128]{2,1,0:T(8,128)(2,1)S(1)}, u32[]{:S(2)}, u32[]{:S(2)}) collective-permute-start(bf16[2,384,128]{2,1,0:T(8,128)(2,1)S(1)} %collective-permute-done.6.refs_1_), channel_id=1, source_target_pairs={{0,16},{16,0},{1,17},{17,1},{2,18},{18,2},{3,19},{19,3},{4,20},{20... | collective-permute-start | bytes 589832 | tf_op jit(solution)/shard_map/ppermute | solution.py:168
  47.7 0.1 collective-permute-start.15
  47.8 1.5 %collective-permute-start.13 = (bf16[2,384,128]{2,1,0:T(8,128)(2,1)S(1)}, bf16[2,384,128]{2,1,0:T(8,128)(2,1)S(1)}, u32[]{:S(2)}, u32[]{:S(2)}) collective-permute-start(bf16[2,384,128]{2,1,0:T(8,128)(2,1)S(1)} %collective-permute-done.8.refs_1_), channel_id=1, source_target_pairs={{0,8},{8,0},{1,9},{9,1},{2,10},{10,2},{3,11},{11,3},{4,12},{12,4},... | collective-permute-start | bytes 589832 | tf_op jit(solution)/shard_map/ppermute | solution.py:168
  49.3 0.7 collective-permute-start.17
  50.0 3.7 %shard_map.92.refs_3_ = f32[2048,128]{1,0:T(8,128)S(1)} custom-call(bf16[2048,128]{1,0:T(8,128)(2,1)S(1)} %bitcast.11, bf16[2,384,128]{2,1,0:T(8,128)(2,1)S(1)} %collective-permute-done.8.refs_1_, bf16[2,384,128]{2,1,0:T(8,128)(2,1)S(1)} %collective-permute-done.9.refs_2_, f32[2048,128]{1,0:T(8,128)S(1)} %shard_map.91.refs_3_), custom_call_target="tpu_custom_call", output_to_operand_aliasing={{}: (3, {})} | custom-call | flops 536870912 | tf_op jit(solution)/shard_map/pallas_call | solution.py:126
  53.7 0.0 collective-permute-done.14.refs_1_
  53.8 0.0 collective-permute-done.15.refs_2_
  53.8 3.7 %shard_map.93.refs_3_ = f32[2048,128]{1,0:T(8,128)S(1)} custom-call(bf16[2048,128]{1,0:T(8,128)(2,1)S(1)} %bitcast.12, bf16[2,384,128]{2,1,0:T(8,128)(2,1)S(1)} %collective-permute-done.14.refs_1_, bf16[2,384,128]{2,1,0:T(8,128)(2,1)S(1)} %collective-permute-done.15.refs_2_, f32[2048,128]{1,0:T(8,128)S(1)} %shard_map.92.refs_3_), custom_call_target="tpu_custom_call", output_to_operand_aliasing={{}: (3, {})} | custom-call | flops 536870912 | tf_op jit(solution)/shard_map/pallas_call | solution.py:126
  57.5 0.0 collective-permute-done.13.refs_2_
  57.5 0.1 collective-permute-start.16
  57.6 0.0 collective-permute-done.17.refs_1_
  57.6 3.7 %shard_map.94.refs_2_ = f32[2048,128]{1,0:T(8,128)S(1)} custom-call(bf16[2048,128]{1,0:T(8,128)(2,1)S(1)} %bitcast.13, bf16[2,384,128]{2,1,0:T(8,128)(2,1)S(1)} %collective-permute-done.17.refs_1_, bf16[2,384,128]{2,1,0:T(8,128)(2,1)S(1)} %collective-permute-done.13.refs_2_, f32[2048,128]{1,0:T(8,128)S(1)} %shard_map.93.refs_3_), custom_call_target="tpu_custom_call", output_to_operand_aliasing={{}: (3, {})} | custom-call | flops 536870912 | tf_op jit(solution)/shard_map/pallas_call | solution.py:126
  61.3 0.0 collective-permute-done.16.refs_1_
  61.3 2.9 %shard_map.95 = bf16[2048,128]{1,0:T(8,128)(2,1)} custom-call(bf16[2048,128]{1,0:T(8,128)(2,1)S(1)} %bitcast.14, bf16[2,384,128]{2,1,0:T(8,128)(2,1)S(1)} %collective-permute-done.16.refs_1_, f32[2048,128]{1,0:T(8,128)S(1)} %shard_map.94.refs_2_), custom_call_target="tpu_custom_call" | custom-call | flops 268435456 | tf_op jit(solution)/shard_map/pallas_call | solution.py:126
  64.2 0.0 copy-start
  64.2 0.0 copy-start.1
  64.2 4.9 %all-to-all-start.1 = ((bf16[8,256,128]{2,1,0:T(8,128)(2,1)}), bf16[8,256,128]{2,1,0:T(8,128)(2,1)S(1)}, u32[]{:S(2)}, u32[]{:S(2)}) async-start(bf16[8,256,128]{2,1,0:T(8,128)(2,1)} %bitcast.3), calls=%async_computation.1 | async-start | bytes 1048576 | tf_op jit(solution)/shard_map/all_to_all | solution.py:245
  69.8 8.4 %all-to-all-done.1.parts_ref = bf16[8,256,128]{2,1,0:T(8,128)(2,1)S(1)} async-done(((bf16[8,256,128]{2,1,0:T(8,128)(2,1)}), bf16[8,256,128]{2,1,0:T(8,128)(2,1)S(1)}, u32[]{:S(2)}, u32[]{:S(2)}) %all-to-all-start.1) | async-done | bytes 524320 | tf_op jit(solution)/shard_map/all_to_all | solution.py:245
  78.2 0.0 copy-done
  78.2 0.0 copy-done.1
  78.2 0.1 shard_map.96
  78.3 0.0 copy-start.3
  78.4 12.6 %all_to_all.20 = f32[32,4,128]{2,1,0:T(4,128)S(1)} all-to-all(f32[32,4,128]{2,1,0:T(4,128)S(1)} %broadcast_in_dim.4), channel_id=1, replica_groups=mesh['xh'=2,'xl'=2,'yl'=2,'c'=2,'yh'=2,'zh'=2,'zm'=2,'zl'=2] {'xh','xl',..., dimensions={0} | all-to-all | bytes 131072 | tf_op jit(solution)/shard_map/all_to_all | solution.py:178
  91.0 12.0 %all_to_all.21.sums_ref = f32[8,4,128]{2,1,0:T(4,128)S(1)} all-to-all(f32[8,4,128]{2,1,0:T(4,128)S(1)} %broadcast_in_dim.5), channel_id=1, replica_groups=mesh['xh'=2,'xl'=2,'yl'=2,'c'=2,'yh'=2,'zh'=2,'zm'=2,'zl'=2] {'zh','zm',..., dimensions={0} | all-to-all | bytes 32768 | tf_op jit(solution)/shard_map/all_to_all | solution.py:178
  103.0 0.0 copy-done.3
  103.0 0.8 shard_map.97
  (7 shorter events, 0.1 us)
Async XLA Ops:
  2.5 6.0 %copy-start.2 = (bf16[1,384,128]{2,1,0:T(8,128)(2,1)S(1)}, bf16[1,384,128]{2,1,0:T(8,128)(2,1)}, u32[]{:S(2)}) copy-start(bf16[1,384,128]{2,1,0:T(8,128)(2,1)} %get-tuple-element.23.refs_1_) | copy-start | bytes 294916
  2.5 13.8 %all-to-all-start = ((bf16[8,128,128]{2,1,0:T(8,128)(2,1)}), bf16[8,128,128]{2,1,0:T(8,128)(2,1)S(1)}, u32[]{:S(2)}, u32[]{:S(2)}) async-start(bf16[8,128,128]{2,1,0:T(8,128)(2,1)} %get-tuple-element.22), calls=%async_computation | async-start | bytes 524288 | tf_op jit(solution)/shard_map/all_to_all | solution.py:215
  8.6 8.0 %collective-permute-start.1 = (bf16[1,384,128]{2,1,0:T(8,128)(2,1)S(1)}, bf16[1,384,128]{2,1,0:T(8,128)(2,1)S(1)}, u32[]{:S(2)}, u32[]{:S(2)}) collective-permute-start(bf16[1,384,128]{2,1,0:T(8,128)(2,1)S(1)} %copy-done.2), channel_id=1, source_target_pairs={{0,16},{16,0},{1,17},{17,1},{2,18},{18,2},{3,19},{19,3},{4,20},{20... | collective-permute-start | bytes 294920 | tf_op jit(solution)/shard_map/ppermute | solution.py:168
  9.6 9.0 %collective-permute-start = (bf16[1,384,128]{2,1,0:T(8,128)(2,1)S(1)}, bf16[1,384,128]{2,1,0:T(8,128)(2,1)S(1)}, u32[]{:S(2)}, u32[]{:S(2)}) collective-permute-start(bf16[1,384,128]{2,1,0:T(8,128)(2,1)S(1)} %copy-done.2), channel_id=1, source_target_pairs={{0,2},{2,0},{1,3},{3,1},{4,6},{6,4},{5,7},{7,5},{8,10},{10,8},{9,1... | collective-permute-start | bytes 294920 | tf_op jit(solution)/shard_map/ppermute | solution.py:168
  12.6 11.6 %collective-permute-start.5 = (bf16[1,384,128]{2,1,0:T(8,128)(2,1)S(1)}, bf16[1,384,128]{2,1,0:T(8,128)(2,1)S(1)}, u32[]{:S(2)}, u32[]{:S(2)}) collective-permute-start(bf16[1,384,128]{2,1,0:T(8,128)(2,1)S(1)} %copy-done.2), channel_id=1, source_target_pairs={{0,7},{1,6},{2,5},{3,4},{4,3},{5,2},{6,1},{7,0},{8,15},{9,14},{10,... | collective-permute-start | bytes 294920 | tf_op jit(solution)/shard_map/ppermute | solution.py:173
  18.6 11.1 %collective-permute-start.2 = (bf16[2,384,128]{2,1,0:T(8,128)(2,1)S(1)}, bf16[2,384,128]{2,1,0:T(8,128)(2,1)S(1)}, u32[]{:S(2)}, u32[]{:S(2)}) collective-permute-start(bf16[2,384,128]{2,1,0:T(8,128)(2,1)S(1)} %constant_dynamic-update-slice_fusion), channel_id=1, source_target_pairs={{0,1},{1,0},{2,3},{3,2},{4,5},{5,4},{6,7},{7,6},{8,9},{9,8},{10,11... | collective-permute-start | bytes 589832 | tf_op jit(solution)/shard_map/ppermute | solution.py:168
  20.4 9.4 %collective-permute-start.3 = (bf16[2,384,128]{2,1,0:T(8,128)(2,1)S(1)}, bf16[2,384,128]{2,1,0:T(8,128)(2,1)S(1)}, u32[]{:S(2)}, u32[]{:S(2)}) collective-permute-start(bf16[2,384,128]{2,1,0:T(8,128)(2,1)S(1)} %constant_dynamic-update-slice_fusion), channel_id=1, source_target_pairs={{0,8},{8,0},{1,9},{9,1},{2,10},{10,2},{3,11},{11,3},{4,12},{12,4},... | collective-permute-start | bytes 589832 | tf_op jit(solution)/shard_map/ppermute | solution.py:168
  23.0 3.9 %collective-permute-start.4 = (bf16[1,384,128]{2,1,0:T(8,128)(2,1)S(1)}, bf16[1,384,128]{2,1,0:T(8,128)(2,1)S(1)}, u32[]{:S(2)}, u32[]{:S(2)}) collective-permute-start(bf16[1,384,128]{2,1,0:T(8,128)(2,1)S(1)} %collective-permute-done.refs_1_), channel_id=1, source_target_pairs={{0,16},{16,0},{1,17},{17,1},{2,18},{18,2},{3,19},{19,3},{4,20},{20... | collective-permute-start | bytes 294920 | tf_op jit(solution)/shard_map/ppermute | solution.py:168
  24.2 9.9 %collective-permute-start.7 = (bf16[1,384,128]{2,1,0:T(8,128)(2,1)S(1)}, bf16[1,384,128]{2,1,0:T(8,128)(2,1)S(1)}, u32[]{:S(2)}, u32[]{:S(2)}) collective-permute-start(bf16[1,384,128]{2,1,0:T(8,128)(2,1)S(1)} %collective-permute-done.5.refs_3_), channel_id=1, source_target_pairs={{0,2},{2,0},{1,3},{3,1},{4,6},{6,4},{5,7},{7,5},{8,10},{10,8},{9,1... | collective-permute-start | bytes 294920 | tf_op jit(solution)/shard_map/ppermute | solution.py:168
  29.8 6.5 %collective-permute-start.11 = (bf16[2,384,128]{2,1,0:T(8,128)(2,1)S(1)}, bf16[2,384,128]{2,1,0:T(8,128)(2,1)S(1)}, u32[]{:S(2)}, u32[]{:S(2)}) collective-permute-start(bf16[2,384,128]{2,1,0:T(8,128)(2,1)S(1)} %collective-permute-done.2.refs_1_), channel_id=1, source_target_pairs={{0,16},{16,0},{1,17},{17,1},{2,18},{18,2},{3,19},{19,3},{4,20},{20... | collective-permute-start | bytes 589832 | tf_op jit(solution)/shard_map/ppermute | solution.py:168
  30.1 7.3 %collective-permute-start.12 = (bf16[2,384,128]{2,1,0:T(8,128)(2,1)S(1)}, bf16[2,384,128]{2,1,0:T(8,128)(2,1)S(1)}, u32[]{:S(2)}, u32[]{:S(2)}) collective-permute-start(bf16[2,384,128]{2,1,0:T(8,128)(2,1)S(1)} %collective-permute-done.3.refs_2_), channel_id=1, source_target_pairs={{0,16},{16,0},{1,17},{17,1},{2,18},{18,2},{3,19},{19,3},{4,20},{20... | collective-permute-start | bytes 589832 | tf_op jit(solution)/shard_map/ppermute | solution.py:168
  34.1 7.9 %collective-permute-start.10 = (bf16[2,384,128]{2,1,0:T(8,128)(2,1)S(1)}, bf16[2,384,128]{2,1,0:T(8,128)(2,1)S(1)}, u32[]{:S(2)}, u32[]{:S(2)}) collective-permute-start(bf16[2,384,128]{2,1,0:T(8,128)(2,1)S(1)} %constant_dynamic-update-slice_fusion.2), channel_id=1, source_target_pairs={{0,16},{16,0},{1,17},{17,1},{2,18},{18,2},{3,19},{19,3},{4,20},{20... | collective-permute-start | bytes 589832 | tf_op jit(solution)/shard_map/ppermute | solution.py:168
  34.5 7.8 %collective-permute-start.6 = (bf16[2,384,128]{2,1,0:T(8,128)(2,1)S(1)}, bf16[2,384,128]{2,1,0:T(8,128)(2,1)S(1)}, u32[]{:S(2)}, u32[]{:S(2)}) collective-permute-start(bf16[2,384,128]{2,1,0:T(8,128)(2,1)S(1)} %collective-permute-done.2.refs_1_), channel_id=1, source_target_pairs={{0,8},{8,0},{1,9},{9,1},{2,10},{10,2},{3,11},{11,3},{4,12},{12,4},... | collective-permute-start | bytes 589832 | tf_op jit(solution)/shard_map/ppermute | solution.py:168
  36.1 9.8 %collective-permute-start.8 = (bf16[2,384,128]{2,1,0:T(8,128)(2,1)S(1)}, bf16[2,384,128]{2,1,0:T(8,128)(2,1)S(1)}, u32[]{:S(2)}, u32[]{:S(2)}) collective-permute-start(bf16[2,384,128]{2,1,0:T(8,128)(2,1)S(1)} %constant_dynamic-update-slice_fusion.2), channel_id=1, source_target_pairs={{0,1},{1,0},{2,3},{3,2},{4,5},{5,4},{6,7},{7,6},{8,9},{9,8},{10,11... | collective-permute-start | bytes 589832 | tf_op jit(solution)/shard_map/ppermute | solution.py:168
  36.2 10.2 %collective-permute-start.9 = (bf16[2,384,128]{2,1,0:T(8,128)(2,1)S(1)}, bf16[2,384,128]{2,1,0:T(8,128)(2,1)S(1)}, u32[]{:S(2)}, u32[]{:S(2)}) collective-permute-start(bf16[2,384,128]{2,1,0:T(8,128)(2,1)S(1)} %constant_dynamic-update-slice_fusion.2), channel_id=1, source_target_pairs={{0,8},{8,0},{1,9},{9,1},{2,10},{10,2},{3,11},{11,3},{4,12},{12,4},... | collective-permute-start | bytes 589832 | tf_op jit(solution)/shard_map/ppermute | solution.py:168
  46.4 7.3 %collective-permute-start.14 = (bf16[2,384,128]{2,1,0:T(8,128)(2,1)S(1)}, bf16[2,384,128]{2,1,0:T(8,128)(2,1)S(1)}, u32[]{:S(2)}, u32[]{:S(2)}) collective-permute-start(bf16[2,384,128]{2,1,0:T(8,128)(2,1)S(1)} %collective-permute-done.6.refs_1_), channel_id=1, source_target_pairs={{0,16},{16,0},{1,17},{17,1},{2,18},{18,2},{3,19},{19,3},{4,20},{20... | collective-permute-start | bytes 589832 | tf_op jit(solution)/shard_map/ppermute | solution.py:168
  47.7 6.0 %collective-permute-start.15 = (bf16[2,384,128]{2,1,0:T(8,128)(2,1)S(1)}, bf16[2,384,128]{2,1,0:T(8,128)(2,1)S(1)}, u32[]{:S(2)}, u32[]{:S(2)}) collective-permute-start(bf16[2,384,128]{2,1,0:T(8,128)(2,1)S(1)} %collective-permute-done.8.refs_1_), channel_id=1, source_target_pairs={{0,16},{16,0},{1,17},{17,1},{2,18},{18,2},{3,19},{19,3},{4,20},{20... | collective-permute-start | bytes 589832 | tf_op jit(solution)/shard_map/ppermute | solution.py:168
  47.8 9.6 %collective-permute-start.13 = (bf16[2,384,128]{2,1,0:T(8,128)(2,1)S(1)}, bf16[2,384,128]{2,1,0:T(8,128)(2,1)S(1)}, u32[]{:S(2)}, u32[]{:S(2)}) collective-permute-start(bf16[2,384,128]{2,1,0:T(8,128)(2,1)S(1)} %collective-permute-done.8.refs_1_), channel_id=1, source_target_pairs={{0,8},{8,0},{1,9},{9,1},{2,10},{10,2},{3,11},{11,3},{4,12},{12,4},... | collective-permute-start | bytes 589832 | tf_op jit(solution)/shard_map/ppermute | solution.py:168
  49.3 8.2 %collective-permute-start.17 = (bf16[2,384,128]{2,1,0:T(8,128)(2,1)S(1)}, bf16[2,384,128]{2,1,0:T(8,128)(2,1)S(1)}, u32[]{:S(2)}, u32[]{:S(2)}) collective-permute-start(bf16[2,384,128]{2,1,0:T(8,128)(2,1)S(1)} %collective-permute-done.9.refs_2_), channel_id=1, source_target_pairs={{0,16},{16,0},{1,17},{17,1},{2,18},{18,2},{3,19},{19,3},{4,20},{20... | collective-permute-start | bytes 589832 | tf_op jit(solution)/shard_map/ppermute | solution.py:168
  57.5 3.8 %collective-permute-start.16 = (bf16[2,384,128]{2,1,0:T(8,128)(2,1)S(1)}, bf16[2,384,128]{2,1,0:T(8,128)(2,1)S(1)}, u32[]{:S(2)}, u32[]{:S(2)}) collective-permute-start(bf16[2,384,128]{2,1,0:T(8,128)(2,1)S(1)} %collective-permute-done.13.refs_2_), channel_id=1, source_target_pairs={{0,16},{16,0},{1,17},{17,1},{2,18},{18,2},{3,19},{19,3},{4,20},{20... | collective-permute-start | bytes 589832 | tf_op jit(solution)/shard_map/ppermute | solution.py:168
  64.2 14.0 %copy-start = (f32[256,128]{1,0:T(8,128)S(1)}, f32[256,128]{1,0:T(8,128)}, u32[]{:S(2)}) copy-start(f32[256,128]{1,0:T(8,128)} %dir_ref.3) | copy-start | bytes 393220
  64.2 14.0 %copy-start.1 = (f32[256,128]{1,0:T(8,128)S(1)}, f32[256,128]{1,0:T(8,128)}, u32[]{:S(2)}) copy-start(f32[256,128]{1,0:T(8,128)} %res_ref.3) | copy-start | bytes 393220
  64.2 14.0 %all-to-all-start.1 = ((bf16[8,256,128]{2,1,0:T(8,128)(2,1)}), bf16[8,256,128]{2,1,0:T(8,128)(2,1)S(1)}, u32[]{:S(2)}, u32[]{:S(2)}) async-start(bf16[8,256,128]{2,1,0:T(8,128)(2,1)} %bitcast.3), calls=%async_computation.1 | async-start | bytes 1048576 | tf_op jit(solution)/shard_map/all_to_all | solution.py:245
  78.3 24.7 %copy-start.3 = (f32[256,128]{1,0:T(8,128)S(1)}, f32[256,128]{1,0:T(8,128)}, u32[]{:S(2)}) copy-start(f32[256,128]{1,0:T(8,128)} %sol_ref.1) | copy-start | bytes 393220

commit v8 on v7

--- a/solution.py
+++ b/solution.py
@@ -88,39 +88,48 @@
         cols_ref[n, 128:, :] = both * second
     if not has_sum:
         acc_ref[...] = jnp.zeros_like(acc_ref)
-    elif refs:
-        acc_ref[...] = sum_ref[...]
 
     per_piece = rows_ref.shape[0] // tile
 
     def at(k):
-        return pl.ds(pl.multiple_of((k % per_piece) * tile, tile), tile)
+        start = k % per_piece * tile
+        return pl.ds(start if isinstance(k, int) else pl.multiple_of(start, tile), tile)
 
     def distances(k, slot):
         ahead_ref[slot] = lax.dot_general(
             rows_ref[at(k), :], cols_ref[k // per_piece], (((1,), (1,)), ((), ())), preferred_element_type=jnp.float32
         )
 
+    def products(k, slot):
+        return jnp.dot(matern(ahead_ref[slot]), dirs_ref[k // per_piece], preferred_element_type=jnp.float32)
+
     distances(0, 0)
+    count = total * per_piece
+    if refs:
+        for k in range(count):
+            if k + 1 < count:
+                distances(k + 1, (k + 1) % 2)
+            so_far = (sum_ref if k < per_piece else acc_ref)[at(k), :] + products(k, k % 2)
+            if k + per_piece < count:
+                acc_ref[at(k), :] = so_far
+            else:
+                out_ref[at(k), :] = so_far.astype(out_ref.dtype)
+        return
 
     def body(turn, _):
         for s in range(2):
             k = turn * 2 + s
-            distances(jnp.minimum(k + 1, total * per_piece - 1), 1 - s)
-            acc_ref[at(k), :] += jnp.dot(
-                matern(ahead_ref[s]), dirs_ref[k // per_piece], preferred_element_type=jnp.float32
-            )
+            distances(jnp.minimum(k + 1, count - 1), 1 - s)
+            acc_ref[at(k), :] += products(k, s)
         return 0
 
-    lax.fori_loop(0, total * per_piece // 2, body, 0)
-    if refs:
-        out_ref[...] = acc_ref[...].astype(out_ref.dtype)
+    lax.fori_loop(0, count // 2, body, 0)
 
 
 def tiles(rows, bundles, so_far, last=False):
     n = sum(bundle.shape[0] for bundle in bundles)
     count = rows.shape[0]
-    tile = count if n > 4 and n % 2 == 0 else count // 2
+    tile = count if n > 3 and n % 2 == 0 else count // 2
     args = (rows, *bundles) + (() if so_far is None else (so_far,))
     whole = pl.BlockSpec(memory_space=pltpu.VMEM)
     return pl.pallas_call(

time: 104 us -> 103 us (level)
  Pallas kernels: 33.8 us -> 32.4 us
    pallas_call x9, Pallas kernels: 30.9 us -> 29.4 us  [tiles(): pl.pallas_call(functools.partial(tiles_kernel, len(bundles), so_far is no...]
  transfers between devices with their start and end apart: 20 -> 20, of which waited for: 3 -> 3; matrix products, arithmetic and copies ran while one was open for 0% -> 0% of each run, Pallas kernels for 27% -> 26%
where the time goes in v8:
time: 103 us
  starting transfers between devices  34.7 us (34%)
  Pallas kernels  32.4 us (31%)
  blocking collectives  24.5 us (24%)
  waiting for transfers between devices  9.41 us (9%)
  between operations  1.5 us (1%)
    pallas_call x9, Pallas kernels, tiles(): pl.pallas_call(functools.partial(tiles_kernel, len(bundles), so_far is no...  29.4 us
    all_to_all x2, blocking collectives, from_all(): lax.all_to_all(jnp.broadcast_to(x[None], (count,) + x.shape), axes, 0, 0,...  24.5 us
    ppermute x17, starting transfers between devices, turned(): return lax.ppermute(x, axis, [(i, (i + by) % count) for i in range(count)])  20 us
    all_to_all x1, waiting for transfers between devices, on_device(): lax.all_to_all(so_far.reshape(n_rows, 256, 128), ROWS, 0, 0, tiled=True)  8.43 us
    all_to_all x1, starting transfers between devices, on_device(): lax.all_to_all(row, ROWS, 0, 0, tiled=True)  6.01 us
    all_to_all x1, starting transfers between devices, on_device(): lax.all_to_all(so_far.reshape(n_rows, 256, 128), ROWS, 0, 0, tiled=True)  4.87 us
    ppermute x1, starting transfers between devices, mirrored(): return lax.ppermute(x, axes, [(i, count - 1 - i) for i in range(count)])  3.76 us
  transfers between devices with their start and end apart: 20, of which 3 were waited for; matrix products, arithmetic and copies ran while one was open for 0% of the time, Pallas kernels for 26%

profile of v8, /device:TPU:1, one launch (start us, length us, event | category | flops | bytes accessed | tf_op | source)
XLA Modules:
  0.0 102.6 jit_solution(7716281303929000383)
XLA Ops:
  0.6 1.9 %shard_map.85 = (bf16[8,128,128]{2,1,0:T(8,128)(2,1)}, bf16[1,384,128]{2,1,0:T(8,128)(2,1)}) custom-call(bf16[32,256]{1,0:T(8,128)(2,1)} %bitcast.15, f32[1,32]{1,0:T(1,128)} %bitcast.16, f32[256,128]{1,0:T(8,128)} %dir_ref.3), custom_call_target="tpu_custom_call" | custom-call | tf_op jit(solution)/shard_map/pallas_call | solution.py:201
  2.5 0.0 copy-start.2
  2.5 6.0 %all-to-all-start = ((bf16[8,128,128]{2,1,0:T(8,128)(2,1)}), bf16[8,128,128]{2,1,0:T(8,128)(2,1)S(1)}, u32[]{:S(2)}, u32[]{:S(2)}) async-start(bf16[8,128,128]{2,1,0:T(8,128)(2,1)} %get-tuple-element.22), calls=%async_computation | async-start | bytes 524288 | tf_op jit(solution)/shard_map/all_to_all | solution.py:224
  8.5 0.0 copy-done.2
  8.6 1.0 %collective-permute-start.1 = (bf16[1,384,128]{2,1,0:T(8,128)(2,1)S(1)}, bf16[1,384,128]{2,1,0:T(8,128)(2,1)S(1)}, u32[]{:S(2)}, u32[]{:S(2)}) collective-permute-start(bf16[1,384,128]{2,1,0:T(8,128)(2,1)S(1)} %copy-done.2), channel_id=1, source_target_pairs={{0,16},{16,0},{1,17},{17,1},{2,18},{18,2},{3,19},{19,3},{4,20},{20... | collective-permute-start | bytes 294920 | tf_op jit(solution)/shard_map/ppermute | solution.py:177
  9.6 3.0 %collective-permute-start = (bf16[1,384,128]{2,1,0:T(8,128)(2,1)S(1)}, bf16[1,384,128]{2,1,0:T(8,128)(2,1)S(1)}, u32[]{:S(2)}, u32[]{:S(2)}) collective-permute-start(bf16[1,384,128]{2,1,0:T(8,128)(2,1)S(1)} %copy-done.2), channel_id=1, source_target_pairs={{0,2},{2,0},{1,3},{3,1},{4,6},{6,4},{5,7},{7,5},{8,10},{10,8},{9,1... | collective-permute-start | bytes 294920 | tf_op jit(solution)/shard_map/ppermute | solution.py:177
  12.6 3.8 %collective-permute-start.5 = (bf16[1,384,128]{2,1,0:T(8,128)(2,1)S(1)}, bf16[1,384,128]{2,1,0:T(8,128)(2,1)S(1)}, u32[]{:S(2)}, u32[]{:S(2)}) collective-permute-start(bf16[1,384,128]{2,1,0:T(8,128)(2,1)S(1)} %copy-done.2), channel_id=1, source_target_pairs={{0,7},{1,6},{2,5},{3,4},{4,3},{5,2},{6,1},{7,0},{8,15},{9,14},{10,... | collective-permute-start | bytes 294920 | tf_op jit(solution)/shard_map/ppermute | solution.py:182
  16.4 0.0 all-to-all-done.x_ref
  16.4 0.1 shard_map.86
  16.5 0.0 collective-permute-done.1.refs_2_
  16.5 2.1 %shard_map.87.refs_4_ = f32[2048,128]{1,0:T(8,128)S(1)} custom-call(bf16[2048,128]{1,0:T(8,128)(2,1)S(1)} %bitcast.6, bf16[1,384,128]{2,1,0:T(8,128)(2,1)S(1)} %copy-done.2, bf16[1,384,128]{2,1,0:T(8,128)(2,1)S(1)} %collective-permute-done.1.refs_2_), custom_call_target="tpu_custom_call" | custom-call | flops 268435456 | tf_op jit(solution)/shard_map/pallas_call | solution.py:135
  18.6 0.0 collective-permute-done.refs_1_
  18.6 1.7 %collective-permute-start.2 = (bf16[2,384,128]{2,1,0:T(8,128)(2,1)S(1)}, bf16[2,384,128]{2,1,0:T(8,128)(2,1)S(1)}, u32[]{:S(2)}, u32[]{:S(2)}) collective-permute-start(bf16[2,384,128]{2,1,0:T(8,128)(2,1)S(1)} %constant_dynamic-update-slice_fusion), channel_id=1, source_target_pairs={{0,1},{1,0},{2,3},{3,2},{4,5},{5,4},{6,7},{7,6},{8,9},{9,8},{10,11... | collective-permute-start | bytes 589832 | tf_op jit(solution)/shard_map/ppermute | solution.py:177
  20.4 2.6 %collective-permute-start.3 = (bf16[2,384,128]{2,1,0:T(8,128)(2,1)S(1)}, bf16[2,384,128]{2,1,0:T(8,128)(2,1)S(1)}, u32[]{:S(2)}, u32[]{:S(2)}) collective-permute-start(bf16[2,384,128]{2,1,0:T(8,128)(2,1)S(1)} %constant_dynamic-update-slice_fusion), channel_id=1, source_target_pairs={{0,8},{8,0},{1,9},{9,1},{2,10},{10,2},{3,11},{11,3},{4,12},{12,4},... | collective-permute-start | bytes 589832 | tf_op jit(solution)/shard_map/ppermute | solution.py:177
  23.0 1.2 %collective-permute-start.4 = (bf16[1,384,128]{2,1,0:T(8,128)(2,1)S(1)}, bf16[1,384,128]{2,1,0:T(8,128)(2,1)S(1)}, u32[]{:S(2)}, u32[]{:S(2)}) collective-permute-start(bf16[1,384,128]{2,1,0:T(8,128)(2,1)S(1)} %collective-permute-done.refs_1_), channel_id=1, source_target_pairs={{0,16},{16,0},{1,17},{17,1},{2,18},{18,2},{3,19},{19,3},{4,20},{20... | collective-permute-start | bytes 294920 | tf_op jit(solution)/shard_map/ppermute | solution.py:177
  24.2 0.0 collective-permute-done.5.refs_3_
  24.2 2.7 %collective-permute-start.7 = (bf16[1,384,128]{2,1,0:T(8,128)(2,1)S(1)}, bf16[1,384,128]{2,1,0:T(8,128)(2,1)S(1)}, u32[]{:S(2)}, u32[]{:S(2)}) collective-permute-start(bf16[1,384,128]{2,1,0:T(8,128)(2,1)S(1)} %collective-permute-done.5.refs_3_), channel_id=1, source_target_pairs={{0,2},{2,0},{1,3},{3,1},{4,6},{6,4},{5,7},{7,5},{8,10},{10,8},{9,1... | collective-permute-start | bytes 294920 | tf_op jit(solution)/shard_map/ppermute | solution.py:177
  26.9 0.0 collective-permute-done.4.refs_2_
  26.9 2.9 %shard_map.88.refs_3_ = f32[2048,128]{1,0:T(8,128)S(1)} custom-call(bf16[2048,128]{1,0:T(8,128)(2,1)S(1)} %bitcast.7, bf16[1,384,128]{2,1,0:T(8,128)(2,1)S(1)} %collective-permute-done.refs_1_, bf16[1,384,128]{2,1,0:T(8,128)(2,1)S(1)} %collective-permute-done.4.refs_2_, ...), custom_call_target="tpu_custom_call", output_to_operand_aliasing={{}: (4, {})} | custom-call | flops 402653184 | tf_op jit(solution)/shard_map/pallas_call | solution.py:135
  29.8 0.0 collective-permute-done.2.refs_1_
  29.8 0.0 collective-permute-done.3.refs_2_
  29.8 0.4 collective-permute-start.11
  30.1 0.2 collective-permute-start.12
  30.4 3.5 %shard_map.89.refs_4_ = f32[2048,128]{1,0:T(8,128)S(1)} custom-call(bf16[2048,128]{1,0:T(8,128)(2,1)S(1)} %bitcast.8, bf16[2,384,128]{2,1,0:T(8,128)(2,1)S(1)} %collective-permute-done.2.refs_1_, bf16[2,384,128]{2,1,0:T(8,128)(2,1)S(1)} %collective-permute-done.3.refs_2_, f32[2048,128]{1,0:T(8,128)S(1)} %shard_map.88.refs_3_), custom_call_target="tpu_custom_call", output_to_operand_aliasing={{}: (3, {})} | custom-call | flops 536870912 | tf_op jit(solution)/shard_map/pallas_call | solution.py:135
  33.9 0.0 collective-permute-done.7.refs_3_
  33.9 0.4 collective-permute-start.10
  34.3 1.7 %collective-permute-start.6 = (bf16[2,384,128]{2,1,0:T(8,128)(2,1)S(1)}, bf16[2,384,128]{2,1,0:T(8,128)(2,1)S(1)}, u32[]{:S(2)}, u32[]{:S(2)}) collective-permute-start(bf16[2,384,128]{2,1,0:T(8,128)(2,1)S(1)} %collective-permute-done.2.refs_1_), channel_id=1, source_target_pairs={{0,8},{8,0},{1,9},{9,1},{2,10},{10,2},{3,11},{11,3},{4,12},{12,4},... | collective-permute-start | bytes 589832 | tf_op jit(solution)/shard_map/ppermute | solution.py:177
  35.9 0.1 collective-permute-start.8
  36.0 0.0 collective-permute-done.11.refs_1_
  36.0 1.2 %collective-permute-start.9 = (bf16[2,384,128]{2,1,0:T(8,128)(2,1)S(1)}, bf16[2,384,128]{2,1,0:T(8,128)(2,1)S(1)}, u32[]{:S(2)}, u32[]{:S(2)}) collective-permute-start(bf16[2,384,128]{2,1,0:T(8,128)(2,1)S(1)} %constant_dynamic-update-slice_fusion.2), channel_id=1, source_target_pairs={{0,8},{8,0},{1,9},{9,1},{2,10},{10,2},{3,11},{11,3},{4,12},{12,4},... | collective-permute-start | bytes 589832 | tf_op jit(solution)/shard_map/ppermute | solution.py:177
  37.2 0.0 collective-permute-done.12.refs_2_
  37.2 4.5 %shard_map.90.refs_3_ = f32[2048,128]{1,0:T(8,128)S(1)} custom-call(bf16[2048,128]{1,0:T(8,128)(2,1)S(1)} %bitcast.9, bf16[2,384,128]{2,1,0:T(8,128)(2,1)S(1)} %collective-permute-done.11.refs_1_, bf16[2,384,128]{2,1,0:T(8,128)(2,1)S(1)} %collective-permute-done.12.refs_2_, ...), custom_call_target="tpu_custom_call", output_to_operand_aliasing={{}: (4, {})} | custom-call | flops 671088640 | tf_op jit(solution)/shard_map/pallas_call | solution.py:135
  41.8 0.0 collective-permute-done.10.refs_2_
  41.8 0.2 collective-permute-done.6.refs_1_
  42.0 3.5 %shard_map.91.refs_3_ = f32[2048,128]{1,0:T(8,128)S(1)} custom-call(bf16[2048,128]{1,0:T(8,128)(2,1)S(1)} %bitcast.10, bf16[2,384,128]{2,1,0:T(8,128)(2,1)S(1)} %collective-permute-done.6.refs_1_, bf16[2,384,128]{2,1,0:T(8,128)(2,1)S(1)} %collective-permute-done.10.refs_2_, f32[2048,128]{1,0:T(8,128)S(1)} %shard_map.90.refs_3_), custom_call_target="tpu_custom_call", output_to_operand_aliasing={{}: (3, {})} | custom-call | flops 536870912 | tf_op jit(solution)/shard_map/pallas_call | solution.py:135
  45.5 0.0 collective-permute-done.8.refs_1_
  45.5 0.7 collective-permute-done.9.refs_2_
  46.2 1.1 %collective-permute-start.14 = (bf16[2,384,128]{2,1,0:T(8,128)(2,1)S(1)}, bf16[2,384,128]{2,1,0:T(8,128)(2,1)S(1)}, u32[]{:S(2)}, u32[]{:S(2)}) collective-permute-start(bf16[2,384,128]{2,1,0:T(8,128)(2,1)S(1)} %collective-permute-done.6.refs_1_), channel_id=1, source_target_pairs={{0,16},{16,0},{1,17},{17,1},{2,18},{18,2},{3,19},{19,3},{4,20},{20... | collective-permute-start | bytes 589832 | tf_op jit(solution)/shard_map/ppermute | solution.py:177
  47.3 0.1 collective-permute-start.15
  47.4 1.5 %collective-permute-start.13 = (bf16[2,384,128]{2,1,0:T(8,128)(2,1)S(1)}, bf16[2,384,128]{2,1,0:T(8,128)(2,1)S(1)}, u32[]{:S(2)}, u32[]{:S(2)}) collective-permute-start(bf16[2,384,128]{2,1,0:T(8,128)(2,1)S(1)} %collective-permute-done.8.refs_1_), channel_id=1, source_target_pairs={{0,8},{8,0},{1,9},{9,1},{2,10},{10,2},{3,11},{11,3},{4,12},{12,4},... | collective-permute-start | bytes 589832 | tf_op jit(solution)/shard_map/ppermute | solution.py:177
  49.0 0.8 collective-permute-start.17
  49.8 3.5 %shard_map.92.refs_3_ = f32[2048,128]{1,0:T(8,128)S(1)} custom-call(bf16[2048,128]{1,0:T(8,128)(2,1)S(1)} %bitcast.11, bf16[2,384,128]{2,1,0:T(8,128)(2,1)S(1)} %collective-permute-done.8.refs_1_, bf16[2,384,128]{2,1,0:T(8,128)(2,1)S(1)} %collective-permute-done.9.refs_2_, f32[2048,128]{1,0:T(8,128)S(1)} %shard_map.91.refs_3_), custom_call_target="tpu_custom_call", output_to_operand_aliasing={{}: (3, {})} | custom-call | flops 536870912 | tf_op jit(solution)/shard_map/pallas_call | solution.py:135
  53.2 0.0 collective-permute-done.14.refs_1_
  53.2 0.0 collective-permute-done.15.refs_2_
  53.3 3.5 %shard_map.93.refs_3_ = f32[2048,128]{1,0:T(8,128)S(1)} custom-call(bf16[2048,128]{1,0:T(8,128)(2,1)S(1)} %bitcast.12, bf16[2,384,128]{2,1,0:T(8,128)(2,1)S(1)} %collective-permute-done.14.refs_1_, bf16[2,384,128]{2,1,0:T(8,128)(2,1)S(1)} %collective-permute-done.15.refs_2_, f32[2048,128]{1,0:T(8,128)S(1)} %shard_map.92.refs_3_), custom_call_target="tpu_custom_call", output_to_operand_aliasing={{}: (3, {})} | custom-call | flops 536870912 | tf_op jit(solution)/shard_map/pallas_call | solution.py:135
  56.7 0.0 collective-permute-done.13.refs_2_
  56.8 0.3 collective-permute-start.16
  57.1 0.0 collective-permute-done.17.refs_1_
  57.1 3.5 %shard_map.94.refs_2_ = f32[2048,128]{1,0:T(8,128)S(1)} custom-call(bf16[2048,128]{1,0:T(8,128)(2,1)S(1)} %bitcast.13, bf16[2,384,128]{2,1,0:T(8,128)(2,1)S(1)} %collective-permute-done.17.refs_1_, bf16[2,384,128]{2,1,0:T(8,128)(2,1)S(1)} %collective-permute-done.13.refs_2_, f32[2048,128]{1,0:T(8,128)S(1)} %shard_map.93.refs_3_), custom_call_target="tpu_custom_call", output_to_operand_aliasing={{}: (3, {})} | custom-call | flops 536870912 | tf_op jit(solution)/shard_map/pallas_call | solution.py:135
  60.6 0.0 collective-permute-done.16.refs_1_
  60.6 2.5 %shard_map.95 = bf16[2048,128]{1,0:T(8,128)(2,1)} custom-call(bf16[2048,128]{1,0:T(8,128)(2,1)S(1)} %bitcast.14, bf16[2,384,128]{2,1,0:T(8,128)(2,1)S(1)} %collective-permute-done.16.refs_1_, f32[2048,128]{1,0:T(8,128)S(1)} %shard_map.94.refs_2_), custom_call_target="tpu_custom_call" | custom-call | flops 268435456 | tf_op jit(solution)/shard_map/pallas_call | solution.py:135
  63.1 0.0 copy-start
  63.1 0.0 copy-start.1
  63.1 4.9 %all-to-all-start.1 = ((bf16[8,256,128]{2,1,0:T(8,128)(2,1)}), bf16[8,256,128]{2,1,0:T(8,128)(2,1)S(1)}, u32[]{:S(2)}, u32[]{:S(2)}) async-start(bf16[8,256,128]{2,1,0:T(8,128)(2,1)} %bitcast.3), calls=%async_computation.1 | async-start | bytes 1048576 | tf_op jit(solution)/shard_map/all_to_all | solution.py:254
  68.7 8.4 %all-to-all-done.1.parts_ref = bf16[8,256,128]{2,1,0:T(8,128)(2,1)S(1)} async-done(((bf16[8,256,128]{2,1,0:T(8,128)(2,1)}), bf16[8,256,128]{2,1,0:T(8,128)(2,1)S(1)}, u32[]{:S(2)}, u32[]{:S(2)}) %all-to-all-start.1) | async-done | bytes 524320 | tf_op jit(solution)/shard_map/all_to_all | solution.py:254
  77.1 0.0 copy-done
  77.1 0.0 copy-done.1
  77.1 0.1 shard_map.96
  77.2 0.0 copy-start.3
  77.2 12.6 %all_to_all.20 = f32[32,4,128]{2,1,0:T(4,128)S(1)} all-to-all(f32[32,4,128]{2,1,0:T(4,128)S(1)} %broadcast_in_dim.4), channel_id=1, replica_groups=mesh['xh'=2,'xl'=2,'yl'=2,'c'=2,'yh'=2,'zh'=2,'zm'=2,'zl'=2] {'xh','xl',..., dimensions={0} | all-to-all | bytes 131072 | tf_op jit(solution)/shard_map/all_to_all | solution.py:187
  89.9 11.9 %all_to_all.21.sums_ref = f32[8,4,128]{2,1,0:T(4,128)S(1)} all-to-all(f32[8,4,128]{2,1,0:T(4,128)S(1)} %broadcast_in_dim.5), channel_id=1, replica_groups=mesh['xh'=2,'xl'=2,'yl'=2,'c'=2,'yh'=2,'zh'=2,'zm'=2,'zl'=2] {'zh','zm',..., dimensions={0} | all-to-all | bytes 32768 | tf_op jit(solution)/shard_map/all_to_all | solution.py:187
  101.8 0.0 copy-done.3
  101.8 0.8 shard_map.97
  (7 shorter events, 0.1 us)
Async XLA Ops:
  2.5 6.0 %copy-start.2 = (bf16[1,384,128]{2,1,0:T(8,128)(2,1)S(1)}, bf16[1,384,128]{2,1,0:T(8,128)(2,1)}, u32[]{:S(2)}) copy-start(bf16[1,384,128]{2,1,0:T(8,128)(2,1)} %get-tuple-element.23.refs_1_) | copy-start | bytes 294916
  2.5 13.8 %all-to-all-start = ((bf16[8,128,128]{2,1,0:T(8,128)(2,1)}), bf16[8,128,128]{2,1,0:T(8,128)(2,1)S(1)}, u32[]{:S(2)}, u32[]{:S(2)}) async-start(bf16[8,128,128]{2,1,0:T(8,128)(2,1)} %get-tuple-element.22), calls=%async_computation | async-start | bytes 524288 | tf_op jit(solution)/shard_map/all_to_all | solution.py:224
  8.6 8.0 %collective-permute-start.1 = (bf16[1,384,128]{2,1,0:T(8,128)(2,1)S(1)}, bf16[1,384,128]{2,1,0:T(8,128)(2,1)S(1)}, u32[]{:S(2)}, u32[]{:S(2)}) collective-permute-start(bf16[1,384,128]{2,1,0:T(8,128)(2,1)S(1)} %copy-done.2), channel_id=1, source_target_pairs={{0,16},{16,0},{1,17},{17,1},{2,18},{18,2},{3,19},{19,3},{4,20},{20... | collective-permute-start | bytes 294920 | tf_op jit(solution)/shard_map/ppermute | solution.py:177
  9.6 9.0 %collective-permute-start = (bf16[1,384,128]{2,1,0:T(8,128)(2,1)S(1)}, bf16[1,384,128]{2,1,0:T(8,128)(2,1)S(1)}, u32[]{:S(2)}, u32[]{:S(2)}) collective-permute-start(bf16[1,384,128]{2,1,0:T(8,128)(2,1)S(1)} %copy-done.2), channel_id=1, source_target_pairs={{0,2},{2,0},{1,3},{3,1},{4,6},{6,4},{5,7},{7,5},{8,10},{10,8},{9,1... | collective-permute-start | bytes 294920 | tf_op jit(solution)/shard_map/ppermute | solution.py:177
  12.6 11.6 %collective-permute-start.5 = (bf16[1,384,128]{2,1,0:T(8,128)(2,1)S(1)}, bf16[1,384,128]{2,1,0:T(8,128)(2,1)S(1)}, u32[]{:S(2)}, u32[]{:S(2)}) collective-permute-start(bf16[1,384,128]{2,1,0:T(8,128)(2,1)S(1)} %copy-done.2), channel_id=1, source_target_pairs={{0,7},{1,6},{2,5},{3,4},{4,3},{5,2},{6,1},{7,0},{8,15},{9,14},{10,... | collective-permute-start | bytes 294920 | tf_op jit(solution)/shard_map/ppermute | solution.py:182
  18.6 11.1 %collective-permute-start.2 = (bf16[2,384,128]{2,1,0:T(8,128)(2,1)S(1)}, bf16[2,384,128]{2,1,0:T(8,128)(2,1)S(1)}, u32[]{:S(2)}, u32[]{:S(2)}) collective-permute-start(bf16[2,384,128]{2,1,0:T(8,128)(2,1)S(1)} %constant_dynamic-update-slice_fusion), channel_id=1, source_target_pairs={{0,1},{1,0},{2,3},{3,2},{4,5},{5,4},{6,7},{7,6},{8,9},{9,8},{10,11... | collective-permute-start | bytes 589832 | tf_op jit(solution)/shard_map/ppermute | solution.py:177
  20.4 9.4 %collective-permute-start.3 = (bf16[2,384,128]{2,1,0:T(8,128)(2,1)S(1)}, bf16[2,384,128]{2,1,0:T(8,128)(2,1)S(1)}, u32[]{:S(2)}, u32[]{:S(2)}) collective-permute-start(bf16[2,384,128]{2,1,0:T(8,128)(2,1)S(1)} %constant_dynamic-update-slice_fusion), channel_id=1, source_target_pairs={{0,8},{8,0},{1,9},{9,1},{2,10},{10,2},{3,11},{11,3},{4,12},{12,4},... | collective-permute-start | bytes 589832 | tf_op jit(solution)/shard_map/ppermute | solution.py:177
  23.0 3.9 %collective-permute-start.4 = (bf16[1,384,128]{2,1,0:T(8,128)(2,1)S(1)}, bf16[1,384,128]{2,1,0:T(8,128)(2,1)S(1)}, u32[]{:S(2)}, u32[]{:S(2)}) collective-permute-start(bf16[1,384,128]{2,1,0:T(8,128)(2,1)S(1)} %collective-permute-done.refs_1_), channel_id=1, source_target_pairs={{0,16},{16,0},{1,17},{17,1},{2,18},{18,2},{3,19},{19,3},{4,20},{20... | collective-permute-start | bytes 294920 | tf_op jit(solution)/shard_map/ppermute | solution.py:177
  24.2 9.7 %collective-permute-start.7 = (bf16[1,384,128]{2,1,0:T(8,128)(2,1)S(1)}, bf16[1,384,128]{2,1,0:T(8,128)(2,1)S(1)}, u32[]{:S(2)}, u32[]{:S(2)}) collective-permute-start(bf16[1,384,128]{2,1,0:T(8,128)(2,1)S(1)} %collective-permute-done.5.refs_3_), channel_id=1, source_target_pairs={{0,2},{2,0},{1,3},{3,1},{4,6},{6,4},{5,7},{7,5},{8,10},{10,8},{9,1... | collective-permute-start | bytes 294920 | tf_op jit(solution)/shard_map/ppermute | solution.py:177
  29.8 6.2 %collective-permute-start.11 = (bf16[2,384,128]{2,1,0:T(8,128)(2,1)S(1)}, bf16[2,384,128]{2,1,0:T(8,128)(2,1)S(1)}, u32[]{:S(2)}, u32[]{:S(2)}) collective-permute-start(bf16[2,384,128]{2,1,0:T(8,128)(2,1)S(1)} %collective-permute-done.2.refs_1_), channel_id=1, source_target_pairs={{0,16},{16,0},{1,17},{17,1},{2,18},{18,2},{3,19},{19,3},{4,20},{20... | collective-permute-start | bytes 589832 | tf_op jit(solution)/shard_map/ppermute | solution.py:177
  30.1 7.1 %collective-permute-start.12 = (bf16[2,384,128]{2,1,0:T(8,128)(2,1)S(1)}, bf16[2,384,128]{2,1,0:T(8,128)(2,1)S(1)}, u32[]{:S(2)}, u32[]{:S(2)}) collective-permute-start(bf16[2,384,128]{2,1,0:T(8,128)(2,1)S(1)} %collective-permute-done.3.refs_2_), channel_id=1, source_target_pairs={{0,16},{16,0},{1,17},{17,1},{2,18},{18,2},{3,19},{19,3},{4,20},{20... | collective-permute-start | bytes 589832 | tf_op jit(solution)/shard_map/ppermute | solution.py:177
  33.9 7.9 %collective-permute-start.10 = (bf16[2,384,128]{2,1,0:T(8,128)(2,1)S(1)}, bf16[2,384,128]{2,1,0:T(8,128)(2,1)S(1)}, u32[]{:S(2)}, u32[]{:S(2)}) collective-permute-start(bf16[2,384,128]{2,1,0:T(8,128)(2,1)S(1)} %constant_dynamic-update-slice_fusion.2), channel_id=1, source_target_pairs={{0,16},{16,0},{1,17},{17,1},{2,18},{18,2},{3,19},{19,3},{4,20},{20... | collective-permute-start | bytes 589832 | tf_op jit(solution)/shard_map/ppermute | solution.py:177
  34.3 7.8 %collective-permute-start.6 = (bf16[2,384,128]{2,1,0:T(8,128)(2,1)S(1)}, bf16[2,384,128]{2,1,0:T(8,128)(2,1)S(1)}, u32[]{:S(2)}, u32[]{:S(2)}) collective-permute-start(bf16[2,384,128]{2,1,0:T(8,128)(2,1)S(1)} %collective-permute-done.2.refs_1_), channel_id=1, source_target_pairs={{0,8},{8,0},{1,9},{9,1},{2,10},{10,2},{3,11},{11,3},{4,12},{12,4},... | collective-permute-start | bytes 589832 | tf_op jit(solution)/shard_map/ppermute | solution.py:177
  35.9 9.6 %collective-permute-start.8 = (bf16[2,384,128]{2,1,0:T(8,128)(2,1)S(1)}, bf16[2,384,128]{2,1,0:T(8,128)(2,1)S(1)}, u32[]{:S(2)}, u32[]{:S(2)}) collective-permute-start(bf16[2,384,128]{2,1,0:T(8,128)(2,1)S(1)} %constant_dynamic-update-slice_fusion.2), channel_id=1, source_target_pairs={{0,1},{1,0},{2,3},{3,2},{4,5},{5,4},{6,7},{7,6},{8,9},{9,8},{10,11... | collective-permute-start | bytes 589832 | tf_op jit(solution)/shard_map/ppermute | solution.py:177
  36.0 10.2 %collective-permute-start.9 = (bf16[2,384,128]{2,1,0:T(8,128)(2,1)S(1)}, bf16[2,384,128]{2,1,0:T(8,128)(2,1)S(1)}, u32[]{:S(2)}, u32[]{:S(2)}) collective-permute-start(bf16[2,384,128]{2,1,0:T(8,128)(2,1)S(1)} %constant_dynamic-update-slice_fusion.2), channel_id=1, source_target_pairs={{0,8},{8,0},{1,9},{9,1},{2,10},{10,2},{3,11},{11,3},{4,12},{12,4},... | collective-permute-start | bytes 589832 | tf_op jit(solution)/shard_map/ppermute | solution.py:177
  46.2 7.0 %collective-permute-start.14 = (bf16[2,384,128]{2,1,0:T(8,128)(2,1)S(1)}, bf16[2,384,128]{2,1,0:T(8,128)(2,1)S(1)}, u32[]{:S(2)}, u32[]{:S(2)}) collective-permute-start(bf16[2,384,128]{2,1,0:T(8,128)(2,1)S(1)} %collective-permute-done.6.refs_1_), channel_id=1, source_target_pairs={{0,16},{16,0},{1,17},{17,1},{2,18},{18,2},{3,19},{19,3},{4,20},{20... | collective-permute-start | bytes 589832 | tf_op jit(solution)/shard_map/ppermute | solution.py:177
  47.3 5.9 %collective-permute-start.15 = (bf16[2,384,128]{2,1,0:T(8,128)(2,1)S(1)}, bf16[2,384,128]{2,1,0:T(8,128)(2,1)S(1)}, u32[]{:S(2)}, u32[]{:S(2)}) collective-permute-start(bf16[2,384,128]{2,1,0:T(8,128)(2,1)S(1)} %collective-permute-done.8.refs_1_), channel_id=1, source_target_pairs={{0,16},{16,0},{1,17},{17,1},{2,18},{18,2},{3,19},{19,3},{4,20},{20... | collective-permute-start | bytes 589832 | tf_op jit(solution)/shard_map/ppermute | solution.py:177
  47.4 9.3 %collective-permute-start.13 = (bf16[2,384,128]{2,1,0:T(8,128)(2,1)S(1)}, bf16[2,384,128]{2,1,0:T(8,128)(2,1)S(1)}, u32[]{:S(2)}, u32[]{:S(2)}) collective-permute-start(bf16[2,384,128]{2,1,0:T(8,128)(2,1)S(1)} %collective-permute-done.8.refs_1_), channel_id=1, source_target_pairs={{0,8},{8,0},{1,9},{9,1},{2,10},{10,2},{3,11},{11,3},{4,12},{12,4},... | collective-permute-start | bytes 589832 | tf_op jit(solution)/shard_map/ppermute | solution.py:177
  49.0 8.1 %collective-permute-start.17 = (bf16[2,384,128]{2,1,0:T(8,128)(2,1)S(1)}, bf16[2,384,128]{2,1,0:T(8,128)(2,1)S(1)}, u32[]{:S(2)}, u32[]{:S(2)}) collective-permute-start(bf16[2,384,128]{2,1,0:T(8,128)(2,1)S(1)} %collective-permute-done.9.refs_2_), channel_id=1, source_target_pairs={{0,16},{16,0},{1,17},{17,1},{2,18},{18,2},{3,19},{19,3},{4,20},{20... | collective-permute-start | bytes 589832 | tf_op jit(solution)/shard_map/ppermute | solution.py:177
  56.8 3.8 %collective-permute-start.16 = (bf16[2,384,128]{2,1,0:T(8,128)(2,1)S(1)}, bf16[2,384,128]{2,1,0:T(8,128)(2,1)S(1)}, u32[]{:S(2)}, u32[]{:S(2)}) collective-permute-start(bf16[2,384,128]{2,1,0:T(8,128)(2,1)S(1)} %collective-permute-done.13.refs_2_), channel_id=1, source_target_pairs={{0,16},{16,0},{1,17},{17,1},{2,18},{18,2},{3,19},{19,3},{4,20},{20... | collective-permute-start | bytes 589832 | tf_op jit(solution)/shard_map/ppermute | solution.py:177
  63.1 14.0 %copy-start = (f32[256,128]{1,0:T(8,128)S(1)}, f32[256,128]{1,0:T(8,128)}, u32[]{:S(2)}) copy-start(f32[256,128]{1,0:T(8,128)} %dir_ref.3) | copy-start | bytes 393220
  63.1 14.0 %copy-start.1 = (f32[256,128]{1,0:T(8,128)S(1)}, f32[256,128]{1,0:T(8,128)}, u32[]{:S(2)}) copy-start(f32[256,128]{1,0:T(8,128)} %res_ref.3) | copy-start | bytes 393220
  63.1 14.0 %all-to-all-start.1 = ((bf16[8,256,128]{2,1,0:T(8,128)(2,1)}), bf16[8,256,128]{2,1,0:T(8,128)(2,1)S(1)}, u32[]{:S(2)}, u32[]{:S(2)}) async-start(bf16[8,256,128]{2,1,0:T(8,128)(2,1)} %bitcast.3), calls=%async_computation.1 | async-start | bytes 1048576 | tf_op jit(solution)/shard_map/all_to_all | solution.py:254
  77.2 24.5 %copy-start.3 = (f32[256,128]{1,0:T(8,128)S(1)}, f32[256,128]{1,0:T(8,128)}, u32[]{:S(2)}) copy-start(f32[256,128]{1,0:T(8,128)} %sol_ref.1) | copy-start | bytes 393220

commit v9 on v8

--- a/solution.py
+++ b/solution.py
@@ -116,6 +116,13 @@
                 out_ref[at(k), :] = so_far.astype(out_ref.dtype)
         return
 
+    if count == 4:
+        for k in range(count):
+            if k + 1 < count:
+                distances(k + 1, (k + 1) % 2)
+            acc_ref[at(k), :] += products(k, k % 2)
+        return
+
     def body(turn, _):
         for s in range(2):
             k = turn * 2 + s

time: 103 us -> 102 us (level)
  Pallas kernels: 32.4 us -> 30.4 us
    pallas_call x9, Pallas kernels: 29.4 us -> 27.5 us  [tiles(): pl.pallas_call(functools.partial(tiles_kernel, len(bundles), so_far is no...]
  transfers between devices with their start and end apart: 20 -> 20, of which waited for: 3 -> 3; matrix products, arithmetic and copies ran while one was open for 0% -> 0% of each run, Pallas kernels for 26% -> 25%
where the time goes in v9:
time: 102 us
  starting transfers between devices  34.4 us (34%)
  Pallas kernels  30.4 us (30%)
  blocking collectives  25.4 us (25%)
  waiting for transfers between devices  9.7 us (10%)
  between operations  1.53 us (2%)
    pallas_call x9, Pallas kernels, tiles(): pl.pallas_call(functools.partial(tiles_kernel, len(bundles), so_far is no...  27.5 us
    all_to_all x2, blocking collectives, from_all(): lax.all_to_all(jnp.broadcast_to(x[None], (count,) + x.shape), axes, 0, 0,...  25.4 us
    ppermute x17, starting transfers between devices, turned(): return lax.ppermute(x, axis, [(i, (i + by) % count) for i in range(count)])  19.8 us
    all_to_all x1, waiting for transfers between devices, on_device(): lax.all_to_all(so_far.reshape(n_rows, 256, 128), ROWS, 0, 0, tiled=True)  8.43 us
    all_to_all x1, starting transfers between devices, on_device(): lax.all_to_all(row, ROWS, 0, 0, tiled=True)  6.01 us
    all_to_all x1, starting transfers between devices, on_device(): lax.all_to_all(so_far.reshape(n_rows, 256, 128), ROWS, 0, 0, tiled=True)  4.86 us
    ppermute x1, starting transfers between devices, mirrored(): return lax.ppermute(x, axes, [(i, count - 1 - i) for i in range(count)])  3.76 us
  transfers between devices with their start and end apart: 20, of which 3 were waited for; matrix products, arithmetic and copies ran while one was open for 0% of the time, Pallas kernels for 25%

profile of v9, /device:TPU:1, one launch (start us, length us, event | category | flops | bytes accessed | tf_op | source)
XLA Modules:
  0.0 101.6 jit_solution(9925352885680855458)
XLA Ops:
  0.6 1.9 %shard_map.85 = (bf16[8,128,128]{2,1,0:T(8,128)(2,1)}, bf16[1,384,128]{2,1,0:T(8,128)(2,1)}) custom-call(bf16[32,256]{1,0:T(8,128)(2,1)} %bitcast.15, f32[1,32]{1,0:T(1,128)} %bitcast.16, f32[256,128]{1,0:T(8,128)} %dir_ref.3), custom_call_target="tpu_custom_call" | custom-call | tf_op jit(solution)/shard_map/pallas_call | solution.py:208
  2.5 0.0 copy-start.2
  2.5 6.0 %all-to-all-start = ((bf16[8,128,128]{2,1,0:T(8,128)(2,1)}), bf16[8,128,128]{2,1,0:T(8,128)(2,1)S(1)}, u32[]{:S(2)}, u32[]{:S(2)}) async-start(bf16[8,128,128]{2,1,0:T(8,128)(2,1)} %get-tuple-element.22), calls=%async_computation | async-start | bytes 524288 | tf_op jit(solution)/shard_map/all_to_all | solution.py:231
  8.5 0.0 copy-done.2
  8.6 1.0 %collective-permute-start.1 = (bf16[1,384,128]{2,1,0:T(8,128)(2,1)S(1)}, bf16[1,384,128]{2,1,0:T(8,128)(2,1)S(1)}, u32[]{:S(2)}, u32[]{:S(2)}) collective-permute-start(bf16[1,384,128]{2,1,0:T(8,128)(2,1)S(1)} %copy-done.2), channel_id=1, source_target_pairs={{0,16},{16,0},{1,17},{17,1},{2,18},{18,2},{3,19},{19,3},{4,20},{20... | collective-permute-start | bytes 294920 | tf_op jit(solution)/shard_map/ppermute | solution.py:184
  9.6 3.0 %collective-permute-start = (bf16[1,384,128]{2,1,0:T(8,128)(2,1)S(1)}, bf16[1,384,128]{2,1,0:T(8,128)(2,1)S(1)}, u32[]{:S(2)}, u32[]{:S(2)}) collective-permute-start(bf16[1,384,128]{2,1,0:T(8,128)(2,1)S(1)} %copy-done.2), channel_id=1, source_target_pairs={{0,2},{2,0},{1,3},{3,1},{4,6},{6,4},{5,7},{7,5},{8,10},{10,8},{9,1... | collective-permute-start | bytes 294920 | tf_op jit(solution)/shard_map/ppermute | solution.py:184
  12.6 3.8 %collective-permute-start.5 = (bf16[1,384,128]{2,1,0:T(8,128)(2,1)S(1)}, bf16[1,384,128]{2,1,0:T(8,128)(2,1)S(1)}, u32[]{:S(2)}, u32[]{:S(2)}) collective-permute-start(bf16[1,384,128]{2,1,0:T(8,128)(2,1)S(1)} %copy-done.2), channel_id=1, source_target_pairs={{0,7},{1,6},{2,5},{3,4},{4,3},{5,2},{6,1},{7,0},{8,15},{9,14},{10,... | collective-permute-start | bytes 294920 | tf_op jit(solution)/shard_map/ppermute | solution.py:189
  16.4 0.0 all-to-all-done.x_ref
  16.4 0.1 shard_map.86
  16.5 0.0 collective-permute-done.1.refs_2_
  16.5 1.7 %shard_map.87.refs_4_ = f32[2048,128]{1,0:T(8,128)S(1)} custom-call(bf16[2048,128]{1,0:T(8,128)(2,1)S(1)} %bitcast.6, bf16[1,384,128]{2,1,0:T(8,128)(2,1)S(1)} %copy-done.2, bf16[1,384,128]{2,1,0:T(8,128)(2,1)S(1)} %collective-permute-done.1.refs_2_), custom_call_target="tpu_custom_call" | custom-call | flops 268435456 | tf_op jit(solution)/shard_map/pallas_call | solution.py:142
  18.2 0.0 collective-permute-done.refs_1_
  18.3 1.7 %collective-permute-start.2 = (bf16[2,384,128]{2,1,0:T(8,128)(2,1)S(1)}, bf16[2,384,128]{2,1,0:T(8,128)(2,1)S(1)}, u32[]{:S(2)}, u32[]{:S(2)}) collective-permute-start(bf16[2,384,128]{2,1,0:T(8,128)(2,1)S(1)} %constant_dynamic-update-slice_fusion), channel_id=1, source_target_pairs={{0,1},{1,0},{2,3},{3,2},{4,5},{5,4},{6,7},{7,6},{8,9},{9,8},{10,11... | collective-permute-start | bytes 589832 | tf_op jit(solution)/shard_map/ppermute | solution.py:184
  20.0 2.6 %collective-permute-start.3 = (bf16[2,384,128]{2,1,0:T(8,128)(2,1)S(1)}, bf16[2,384,128]{2,1,0:T(8,128)(2,1)S(1)}, u32[]{:S(2)}, u32[]{:S(2)}) collective-permute-start(bf16[2,384,128]{2,1,0:T(8,128)(2,1)S(1)} %constant_dynamic-update-slice_fusion), channel_id=1, source_target_pairs={{0,8},{8,0},{1,9},{9,1},{2,10},{10,2},{3,11},{11,3},{4,12},{12,4},... | collective-permute-start | bytes 589832 | tf_op jit(solution)/shard_map/ppermute | solution.py:184
  22.6 1.2 %collective-permute-start.4 = (bf16[1,384,128]{2,1,0:T(8,128)(2,1)S(1)}, bf16[1,384,128]{2,1,0:T(8,128)(2,1)S(1)}, u32[]{:S(2)}, u32[]{:S(2)}) collective-permute-start(bf16[1,384,128]{2,1,0:T(8,128)(2,1)S(1)} %collective-permute-done.refs_1_), channel_id=1, source_target_pairs={{0,16},{16,0},{1,17},{17,1},{2,18},{18,2},{3,19},{19,3},{4,20},{20... | collective-permute-start | bytes 294920 | tf_op jit(solution)/shard_map/ppermute | solution.py:184
  23.8 0.0 collective-permute-done.5.refs_3_
  23.8 2.7 %collective-permute-start.7 = (bf16[1,384,128]{2,1,0:T(8,128)(2,1)S(1)}, bf16[1,384,128]{2,1,0:T(8,128)(2,1)S(1)}, u32[]{:S(2)}, u32[]{:S(2)}) collective-permute-start(bf16[1,384,128]{2,1,0:T(8,128)(2,1)S(1)} %collective-permute-done.5.refs_3_), channel_id=1, source_target_pairs={{0,2},{2,0},{1,3},{3,1},{4,6},{6,4},{5,7},{7,5},{8,10},{10,8},{9,1... | collective-permute-start | bytes 294920 | tf_op jit(solution)/shard_map/ppermute | solution.py:184
  26.5 0.0 collective-permute-done.4.refs_2_
  26.5 2.9 %shard_map.88.refs_3_ = f32[2048,128]{1,0:T(8,128)S(1)} custom-call(bf16[2048,128]{1,0:T(8,128)(2,1)S(1)} %bitcast.7, bf16[1,384,128]{2,1,0:T(8,128)(2,1)S(1)} %collective-permute-done.refs_1_, bf16[1,384,128]{2,1,0:T(8,128)(2,1)S(1)} %collective-permute-done.4.refs_2_, ...), custom_call_target="tpu_custom_call", output_to_operand_aliasing={{}: (4, {})} | custom-call | flops 402653184 | tf_op jit(solution)/shard_map/pallas_call | solution.py:142
  29.4 0.0 collective-permute-done.2.refs_1_
  29.4 0.0 collective-permute-done.3.refs_2_
  29.4 0.3 collective-permute-start.11
  29.8 0.2 collective-permute-start.12
  30.0 3.2 %shard_map.89.refs_4_ = f32[2048,128]{1,0:T(8,128)S(1)} custom-call(bf16[2048,128]{1,0:T(8,128)(2,1)S(1)} %bitcast.8, bf16[2,384,128]{2,1,0:T(8,128)(2,1)S(1)} %collective-permute-done.2.refs_1_, bf16[2,384,128]{2,1,0:T(8,128)(2,1)S(1)} %collective-permute-done.3.refs_2_, f32[2048,128]{1,0:T(8,128)S(1)} %shard_map.88.refs_3_), custom_call_target="tpu_custom_call", output_to_operand_aliasing={{}: (3, {})} | custom-call | flops 536870912 | tf_op jit(solution)/shard_map/pallas_call | solution.py:142
  33.2 0.0 collective-permute-done.7.refs_3_
  33.2 0.3 collective-permute-start.10
  33.6 1.7 %collective-permute-start.6 = (bf16[2,384,128]{2,1,0:T(8,128)(2,1)S(1)}, bf16[2,384,128]{2,1,0:T(8,128)(2,1)S(1)}, u32[]{:S(2)}, u32[]{:S(2)}) collective-permute-start(bf16[2,384,128]{2,1,0:T(8,128)(2,1)S(1)} %collective-permute-done.2.refs_1_), channel_id=1, source_target_pairs={{0,8},{8,0},{1,9},{9,1},{2,10},{10,2},{3,11},{11,3},{4,12},{12,4},... | collective-permute-start | bytes 589832 | tf_op jit(solution)/shard_map/ppermute | solution.py:184
  35.2 0.1 collective-permute-start.8
  35.3 0.0 collective-permute-done.11.refs_1_
  35.3 1.2 %collective-permute-start.9 = (bf16[2,384,128]{2,1,0:T(8,128)(2,1)S(1)}, bf16[2,384,128]{2,1,0:T(8,128)(2,1)S(1)}, u32[]{:S(2)}, u32[]{:S(2)}) collective-permute-start(bf16[2,384,128]{2,1,0:T(8,128)(2,1)S(1)} %constant_dynamic-update-slice_fusion.2), channel_id=1, source_target_pairs={{0,8},{8,0},{1,9},{9,1},{2,10},{10,2},{3,11},{11,3},{4,12},{12,4},... | collective-permute-start | bytes 589832 | tf_op jit(solution)/shard_map/ppermute | solution.py:184
  36.6 0.0 collective-permute-done.12.refs_2_
  36.6 4.6 %shard_map.90.refs_3_ = f32[2048,128]{1,0:T(8,128)S(1)} custom-call(bf16[2048,128]{1,0:T(8,128)(2,1)S(1)} %bitcast.9, bf16[2,384,128]{2,1,0:T(8,128)(2,1)S(1)} %collective-permute-done.11.refs_1_, bf16[2,384,128]{2,1,0:T(8,128)(2,1)S(1)} %collective-permute-done.12.refs_2_, ...), custom_call_target="tpu_custom_call", output_to_operand_aliasing={{}: (4, {})} | custom-call | flops 671088640 | tf_op jit(solution)/shard_map/pallas_call | solution.py:142
  41.1 0.0 collective-permute-done.10.refs_2_
  41.1 0.2 collective-permute-done.6.refs_1_
  41.3 3.2 %shard_map.91.refs_3_ = f32[2048,128]{1,0:T(8,128)S(1)} custom-call(bf16[2048,128]{1,0:T(8,128)(2,1)S(1)} %bitcast.10, bf16[2,384,128]{2,1,0:T(8,128)(2,1)S(1)} %collective-permute-done.6.refs_1_, bf16[2,384,128]{2,1,0:T(8,128)(2,1)S(1)} %collective-permute-done.10.refs_2_, f32[2048,128]{1,0:T(8,128)S(1)} %shard_map.90.refs_3_), custom_call_target="tpu_custom_call", output_to_operand_aliasing={{}: (3, {})} | custom-call | flops 536870912 | tf_op jit(solution)/shard_map/pallas_call | solution.py:142
  44.5 0.0 collective-permute-done.8.refs_1_
  44.5 1.0 %collective-permute-done.9.refs_2_ = bf16[2,384,128]{2,1,0:T(8,128)(2,1)S(1)} collective-permute-done((bf16[2,384,128]{2,1,0:T(8,128)(2,1)S(1)}, bf16[2,384,128]{2,1,0:T(8,128)(2,1)S(1)}, u32[]{:S(2)}, u32[]{:S(2)}) %collective-permute-start.9) | collective-permute-done | bytes 196640 | tf_op jit(solution)/shard_map/ppermute | solution.py:184
  45.5 1.1 %collective-permute-start.14 = (bf16[2,384,128]{2,1,0:T(8,128)(2,1)S(1)}, bf16[2,384,128]{2,1,0:T(8,128)(2,1)S(1)}, u32[]{:S(2)}, u32[]{:S(2)}) collective-permute-start(bf16[2,384,128]{2,1,0:T(8,128)(2,1)S(1)} %collective-permute-done.6.refs_1_), channel_id=1, source_target_pairs={{0,16},{16,0},{1,17},{17,1},{2,18},{18,2},{3,19},{19,3},{4,20},{20... | collective-permute-start | bytes 589832 | tf_op jit(solution)/shard_map/ppermute | solution.py:184
  46.6 0.0 collective-permute-start.15
  46.6 1.6 %collective-permute-start.13 = (bf16[2,384,128]{2,1,0:T(8,128)(2,1)S(1)}, bf16[2,384,128]{2,1,0:T(8,128)(2,1)S(1)}, u32[]{:S(2)}, u32[]{:S(2)}) collective-permute-start(bf16[2,384,128]{2,1,0:T(8,128)(2,1)S(1)} %collective-permute-done.8.refs_1_), channel_id=1, source_target_pairs={{0,8},{8,0},{1,9},{9,1},{2,10},{10,2},{3,11},{11,3},{4,12},{12,4},... | collective-permute-start | bytes 589832 | tf_op jit(solution)/shard_map/ppermute | solution.py:184
  48.3 0.8 collective-permute-start.17
  49.1 3.2 %shard_map.92.refs_3_ = f32[2048,128]{1,0:T(8,128)S(1)} custom-call(bf16[2048,128]{1,0:T(8,128)(2,1)S(1)} %bitcast.11, bf16[2,384,128]{2,1,0:T(8,128)(2,1)S(1)} %collective-permute-done.8.refs_1_, bf16[2,384,128]{2,1,0:T(8,128)(2,1)S(1)} %collective-permute-done.9.refs_2_, f32[2048,128]{1,0:T(8,128)S(1)} %shard_map.91.refs_3_), custom_call_target="tpu_custom_call", output_to_operand_aliasing={{}: (3, {})} | custom-call | flops 536870912 | tf_op jit(solution)/shard_map/pallas_call | solution.py:142
  52.2 0.0 collective-permute-done.14.refs_1_
  52.2 0.0 collective-permute-done.15.refs_2_
  52.2 3.2 %shard_map.93.refs_3_ = f32[2048,128]{1,0:T(8,128)S(1)} custom-call(bf16[2048,128]{1,0:T(8,128)(2,1)S(1)} %bitcast.12, bf16[2,384,128]{2,1,0:T(8,128)(2,1)S(1)} %collective-permute-done.14.refs_1_, bf16[2,384,128]{2,1,0:T(8,128)(2,1)S(1)} %collective-permute-done.15.refs_2_, f32[2048,128]{1,0:T(8,128)S(1)} %shard_map.92.refs_3_), custom_call_target="tpu_custom_call", output_to_operand_aliasing={{}: (3, {})} | custom-call | flops 536870912 | tf_op jit(solution)/shard_map/pallas_call | solution.py:142
  55.4 0.0 collective-permute-done.13.refs_2_
  55.4 0.1 collective-permute-start.16
  55.5 0.0 collective-permute-done.17.refs_1_
  55.5 3.2 %shard_map.94.refs_2_ = f32[2048,128]{1,0:T(8,128)S(1)} custom-call(bf16[2048,128]{1,0:T(8,128)(2,1)S(1)} %bitcast.13, bf16[2,384,128]{2,1,0:T(8,128)(2,1)S(1)} %collective-permute-done.17.refs_1_, bf16[2,384,128]{2,1,0:T(8,128)(2,1)S(1)} %collective-permute-done.13.refs_2_, f32[2048,128]{1,0:T(8,128)S(1)} %shard_map.93.refs_3_), custom_call_target="tpu_custom_call", output_to_operand_aliasing={{}: (3, {})} | custom-call | flops 536870912 | tf_op jit(solution)/shard_map/pallas_call | solution.py:142
  58.7 0.0 collective-permute-done.16.refs_1_
  58.7 2.5 %shard_map.95 = bf16[2048,128]{1,0:T(8,128)(2,1)} custom-call(bf16[2048,128]{1,0:T(8,128)(2,1)S(1)} %bitcast.14, bf16[2,384,128]{2,1,0:T(8,128)(2,1)S(1)} %collective-permute-done.16.refs_1_, f32[2048,128]{1,0:T(8,128)S(1)} %shard_map.94.refs_2_), custom_call_target="tpu_custom_call" | custom-call | flops 268435456 | tf_op jit(solution)/shard_map/pallas_call | solution.py:142
  61.3 0.0 copy-start
  61.3 0.0 copy-start.1
  61.3 4.9 %all-to-all-start.1 = ((bf16[8,256,128]{2,1,0:T(8,128)(2,1)}), bf16[8,256,128]{2,1,0:T(8,128)(2,1)S(1)}, u32[]{:S(2)}, u32[]{:S(2)}) async-start(bf16[8,256,128]{2,1,0:T(8,128)(2,1)} %bitcast.3), calls=%async_computation.1 | async-start | bytes 1048576 | tf_op jit(solution)/shard_map/all_to_all | solution.py:261
  66.8 8.4 %all-to-all-done.1.parts_ref = bf16[8,256,128]{2,1,0:T(8,128)(2,1)S(1)} async-done(((bf16[8,256,128]{2,1,0:T(8,128)(2,1)}), bf16[8,256,128]{2,1,0:T(8,128)(2,1)S(1)}, u32[]{:S(2)}, u32[]{:S(2)}) %all-to-all-start.1) | async-done | bytes 524320 | tf_op jit(solution)/shard_map/all_to_all | solution.py:261
  75.2 0.0 copy-done
  75.2 0.0 copy-done.1
  75.2 0.1 shard_map.96
  75.4 0.0 copy-start.3
  75.4 13.2 %all_to_all.20 = f32[32,4,128]{2,1,0:T(4,128)S(1)} all-to-all(f32[32,4,128]{2,1,0:T(4,128)S(1)} %broadcast_in_dim.4), channel_id=1, replica_groups=mesh['xh'=2,'xl'=2,'yl'=2,'c'=2,'yh'=2,'zh'=2,'zm'=2,'zl'=2] {'xh','xl',..., dimensions={0} | all-to-all | bytes 131072 | tf_op jit(solution)/shard_map/all_to_all | solution.py:194
  88.6 12.2 %all_to_all.21.sums_ref = f32[8,4,128]{2,1,0:T(4,128)S(1)} all-to-all(f32[8,4,128]{2,1,0:T(4,128)S(1)} %broadcast_in_dim.5), channel_id=1, replica_groups=mesh['xh'=2,'xl'=2,'yl'=2,'c'=2,'yh'=2,'zh'=2,'zm'=2,'zl'=2] {'zh','zm',..., dimensions={0} | all-to-all | bytes 32768 | tf_op jit(solution)/shard_map/all_to_all | solution.py:194
  100.8 0.0 copy-done.3
  100.8 0.8 shard_map.97
  (7 shorter events, 0.1 us)
Async XLA Ops:
  2.5 6.0 %copy-start.2 = (bf16[1,384,128]{2,1,0:T(8,128)(2,1)S(1)}, bf16[1,384,128]{2,1,0:T(8,128)(2,1)}, u32[]{:S(2)}) copy-start(bf16[1,384,128]{2,1,0:T(8,128)(2,1)} %get-tuple-element.23.refs_1_) | copy-start | bytes 294916
  2.5 13.8 %all-to-all-start = ((bf16[8,128,128]{2,1,0:T(8,128)(2,1)}), bf16[8,128,128]{2,1,0:T(8,128)(2,1)S(1)}, u32[]{:S(2)}, u32[]{:S(2)}) async-start(bf16[8,128,128]{2,1,0:T(8,128)(2,1)} %get-tuple-element.22), calls=%async_computation | async-start | bytes 524288 | tf_op jit(solution)/shard_map/all_to_all | solution.py:231
  8.6 8.0 %collective-permute-start.1 = (bf16[1,384,128]{2,1,0:T(8,128)(2,1)S(1)}, bf16[1,384,128]{2,1,0:T(8,128)(2,1)S(1)}, u32[]{:S(2)}, u32[]{:S(2)}) collective-permute-start(bf16[1,384,128]{2,1,0:T(8,128)(2,1)S(1)} %copy-done.2), channel_id=1, source_target_pairs={{0,16},{16,0},{1,17},{17,1},{2,18},{18,2},{3,19},{19,3},{4,20},{20... | collective-permute-start | bytes 294920 | tf_op jit(solution)/shard_map/ppermute | solution.py:184
  9.6 8.6 %collective-permute-start = (bf16[1,384,128]{2,1,0:T(8,128)(2,1)S(1)}, bf16[1,384,128]{2,1,0:T(8,128)(2,1)S(1)}, u32[]{:S(2)}, u32[]{:S(2)}) collective-permute-start(bf16[1,384,128]{2,1,0:T(8,128)(2,1)S(1)} %copy-done.2), channel_id=1, source_target_pairs={{0,2},{2,0},{1,3},{3,1},{4,6},{6,4},{5,7},{7,5},{8,10},{10,8},{9,1... | collective-permute-start | bytes 294920 | tf_op jit(solution)/shard_map/ppermute | solution.py:184
  12.6 11.2 %collective-permute-start.5 = (bf16[1,384,128]{2,1,0:T(8,128)(2,1)S(1)}, bf16[1,384,128]{2,1,0:T(8,128)(2,1)S(1)}, u32[]{:S(2)}, u32[]{:S(2)}) collective-permute-start(bf16[1,384,128]{2,1,0:T(8,128)(2,1)S(1)} %copy-done.2), channel_id=1, source_target_pairs={{0,7},{1,6},{2,5},{3,4},{4,3},{5,2},{6,1},{7,0},{8,15},{9,14},{10,... | collective-permute-start | bytes 294920 | tf_op jit(solution)/shard_map/ppermute | solution.py:189
  18.3 11.1 %collective-permute-start.2 = (bf16[2,384,128]{2,1,0:T(8,128)(2,1)S(1)}, bf16[2,384,128]{2,1,0:T(8,128)(2,1)S(1)}, u32[]{:S(2)}, u32[]{:S(2)}) collective-permute-start(bf16[2,384,128]{2,1,0:T(8,128)(2,1)S(1)} %constant_dynamic-update-slice_fusion), channel_id=1, source_target_pairs={{0,1},{1,0},{2,3},{3,2},{4,5},{5,4},{6,7},{7,6},{8,9},{9,8},{10,11... | collective-permute-start | bytes 589832 | tf_op jit(solution)/shard_map/ppermute | solution.py:184
  20.0 9.4 %collective-permute-start.3 = (bf16[2,384,128]{2,1,0:T(8,128)(2,1)S(1)}, bf16[2,384,128]{2,1,0:T(8,128)(2,1)S(1)}, u32[]{:S(2)}, u32[]{:S(2)}) collective-permute-start(bf16[2,384,128]{2,1,0:T(8,128)(2,1)S(1)} %constant_dynamic-update-slice_fusion), channel_id=1, source_target_pairs={{0,8},{8,0},{1,9},{9,1},{2,10},{10,2},{3,11},{11,3},{4,12},{12,4},... | collective-permute-start | bytes 589832 | tf_op jit(solution)/shard_map/ppermute | solution.py:184
  22.6 3.9 %collective-permute-start.4 = (bf16[1,384,128]{2,1,0:T(8,128)(2,1)S(1)}, bf16[1,384,128]{2,1,0:T(8,128)(2,1)S(1)}, u32[]{:S(2)}, u32[]{:S(2)}) collective-permute-start(bf16[1,384,128]{2,1,0:T(8,128)(2,1)S(1)} %collective-permute-done.refs_1_), channel_id=1, source_target_pairs={{0,16},{16,0},{1,17},{17,1},{2,18},{18,2},{3,19},{19,3},{4,20},{20... | collective-permute-start | bytes 294920 | tf_op jit(solution)/shard_map/ppermute | solution.py:184
  23.8 9.4 %collective-permute-start.7 = (bf16[1,384,128]{2,1,0:T(8,128)(2,1)S(1)}, bf16[1,384,128]{2,1,0:T(8,128)(2,1)S(1)}, u32[]{:S(2)}, u32[]{:S(2)}) collective-permute-start(bf16[1,384,128]{2,1,0:T(8,128)(2,1)S(1)} %collective-permute-done.5.refs_3_), channel_id=1, source_target_pairs={{0,2},{2,0},{1,3},{3,1},{4,6},{6,4},{5,7},{7,5},{8,10},{10,8},{9,1... | collective-permute-start | bytes 294920 | tf_op jit(solution)/shard_map/ppermute | solution.py:184
  29.4 5.9 %collective-permute-start.11 = (bf16[2,384,128]{2,1,0:T(8,128)(2,1)S(1)}, bf16[2,384,128]{2,1,0:T(8,128)(2,1)S(1)}, u32[]{:S(2)}, u32[]{:S(2)}) collective-permute-start(bf16[2,384,128]{2,1,0:T(8,128)(2,1)S(1)} %collective-permute-done.2.refs_1_), channel_id=1, source_target_pairs={{0,16},{16,0},{1,17},{17,1},{2,18},{18,2},{3,19},{19,3},{4,20},{20... | collective-permute-start | bytes 589832 | tf_op jit(solution)/shard_map/ppermute | solution.py:184
  29.8 6.8 %collective-permute-start.12 = (bf16[2,384,128]{2,1,0:T(8,128)(2,1)S(1)}, bf16[2,384,128]{2,1,0:T(8,128)(2,1)S(1)}, u32[]{:S(2)}, u32[]{:S(2)}) collective-permute-start(bf16[2,384,128]{2,1,0:T(8,128)(2,1)S(1)} %collective-permute-done.3.refs_2_), channel_id=1, source_target_pairs={{0,16},{16,0},{1,17},{17,1},{2,18},{18,2},{3,19},{19,3},{4,20},{20... | collective-permute-start | bytes 589832 | tf_op jit(solution)/shard_map/ppermute | solution.py:184
  33.2 7.9 %collective-permute-start.10 = (bf16[2,384,128]{2,1,0:T(8,128)(2,1)S(1)}, bf16[2,384,128]{2,1,0:T(8,128)(2,1)S(1)}, u32[]{:S(2)}, u32[]{:S(2)}) collective-permute-start(bf16[2,384,128]{2,1,0:T(8,128)(2,1)S(1)} %constant_dynamic-update-slice_fusion.2), channel_id=1, source_target_pairs={{0,16},{16,0},{1,17},{17,1},{2,18},{18,2},{3,19},{19,3},{4,20},{20... | collective-permute-start | bytes 589832 | tf_op jit(solution)/shard_map/ppermute | solution.py:184
  33.6 7.8 %collective-permute-start.6 = (bf16[2,384,128]{2,1,0:T(8,128)(2,1)S(1)}, bf16[2,384,128]{2,1,0:T(8,128)(2,1)S(1)}, u32[]{:S(2)}, u32[]{:S(2)}) collective-permute-start(bf16[2,384,128]{2,1,0:T(8,128)(2,1)S(1)} %collective-permute-done.2.refs_1_), channel_id=1, source_target_pairs={{0,8},{8,0},{1,9},{9,1},{2,10},{10,2},{3,11},{11,3},{4,12},{12,4},... | collective-permute-start | bytes 589832 | tf_op jit(solution)/shard_map/ppermute | solution.py:184
  35.2 9.3 %collective-permute-start.8 = (bf16[2,384,128]{2,1,0:T(8,128)(2,1)S(1)}, bf16[2,384,128]{2,1,0:T(8,128)(2,1)S(1)}, u32[]{:S(2)}, u32[]{:S(2)}) collective-permute-start(bf16[2,384,128]{2,1,0:T(8,128)(2,1)S(1)} %constant_dynamic-update-slice_fusion.2), channel_id=1, source_target_pairs={{0,1},{1,0},{2,3},{3,2},{4,5},{5,4},{6,7},{7,6},{8,9},{9,8},{10,11... | collective-permute-start | bytes 589832 | tf_op jit(solution)/shard_map/ppermute | solution.py:184
  35.3 10.2 %collective-permute-start.9 = (bf16[2,384,128]{2,1,0:T(8,128)(2,1)S(1)}, bf16[2,384,128]{2,1,0:T(8,128)(2,1)S(1)}, u32[]{:S(2)}, u32[]{:S(2)}) collective-permute-start(bf16[2,384,128]{2,1,0:T(8,128)(2,1)S(1)} %constant_dynamic-update-slice_fusion.2), channel_id=1, source_target_pairs={{0,8},{8,0},{1,9},{9,1},{2,10},{10,2},{3,11},{11,3},{4,12},{12,4},... | collective-permute-start | bytes 589832 | tf_op jit(solution)/shard_map/ppermute | solution.py:184
  45.5 6.7 %collective-permute-start.14 = (bf16[2,384,128]{2,1,0:T(8,128)(2,1)S(1)}, bf16[2,384,128]{2,1,0:T(8,128)(2,1)S(1)}, u32[]{:S(2)}, u32[]{:S(2)}) collective-permute-start(bf16[2,384,128]{2,1,0:T(8,128)(2,1)S(1)} %collective-permute-done.6.refs_1_), channel_id=1, source_target_pairs={{0,16},{16,0},{1,17},{17,1},{2,18},{18,2},{3,19},{19,3},{4,20},{20... | collective-permute-start | bytes 589832 | tf_op jit(solution)/shard_map/ppermute | solution.py:184
  46.6 5.6 %collective-permute-start.15 = (bf16[2,384,128]{2,1,0:T(8,128)(2,1)S(1)}, bf16[2,384,128]{2,1,0:T(8,128)(2,1)S(1)}, u32[]{:S(2)}, u32[]{:S(2)}) collective-permute-start(bf16[2,384,128]{2,1,0:T(8,128)(2,1)S(1)} %collective-permute-done.8.refs_1_), channel_id=1, source_target_pairs={{0,16},{16,0},{1,17},{17,1},{2,18},{18,2},{3,19},{19,3},{4,20},{20... | collective-permute-start | bytes 589832 | tf_op jit(solution)/shard_map/ppermute | solution.py:184
  46.6 8.8 %collective-permute-start.13 = (bf16[2,384,128]{2,1,0:T(8,128)(2,1)S(1)}, bf16[2,384,128]{2,1,0:T(8,128)(2,1)S(1)}, u32[]{:S(2)}, u32[]{:S(2)}) collective-permute-start(bf16[2,384,128]{2,1,0:T(8,128)(2,1)S(1)} %collective-permute-done.8.refs_1_), channel_id=1, source_target_pairs={{0,8},{8,0},{1,9},{9,1},{2,10},{10,2},{3,11},{11,3},{4,12},{12,4},... | collective-permute-start | bytes 589832 | tf_op jit(solution)/shard_map/ppermute | solution.py:184
  48.3 7.3 %collective-permute-start.17 = (bf16[2,384,128]{2,1,0:T(8,128)(2,1)S(1)}, bf16[2,384,128]{2,1,0:T(8,128)(2,1)S(1)}, u32[]{:S(2)}, u32[]{:S(2)}) collective-permute-start(bf16[2,384,128]{2,1,0:T(8,128)(2,1)S(1)} %collective-permute-done.9.refs_2_), channel_id=1, source_target_pairs={{0,16},{16,0},{1,17},{17,1},{2,18},{18,2},{3,19},{19,3},{4,20},{20... | collective-permute-start | bytes 589832 | tf_op jit(solution)/shard_map/ppermute | solution.py:184
  55.4 3.3 %collective-permute-start.16 = (bf16[2,384,128]{2,1,0:T(8,128)(2,1)S(1)}, bf16[2,384,128]{2,1,0:T(8,128)(2,1)S(1)}, u32[]{:S(2)}, u32[]{:S(2)}) collective-permute-start(bf16[2,384,128]{2,1,0:T(8,128)(2,1)S(1)} %collective-permute-done.13.refs_2_), channel_id=1, source_target_pairs={{0,16},{16,0},{1,17},{17,1},{2,18},{18,2},{3,19},{19,3},{4,20},{20... | collective-permute-start | bytes 589832 | tf_op jit(solution)/shard_map/ppermute | solution.py:184
  61.3 13.9 %copy-start = (f32[256,128]{1,0:T(8,128)S(1)}, f32[256,128]{1,0:T(8,128)}, u32[]{:S(2)}) copy-start(f32[256,128]{1,0:T(8,128)} %dir_ref.3) | copy-start | bytes 393220
  61.3 14.0 %copy-start.1 = (f32[256,128]{1,0:T(8,128)S(1)}, f32[256,128]{1,0:T(8,128)}, u32[]{:S(2)}) copy-start(f32[256,128]{1,0:T(8,128)} %res_ref.3) | copy-start | bytes 393220
  61.3 13.9 %all-to-all-start.1 = ((bf16[8,256,128]{2,1,0:T(8,128)(2,1)}), bf16[8,256,128]{2,1,0:T(8,128)(2,1)S(1)}, u32[]{:S(2)}, u32[]{:S(2)}) async-start(bf16[8,256,128]{2,1,0:T(8,128)(2,1)} %bitcast.3), calls=%async_computation.1 | async-start | bytes 1048576 | tf_op jit(solution)/shard_map/all_to_all | solution.py:261
  75.4 25.5 %copy-start.3 = (f32[256,128]{1,0:T(8,128)S(1)}, f32[256,128]{1,0:T(8,128)}, u32[]{:S(2)}) copy-start(f32[256,128]{1,0:T(8,128)} %sol_ref.1) | copy-start | bytes 393220
